TPU v7x, 32 devices: a whole 2x2x4 slice. The times are simulated.
32 devices in a mesh: items: 4 (over y, x), seq: 8 (over z, core).
Axes of the slice: x: 2, y: 2, z: 4, core: 2. Of those that a mesh axis runs over, the one named last changes fastest.
Arguments:
- tokens: bfloat16 [4, 2048, 1024], P('items', 'seq'), may hold values from -6 to 6
- decay_rate: float32 [8], replicated, may hold values from 0.96 to 1, as said below
- query_weight: bfloat16 [1024, 1024], P(('items', 'seq')), may hold values from -0.1875 to 0.1875
- key_weight: bfloat16 [1024, 1024], P(('items', 'seq')), may hold values from -0.1875 to 0.1875
- value_weight: bfloat16 [1024, 1024], P(('items', 'seq')), may hold values from -0.1875 to 0.1875
- update_weight: bfloat16 [1024, 1024], P(('items', 'seq')), may hold values from -0.1875 to 0.1875
- output_weight: bfloat16 [1024, 1024], P(('items', 'seq')), may hold values from -0.1875 to 0.1875
- gate_weight: bfloat16 [1024, 2816], P(('items', 'seq')), may hold values from -0.1875 to 0.1875
- up_weight: bfloat16 [1024, 2816], P(('items', 'seq')), may hold values from -0.1875 to 0.1875
- down_weight: bfloat16 [2816, 1024], P(None, ('items', 'seq')), may hold values from -0.109375 to 0.109375
- cotangent: bfloat16 [4, 2048, 1024], P('items', 'seq'), may hold values from -6 to 6
Outputs:
- mixed: bfloat16 [4, 2048, 1024], P('items', 'seq')
- tokens_grad: float32 [4, 2048, 1024], P('items', 'seq')
- query_grad: float32 [1024, 1024], P(('items', 'seq'))
- key_grad: float32 [1024, 1024], P(('items', 'seq'))
- value_grad: float32 [1024, 1024], P(('items', 'seq'))
- update_grad: float32 [1024, 1024], P(('items', 'seq'))
- output_grad: float32 [1024, 1024], P(('items', 'seq'))
- gate_grad: float32 [1024, 2816], P(('items', 'seq'))
- up_grad: float32 [1024, 2816], P(('items', 'seq'))
- down_grad: float32 [2816, 1024], P(None, ('items', 'seq'))
Inputs may be any that keep to these rules, and one draw needn't show every extreme that they name: decay_rate[h] is lambda_h, the factor by which head h keeps its state from one position to the next.
All inputs are finite; a program needn't handle non-finite values.
Results may differ from a plain program's by a relative error of at most 0.015.
Values may be sent and summed in bfloat16 or wider, within the bound.
No kernel may reach another device: no remote copies, remote signals or barrier semaphores. Data moves between devices by JAX's collectives and lax.ppermute only.
A program may use at most 320 MiB of HBM per device.

v0:
```python
import functools
import math

import jax
import jax.numpy as jnp
from jax import lax
from jax.experimental import pallas as pl
from jax.experimental.pallas import tpu as pltpu
from jax.sharding import PartitionSpec as P

epsilon = 1e-06
AXES = ("items", "group", "member")
f32 = jnp.float32
bf16 = jnp.bfloat16
MIB = 1024 * 1024
VM = (12, 16, 16, 16)


def mm(a, b):
    return jnp.dot(a, b, preferred_element_type=f32)


def mm_tn(a, b):
    return lax.dot_general(a, b, (((0,), (0,)), ((), ())), preferred_element_type=f32)


def mm_nt(a, b):
    return lax.dot_general(a, b, (((1,), (1,)), ((), ())), preferred_element_type=f32)


def norm_factor(v):
    return lax.rsqrt(jnp.mean(v * v, axis=-1, keepdims=True) + epsilon)


def norm_back(normed, scale, grad):
    return scale * (grad - normed * jnp.mean(grad * normed, axis=-1, keepdims=True))


def like(shape, dtype):
    return jax.ShapeDtypeStruct(tuple(shape), dtype)


def run(name, kernel, outs, scalars, arrays, scratch=(), flops=0, vmem=10, after=()):
    ins = list(scalars) + list(arrays) + list(after)
    used, held = len(scalars) + len(arrays), len(after)

    def body(*refs):
        kernel(*refs[:used], *refs[used + held :])

    size = sum(v.size * v.dtype.itemsize for v in list(arrays) + list(outs)) if flops else 0
    return pl.pallas_call(
        body,
        out_shape=list(outs),
        in_specs=[pl.BlockSpec(memory_space=pltpu.SMEM)] * len(scalars)
        + [pl.BlockSpec(memory_space=pltpu.VMEM)] * len(arrays)
        + [pl.BlockSpec(memory_space=pl.ANY)] * held,
        out_specs=[pl.BlockSpec(memory_space=pltpu.VMEM)] * len(outs),
        scratch_shapes=list(scratch),
        compiler_params=pltpu.CompilerParams(vmem_limit_bytes=vmem * MIB),
        cost_estimate=pl.CostEstimate(flops=flops, bytes_accessed=size, transcendentals=0),
        name=name,
    )(*ins)


def tie(v, *after):
    anywhere = pl.BlockSpec(memory_space=pl.ANY)
    return pl.pallas_call(
        lambda *refs: None,
        out_shape=like(v.shape, v.dtype),
        in_specs=[anywhere] * (1 + len(after)),
        out_specs=anywhere,
        input_output_aliases={0: 0},
        compiler_params=pltpu.CompilerParams(vmem_limit_bytes=MIB),
        name="tie",
        cost_estimate=pl.CostEstimate(flops=0, bytes_accessed=0, transcendentals=0),
    )(v, *after)


class Place:
    def __init__(self, items, seqs):
        self.items, self.seqs, self.groups = items, seqs, seqs // 4
        self.count = items * seqs
        self.item, self.group, self.member = (lax.axis_index(name) for name in AXES)

    def swap(self, v, mask):
        return lax.ppermute(v, AXES, [(d, d ^ mask) for d in range(self.count)])

    def group_swap(self, v, k):
        return self.swap(v, 4 * k)

    def item_swap(self, v, k):
        return self.swap(v, self.seqs * k)

    def group_shift(self, v, k):
        pairs = []
        for d in range(self.count):
            g = (d % self.seqs) // 4 + k
            if 0 <= g < self.groups:
                pairs.append((d, d + 4 * k))
        return lax.ppermute(v, AXES, pairs)

    def spread(self, v):
        far = self.swap(v, 2)
        return [v, self.swap(v, 1), far, self.swap(far, 1)]

    def exchange(self, parts):
        return [parts[0]] + [self.swap(parts[d], d) for d in (1, 2, 3)]

    def collect_far(self, keep2, send3, after=()):
        pair = [keep2, self.swap(send3, 1)]
        (v,) = run("add", add_kernel, [like(keep2.shape, bf16)], [], pair, after=after)
        return v, self.swap(v, 2)

    def collect(self, keep0, send1, keep2, send3, after=()):
        far = self.collect_far(keep2, send3, after)[1]
        return [keep0, self.swap(send1, 1), far]

    def in_order(self, parts):
        out = None
        for m in (3, 2, 1, 0):
            v = jnp.concatenate([parts[m ^ k] for k in range(4)], 0)
            out = v if out is None else jnp.where(self.member == m, v, out)
        return out


def blocks_of(ref, count, size, first):
    if count == 1:
        return ref[...]
    return jnp.concatenate(
        [ref[:, pl.ds(pl.multiple_of((k ^ first) * size, size), size)] for k in range(count)], 1
    )


def rows_of(refs):
    if len(refs) == 1:
        return refs[0][...]
    return jnp.concatenate([r[...] for r in refs], 0)


def pack_kernel(own, hidden, wide, info, q, k, v, u, o, g, up, dn, *refs):
    outs, small, large, sems = refs[:4], refs[4], refs[5], refs[6]
    copies = [
        pltpu.make_async_copy(ref, small.at[n], sems.at[n]) for n, ref in enumerate((q, k, v, u, o))
    ] + [pltpu.make_async_copy(ref, large.at[n], sems.at[5 + n]) for n, ref in enumerate((g, up, dn))]
    for copy in copies:
        copy.start()
    for copy in copies:
        copy.wait()
    member = info[0]
    for m in range(4):

        @pl.when(member == m)
        def _():
            for d in range(4):
                j = m ^ d
                for n in range(5):
                    outs[d][:, n * own : (n + 1) * own] = small[n, :, j * own : (j + 1) * own]
                for n in range(3):
                    v = large[n, :, j * hidden : (j + 1) * hidden]
                    if wide != hidden:
                        v = jnp.concatenate(
                            [v, jnp.zeros((v.shape[0], wide - hidden), v.dtype)], 1
                        )
                    lo = 5 * own + n * wide
                    outs[d][:, lo : lo + wide] = v


def prep_kernel(count, block, info, x, c, h_out, c_out, scr):
    first = info[1]
    v = x[...].astype(f32)
    scr[...] = v * norm_factor(v)
    h_out[...] = blocks_of(scr, count, block, first).astype(bf16)
    scr[...] = c[...].astype(f32)
    c_out[...] = blocks_of(scr, count, block, first).astype(bf16)


def turn(v, cosine, sine):
    return v * cosine + pltpu.roll(v, v.shape[-1] // 2, 1) * sine


def project_kernel(nw, own, size, info, fac, *refs):
    h, w = refs[:4], refs[4 : 4 + nw]
    cosine, sine, qd, kd = refs[4 + nw : 8 + nw]
    q0, k0, u, v, q, k, qs, ks, prefix, total, out_w, local = refs[8 + nw :]
    member = info[0]
    out_w[...] = jnp.concatenate([r[:, 4 * own :] for r in w], 0)
    heads = own // size
    for d in range(4):
        weights = jnp.concatenate([r[:, : 4 * own] for r in w], 0)
        pre = mm(h[d][...], weights)
        q0[d] = pre[:, :own]
        k0[d] = pre[:, own : 2 * own]
        v[d] = pre[:, 2 * own : 3 * own].astype(bf16)
        u[d] = pre[:, 3 * own :]
        for n in range(heads):
            lanes = slice(n * size, (n + 1) * size)
            z = q0[d, :, lanes]
            act = turn(z * jax.nn.sigmoid(z), cosine[d], sine[d])
            q[d, :, lanes] = act.astype(bf16)
            qs[d, :, lanes] = (act * qd[n]).astype(bf16)
            z = k0[d, :, lanes]
            act = turn(z * jax.nn.sigmoid(z), cosine[d], sine[d])
            k[d, :, lanes] = act.astype(bf16)
            scaled = (act * kd[n]).astype(bf16)
            ks[d, :, lanes] = scaled
            local[member ^ d, n] = mm_tn(scaled, v[d, :, lanes])
    for n in range(heads):
        state = jnp.zeros((size, size), f32)
        for b in range(4):
            prefix[b, n] = state
            state = fac[n, 1] * state + local[b, n]
        total[n] = state


def scores_kernel(own, size, q, k, v, mask, w, intra):
    for d in range(4):
        for n in range(own // size):
            lanes = slice(n * size, (n + 1) * size)
            low = (mm_nt(q[d, :, lanes], k[d, :, lanes]) * mask[n]).astype(bf16)
            w[d, n] = low
            intra[d, :, lanes] = mm(low, v[d, :, lanes])


def attend_kernel(own, size, info, fac, prefix, before, qs, intra, u, plow, attn, *z):
    member = info[0]
    for d in range(4):
        b = member ^ d
        for n in range(own // size):
            lanes = slice(n * size, (n + 1) * size)
            low = (prefix[b, n] + fac[n, b] * before[n]).astype(bf16)
            plow[d, n] = low
            a = intra[d, :, lanes] + mm(qs[d, :, lanes], low)
            attn[d, :, lanes] = a
            z[d][:, lanes] = (a * norm_factor(a) * u[d, :, lanes]).astype(bf16)


def mid_kernel(count, block, own, info, x, *refs):
    z, o = refs[:4], refs[4:8]
    y, h2, zp, full, scr = refs[8:]
    member, first = info[0], info[1]
    for d in range(4):
        full[:, pl.ds(pl.multiple_of((member ^ d) * own, own), own)] = z[d][...]
    zp[...] = blocks_of(full, count, block, first)
    mixed = zp[...]
    for d in range(4):
        scr[:, pl.ds(pl.multiple_of((member ^ d) * own, own), own)] = mm(mixed, o[d][...])
    v = x[...].astype(f32) + scr[...]
    y[...] = v
    scr[...] = v * norm_factor(v)
    h2[...] = blocks_of(scr, count, block, first).astype(bf16)


def columns(refs, lo, hi):
    if len(refs) == 1:
        return refs[0][:, lo:hi]
    return jnp.concatenate([r[:, lo:hi] for r in refs], 0)


def columns(refs, lo, hi):
    if len(refs) == 1:
        return refs[0][:, lo:hi]
    return jnp.concatenate([r[:, lo:hi] for r in refs], 0)


def ffn_kernel(wide, h0, h1, c0, c1, *refs):
    h, c, w, outs = (h0, h1), (c0, c1), refs[:-8], refs[-8:]
    for d in range(2):
        hd, dg, df, part = outs[4 * d : 4 * d + 4]
        g = mm(h[d][...], columns(w, 0, wide))
        f = mm(h[d][...], columns(w, wide, 2 * wide))
        hd[...] = (g * f).astype(bf16)
        t = mm(c[d][...], columns(w, 2 * wide, 3 * wide))
        dg[...] = (t * f).astype(bf16)
        df[...] = (t * g).astype(bf16)
        v = mm_nt(dg[...], columns(w, 0, wide)) + mm_nt(df[...], columns(w, wide, 2 * wide))
        part[...] = v.astype(part.dtype)


def ffn_out_kernel(wide, h0, h1, h2, h3, *refs):
    w, outs = refs[:-4], refs[-4:]
    for d, h in enumerate((h0, h1, h2, h3)):
        outs[d][...] = mm_nt(h[...], columns(w, 2 * wide, 3 * wide)).astype(outs[d].dtype)


def store_grads(outs, items, groups, rows, lanes, value):
    half = groups // 2
    for part, one, two in ((0, 1, 2), (1, 2, 1)):
        send, keep2, keep0 = outs[3 * part : 3 * part + 3]
        for i in range(items):
            lo = (i * groups + part * half) * rows
            v = value[lo : lo + half * rows].astype(bf16)
            if i == 0:
                keep0[:, lanes] = v
            elif i == two:
                keep2[:, lanes] = v
            else:
                send[0 if i == one else 1, :, lanes] = v


def hidden_grad_kernel(items, groups, rows, wide, *refs):
    h, dg, df = (refs[4 * n : 4 * n + 4] for n in range(3))
    left = jnp.concatenate([r[...] for r in h], 0)
    for n, right in enumerate((dg, df)):
        value = mm_tn(left, jnp.concatenate([r[...] for r in right], 0))
        store_grads(refs[12:], items, groups, rows, slice(n * wide, (n + 1) * wide), value)


def down_side_kernel(items, groups, rows, wide, own, *refs):
    c, h, hd, du, og, outs = refs[:4], refs[4:8], refs[8:12], refs[12], refs[13:16], refs[16:]
    left = jnp.concatenate([r[...] for r in c], 0)
    value = mm_tn(left, jnp.concatenate([r[...] for r in hd], 0))
    store_grads(outs, items, groups, rows, slice(0, wide), value)
    left = jnp.concatenate([r[...] for r in h], 0)
    value = mm_tn(left, jnp.concatenate([du[d] for d in range(4)], 0))
    store_grads(outs, items, groups, rows, slice(wide, wide + own), value)
    value = og[0][...].astype(f32) + og[1][...].astype(f32) + og[2][...].astype(f32)
    store_grads(outs, items, groups, rows, slice(wide + own, wide + 2 * own), value)


def next_kernel(keep2, got, out):
    out[...] = (keep2[...].astype(f32) + got[1].astype(f32)).astype(bf16)


def sum_kernel(half, *refs):
    parts, outs = (refs[0:3], refs[3:6]), refs[6:]
    rows = outs[0].shape[0]
    for k, out in enumerate(outs):
        keep0, got, far = parts[k // half]
        at = slice((k % half) * rows, (k % half + 1) * rows)
        v = keep0[at].astype(f32) + got[0, at].astype(f32) + far[at].astype(f32)
        out[...] = v.astype(out.dtype)


def add_kernel(keep, got, out):
    out[...] = (keep[...] + got[...].astype(f32)).astype(bf16)


def split_kernel(pieces, info, *refs):
    outs = refs[-4:]
    member = info[0]
    rows = outs[0].shape[0]
    lo = 0
    while len(refs) > 4:
        total, away = refs[0], refs[1:pieces]
        refs = refs[pieces:]
        cols = slice(lo, lo + total.shape[1])
        lo += total.shape[1]
        for d in range(4):
            at = pl.ds(pl.multiple_of((member ^ d) * rows, rows), rows)
            v = total[at, :]
            for r in away:
                v = v + r[at, :].astype(f32)
            outs[d][:, cols] = v.astype(outs[d].dtype)


def mid_back_kernel(count, block, own, info, y, cot, a0, a1, a2, *refs):
    o = refs[:4]
    dy, do, z0, z1, z2, z3, scr = refs[4:]
    z = (z0, z1, z2, z3)
    member, first = info[0], info[1]
    scr[...] = a0[...] + a1[...].astype(f32) + a2[...].astype(f32)
    grad = blocks_of(scr, count, block, first)
    v = y[...]
    scale = norm_factor(v)
    v = cot[...].astype(f32) + norm_back(v * scale, scale, grad)
    dy[...] = v
    do[...] = v.astype(bf16)
    total = None
    for d in range(4):
        part = do[:, pl.ds(pl.multiple_of((member ^ d) * own, own), own)]
        t = mm_nt(part, o[d][...])
        total = t if total is None else total + t
    scr[...] = total
    scr[...] = blocks_of(scr, count, block, first)
    for d in range(4):
        z[d][...] = scr[:, pl.ds(pl.multiple_of((member ^ d) * own, own), own)].astype(bf16)


def out_grad_kernel(own, info, zp, do, *outs):
    member = info[0]
    left = zp[...].T
    for d in range(4):
        part = do[:, pl.ds(pl.multiple_of((member ^ d) * own, own), own)]
        outs[d][...] = mm(left, part).astype(outs[d].dtype)


def back_state_kernel(own, size, info, fac, z0, z1, z2, z3, attn, u, qs, du, da, suffix, total, local):
    member = info[0]
    z = (z0, z1, z2, z3)
    heads = own // size
    for d in range(4):
        for n in range(heads):
            lanes = slice(n * size, (n + 1) * size)
            dz = z[d][:, lanes].astype(f32)
            a = attn[d, :, lanes]
            scale = norm_factor(a)
            normed = a * scale
            du[d, :, lanes] = (dz * normed).astype(bf16)
            low = norm_back(normed, scale, dz * u[d, :, lanes]).astype(bf16)
            da[d, :, lanes] = low
            local[member ^ d, n] = mm_tn(qs[d, :, lanes], low)
    for n in range(heads):
        state = jnp.zeros((size, size), f32)
        for b in (3, 2, 1, 0):
            suffix[b, n] = state
            state = fac[n, 1] * state + local[b, n]
        total[n] = state


def back_local_kernel(own, size, da, v, w, q, k, plow, mask, qd, dq, dk, dv):
    for d in range(4):
        for n in range(own // size):
            lanes = slice(n * size, (n + 1) * size)
            a = da[d, :, lanes]
            ds = (mm_nt(a, v[d, :, lanes]) * mask[n]).astype(bf16)
            dq[d, :, lanes] = mm(ds, k[d, :, lanes]) + mm_nt(a, plow[d, n]) * qd[n]
            dk[d, :, lanes] = mm_tn(ds, q[d, :, lanes])
            dv[d, :, lanes] = mm_tn(w[d, n], a)


def back_final_kernel(nw, own, size, info, fac, suffix, after, v, ks, du, dq, dk, dv, q0, k0, cosine, sine, kd, *refs):
    w, outs = refs[:nw], refs[nw:]
    grads = outs[0]
    parts = outs[1:]
    member = info[0]
    for d in range(4):
        b = member ^ d
        for n in range(own // size):
            lanes = slice(n * size, (n + 1) * size)
            low = (suffix[b, n] + fac[n, 3 - b] * after[n]).astype(bf16)
            dka = dk[d, :, lanes] + mm_nt(v[d, :, lanes], low) * kd[n]
            dvv = dv[d, :, lanes] + mm(ks[d, :, lanes], low)
            z = q0[d, :, lanes]
            s = jax.nn.sigmoid(z)
            g = turn(dq[d, :, lanes], cosine[d], -sine[d]) * s * (1.0 + z * (1.0 - s))
            grads[d, :, n * size : (n + 1) * size] = g.astype(bf16)
            z = k0[d, :, lanes]
            s = jax.nn.sigmoid(z)
            g = turn(dka, cosine[d], -sine[d]) * s * (1.0 + z * (1.0 - s))
            grads[d, :, own + n * size : own + (n + 1) * size] = g.astype(bf16)
            grads[d, :, 2 * own + n * size : 2 * own + (n + 1) * size] = dvv.astype(bf16)
        grads[d, :, 3 * own :] = du[d]
        weights = jnp.concatenate([r[:, : 4 * own] for r in w], 0)
        parts[d][...] = mm_nt(grads[d], weights).astype(parts[d].dtype)


def attn_grad_kernel(items, groups, rows, wide, h0, h1, h2, h3, grads, *outs):
    left = jnp.concatenate([h0[...], h1[...], h2[...], h3[...]], 0)
    value = mm_tn(left, jnp.concatenate([grads[d][:, :wide] for d in range(4)], 0))
    store_grads(outs, items, groups, rows, slice(0, wide), value)


def first_back_kernel(count, block, info, x, dy, a0, a1, a2, out, scr):
    scr[...] = a0[...] + a1[...].astype(f32) + a2[...].astype(f32)
    grad = blocks_of(scr, count, block, info[1])
    v = x[...].astype(f32)
    scale = norm_factor(v)
    out[...] = dy[...] + norm_back(v * scale, scale, grad)


def mixed_kernel(count, block, info, y, a0, a1, a2, out, scr):
    scr[...] = a0[...] + a1[...].astype(f32) + a2[...].astype(f32)
    out[...] = (y[...] + blocks_of(scr, count, block, info[1])).astype(bf16)


def final_kernel(widths, own_cols, info, p0, p1, p2, p3, *outs):
    member = info[0]
    parts = (p0, p1, p2, p3)
    for m in range(4):

        @pl.when(member == m)
        def _():
            for d in range(4):
                j = m ^ d
                lo = 0
                for out, wide, cols in zip(outs, widths, own_cols):
                    out[:, j * cols : (j + 1) * cols] = parts[d][:, lo : lo + cols].astype(f32)
                    lo += wide


def scatter_split(at, info, aligned, sums):
    if aligned:
        rows = sums[0][0].shape[0] // 4
        cols = sum(v[0].shape[1] for v in sums)
        parts = run(
            "split",
            functools.partial(split_kernel, len(sums[0])),
            [like((rows, cols), f32)] + [like((rows, cols), bf16)] * 3,
            [info],
            [v for group in sums for v in group],
        )
    else:
        total = jnp.concatenate([sum(v.astype(f32) for v in group) for group in sums], 1)
        rows = total.shape[0] // 4
        parts = [
            lax.dynamic_slice_in_dim(total, (at.member ^ d) * rows, rows, 0) for d in range(4)
        ]
        parts = [parts[0]] + [v.astype(bf16) for v in parts[1:]]
    return at.exchange(parts)


def rotation_tables(positions, head_size):
    half_width = head_size // 2
    pair_index = jnp.arange(half_width, dtype=jnp.int32)
    step_sizes = jnp.right_shift(jnp.full((half_width,), 8192, jnp.int32), pair_index // 5)
    phase_int = positions[:, None] * step_sizes[None, :] % 65536
    angles = phase_int.astype(f32) * (2.0 * math.pi / 65536.0)
    return (jnp.cos(angles), jnp.sin(angles))


def make_body(items, seqs):
    def body(
        tokens,
        decay_rate,
        query_weight,
        key_weight,
        value_weight,
        update_weight,
        output_weight,
        gate_weight,
        up_weight,
        down_weight,
        cotangent,
    ):
        at = Place(items, seqs)
        groups = at.groups
        width = tokens.shape[-1]
        rows = tokens.shape[1]
        heads = decay_rate.shape[0]
        size = width // heads
        own_heads = heads // 4
        own = width // 4
        shard = query_weight.shape[0]
        hidden = gate_weight.shape[1] // 4
        wide = hidden + -hidden % 256
        count, block = items * groups, 4 * shard
        first = at.item * groups + at.group
        aligned = block % 128 == 0
        if aligned:
            info = jnp.stack([at.member, first])
            kcount, kblock = count, block
        else:
            info = jnp.stack([at.member, jnp.zeros_like(first)])
            kcount, kblock = 1, width
        info = info.astype(jnp.int32)

        def arrange(pieces):
            if aligned:
                return pieces
            v = jnp.stack(pieces)
            return [v[jnp.arange(count) ^ first].reshape(width, -1)]

        def act(dtype=bf16):
            return like((rows, width), dtype)

        blk = functools.partial(like, (4, rows, own))
        x = tokens.reshape(rows, width)
        cot = cotangent.reshape(rows, width)

        half = groups // 2
        packed = pl.pallas_call(
            functools.partial(pack_kernel, own, hidden, wide),
            out_shape=[like((shard, 5 * own + 3 * wide), bf16)] * 4,
            in_specs=[pl.BlockSpec(memory_space=pltpu.SMEM)]
            + [pl.BlockSpec(memory_space=pltpu.HBM)] * 8,
            out_specs=[pl.BlockSpec(memory_space=pltpu.VMEM)] * 4,
            scratch_shapes=[
                pltpu.VMEM((5, shard, width), bf16),
                pltpu.VMEM((3, shard, 4 * hidden), bf16),
                pltpu.SemaphoreType.DMA((8,)),
            ],
            compiler_params=pltpu.CompilerParams(vmem_limit_bytes=56 * MIB),
            cost_estimate=pl.CostEstimate(flops=0, bytes_accessed=0, transcendentals=0),
            name="pack",
        )(
            info,
            query_weight,
            key_weight,
            value_weight,
            update_weight,
            output_weight,
            gate_weight,
            up_weight,
            down_weight.T,
        )
        packed = at.exchange(packed)
        aw = at.in_order([v[:, : 5 * own] for v in packed])
        fw = at.in_order([v[:, 5 * own :] for v in packed])
        near = [aw] + [at.group_swap(aw, k) for k in range(1, groups)]


        def sides(piece, kk):
            one, two = (1, 2) if kk < half else (2, 1)
            return {one: at.item_swap(piece, one), two: at.item_swap(piece, two)}

        def corner(got, kk, after=()):
            one, two = (1, 2) if kk < half else (2, 1)
            if after:
                got[one] = tie(got[one], *after)
            got[3] = at.item_swap(got[one], two)
            return got

        attn_p = [corner(sides(near[k], k), k) for k in range(groups)]
        h1_own, cot_own = run(
            "prep",
            functools.partial(prep_kernel, kcount, kblock),
            [act(), act()],
            [info],
            [x, cot],
            [pltpu.VMEM((rows, width), f32)],
        )
        h1_own = tie(h1_own, aw)
        h1_far = at.swap(h1_own, 2)
        fw = tie(fw, attn_p[0][1], attn_p[0][2], near[-1], h1_far)
        h1 = [h1_own, at.swap(h1_own, 1), h1_far, at.swap(h1_far, 1)]
        far_f = [fw] + [at.group_swap(fw, k) for k in range(1, groups)]
        ffn_p = [sides(far_f[k], k) for k in range(half)]
        early = far_f[1:] + [v for got in ffn_p for v in got.values()]
        attn_w = arrange([near[k] if i == 0 else attn_p[k][i] for i in range(items) for k in range(groups)])
        nw = len(attn_w)

        blocks = at.group * 4 + (at.member ^ jnp.arange(4, dtype=jnp.int32))
        positions = (blocks[:, None] * rows + jnp.arange(rows, dtype=jnp.int32)).reshape(-1)
        cosine, sine = rotation_tables(positions, size)
        cosine = jnp.concatenate([cosine, cosine], 1).reshape(4, rows, size)
        sine = jnp.concatenate([-sine, sine], 1).reshape(4, rows, size)
        log_decay = lax.dynamic_slice(jnp.log(decay_rate), (at.member * own_heads,), (own_heads,))
        local = jnp.arange(rows).astype(f32)
        ld = log_decay[:, None]
        query_decay = jnp.broadcast_to(
            jnp.exp(ld * (local + 1.0))[:, :, None], (own_heads, rows, size)
        )
        key_decay = jnp.broadcast_to(
            jnp.exp(ld * (rows - 1.0 - local))[:, :, None], (own_heads, rows, size)
        )
        offset = local[:, None] - local[None, :]
        mask = jnp.where(
            offset >= 0.0, jnp.exp(log_decay[:, None, None] * jnp.maximum(offset, 0.0)), 0.0
        )
        fac = jnp.exp(ld * rows * jnp.arange(4).astype(f32))
        group_fac = jnp.exp(log_decay * (4.0 * rows))[:, None, None]

        state = like((own_heads, size, size), f32)
        states = like((4, own_heads, size, size), f32)
        states_low = like((4, own_heads, size, size), bf16)
        scratch_states = pltpu.VMEM((4, own_heads, size, size), f32)

        def carried(total, sign):
            out = at.group_shift(total, sign)
            weight = group_fac
            for k in range(2, groups):
                out = out + weight * at.group_shift(total, sign * k)
                weight = weight * group_fac
            return out

        q0, k0, u, v, q, k, qs, ks, prefix, total, out_w = run(
            "project",
            functools.partial(project_kernel, nw, own, size),
            [blk(f32), blk(f32), blk(f32)] + [blk(bf16)] * 5 + [states, state, like((width, own), bf16)],
            [info, fac],
            h1 + attn_w + [cosine, sine, query_decay, key_decay],
            [scratch_states],
            after=early,
            flops=8 * rows * width * 4 * own,
            vmem=VM[0],
        )
        before = carried(total, 1)
        out_far = at.swap(out_w, 2)
        out_core = at.swap(out_w, 1)
        cot_own = tie(cot_own, prefix)
        cot_far = at.swap(cot_own, 2)
        w, intra = run(
            "scores",
            functools.partial(scores_kernel, own, size),
            [like((4, own_heads, rows, rows), bf16), blk(f32)],
            [],
            [q, k, v, mask],
            flops=16 * rows * rows * own,
        )
        plow, attn, *z = run(
            "attend",
            functools.partial(attend_kernel, own, size),
            [states_low, blk(f32)] + [like((rows, own), bf16)] * 4,
            [info, fac],
            [prefix, before, qs, intra, u],
            flops=8 * rows * size * own,
            after=[out_core],
        )
        z = at.exchange(z)
        out_far = tie(out_far, attn)
        out_w = [out_w, out_core, out_far, at.swap(out_far, 1)]
        for kk in range(half, groups):
            far_f[kk] = tie(far_f[kk], prefix)
            ffn_p.append(sides(far_f[kk], kk))
        y, h2_own, zp = run(
            "mid",
            functools.partial(mid_kernel, kcount, kblock, own),
            [act(f32), act(), act()],
            [info],
            [x] + z + out_w,
            [pltpu.VMEM((rows, width), bf16), pltpu.VMEM((rows, width), f32)],
            flops=2 * rows * width * width,
            after=[v for got in ffn_p[half:] for v in got.values()],
        )
        cot_far = tie(cot_far, y)
        cots = [cot_own, at.swap(cot_own, 1), cot_far, at.swap(cot_far, 1)]
        h2 = at.spread(h2_own)
        for kk in range(groups):
            corner(ffn_p[kk], kk, [y])
        ffn_w = arrange(
            [far_f[kk] if i == 0 else ffn_p[kk][i] for i in range(items) for kk in range(groups)]
        )

        hid = like((rows, wide), bf16)
        def gated(a, b, after):
            return run(
                "ffn%d" % a,
                functools.partial(ffn_kernel, wide),
                [hid] * 3 + [act(f32)] + [hid] * 3 + [act()],
                [],
                [h2[a], h2[b], cots[a], cots[b]] + ffn_w,
                vmem=VM[1],
                after=after,
            )

        late = gated(2, 3, [])
        added, mid_far = at.collect_far(late[3], late[7])
        soon = gated(0, 1, [added])
        hd, dg, df = ([soon[n], soon[4 + n], late[n], late[4 + n]] for n in range(3))
        mid_sums = [soon[3], at.swap(soon[7], 1), mid_far]

        def item_blocks(g):
            g = g.astype(bf16).reshape(count, block, -1)[jnp.arange(count) ^ first]
            g = g.reshape(items, groups * block, -1)
            return [g[i] for i in range(items)]

        def halves(g):
            g = item_blocks(g)
            res = []
            for p, one, two in ((0, 1, 2), (1, 2, 1)):
                t = [v[p * half * block : (p + 1) * half * block] for v in g]
                res += [jnp.stack([t[one], t[3]]), t[two], t[0]]
            return res

        def grad_outs(cols):
            return [
                like((2, half * block, cols), bf16),
                like((half * block, cols), bf16),
                like((half * block, cols), bf16),
            ] * 2

        def first_hop(outs):
            return [at.item_swap(outs[0], 1), at.item_swap(outs[3], 2)]

        def second_hop(outs, got, after=()):
            res = []
            for p, two in ((0, 2), (1, 1)):
                keep2, keep0 = outs[3 * p + 1 : 3 * p + 3]
                (v,) = run(
                    "next", next_kernel, [like(keep2.shape, bf16)], [], [keep2, got[p]], after=after
                )
                res += [keep0, got[p], at.item_swap(v, two)]
            return res

        def third_hop(parts, after=()):
            cols = parts[0].shape[1]
            res = run(
                "sum",
                functools.partial(sum_kernel, half),
                [like((block, cols), f32)] + [like((block, cols), bf16)] * (groups - 1),
                [],
                parts,
                after=after,
            )
            return [res[0]] + [at.group_swap(res[k], k) for k in range(1, groups)]

        if aligned:
            hidden_outs = run(
                "hidden_grad",
                functools.partial(hidden_grad_kernel, items, groups, block, wide),
                grad_outs(2 * wide),
                [],
                h2 + dg + df,
                vmem=VM[2],
            )
        else:
            both = [jnp.concatenate(dg, 0), jnp.concatenate(df, 0)]
            hidden_outs = halves(
                jnp.concatenate([mm_tn(jnp.concatenate(h2, 0), v) for v in both], 1)
            )
        hidden_got = first_hop(hidden_outs)

        dy, do, *dz = run(
            "mid_back",
            functools.partial(mid_back_kernel, kcount, kblock, own),
            [act(f32), act()] + [like((rows, own), bf16)] * 4,
            [info],
            [y, cot] + mid_sums + out_w,
            [pltpu.VMEM((rows, width), f32)],
            flops=2 * rows * width * width,
            after=[hidden_outs[0]],
        )
        dz = at.exchange(dz)
        ffn_parts = run(
            "ffn_out",
            functools.partial(ffn_out_kernel, wide),
            [act(f32), act(), act(f32), act()],
            [],
            hd + ffn_w,
            flops=8 * rows * width * wide,
            vmem=VM[3],
        )
        out_sums = at.collect(*ffn_parts)

        og = run(
            "out_grad",
            functools.partial(out_grad_kernel, own),
            [like((width, own), f32), like((width, own), bf16)] * 2,
            [info],
            [zp, do],
            flops=2 * rows * width * width,
        )

        du, da, suffix, gtotal = run(
            "back_state",
            functools.partial(back_state_kernel, own, size),
            [blk(bf16), blk(bf16), states, state],
            [info, fac],
            dz + [attn, u, qs],
            [scratch_states],
            flops=8 * rows * size * own,
            after=[ffn_parts[0]],
        )
        after = carried(gtotal, -1)
        og = at.collect(*og, after=[du])
        hidden_parts = second_hop(hidden_outs, hidden_got, [du])
        dq, dk, dv = run(
            "back_local",
            functools.partial(back_local_kernel, own, size),
            [blk(f32)] * 3,
            [],
            [da, v, w, q, k, plow, mask, query_decay],
            flops=40 * rows * rows * own,
        )
        if aligned:
            ds_outs = run(
                "down_side",
                functools.partial(down_side_kernel, items, groups, block, wide, own),
                grad_outs(wide + 2 * own),
                [],
                cots + h1 + hd + [du] + og,
                flops=8 * rows * width * (wide + own),
                vmem=VM[2],
                after=[dq],
            )
        else:
            hh, cc = jnp.concatenate(h1, 0), jnp.concatenate(cots, 0)
            both = [
                mm_tn(cc, jnp.concatenate(hd, 0)),
                mm_tn(hh, du.reshape(4 * rows, own)),
                sum(v.astype(f32) for v in og),
            ]
            ds_outs = halves(jnp.concatenate(both, 1))
        ds_got = first_hop(ds_outs)
        grads, *part = run(
            "back_final",
            functools.partial(back_final_kernel, nw, own, size),
            [like((4, rows, 4 * own), bf16), act(f32), act(), act(f32), act()],
            [info, fac],
            [suffix, after, v, ks, du, dq, dk, dv, q0, k0, cosine, sine, key_decay] + attn_w,
            flops=8 * rows * width * 4 * own,
            vmem=VM[0],
        )
        if aligned:
            attn_outs = run(
                "attn_grad",
                functools.partial(attn_grad_kernel, items, groups, block, 3 * own),
                grad_outs(3 * own),
                [],
                h1 + [grads],
                flops=6 * rows * width * 4 * own,
                vmem=VM[2],
                after=[hidden_parts[2], hidden_parts[5]],
            )
        else:
            attn_outs = halves(mm_tn(hh, grads[:, :, : 3 * own].reshape(4 * rows, 3 * own)))
        attn_got = first_hop(attn_outs)
        in_sums = at.collect(*part)
        hidden_sums = third_hop(hidden_parts)
        ds_sums = third_hop(second_hop(ds_outs, ds_got, [attn_outs[0], hidden_sums[-1]]))
        attn_sums = third_hop(second_hop(attn_outs, attn_got))
        hidden_own = scatter_split(at, info, aligned, [hidden_sums])
        rest_own = scatter_split(at, info, aligned, [attn_sums, ds_sums])
        (mixed,) = run(
            "mixed",
            functools.partial(mixed_kernel, kcount, kblock),
            [act()],
            [info],
            [y] + out_sums,
            [pltpu.VMEM((rows, width), f32)],
            after=[attn_outs[0]],
        )
        tokens_grad = run(
            "first_back",
            functools.partial(first_back_kernel, kcount, kblock),
            [act(f32)],
            [info],
            [x, dy] + in_sums,
            [pltpu.VMEM((rows, width), f32)],
        )[0]
        gg, pg = run(
            "final_hidden",
            functools.partial(final_kernel, (wide,) * 2, (hidden,) * 2),
            [like((shard, 4 * hidden), f32)] * 2,
            [info],
            hidden_own,
        )
        qg, kg, vg, ng, ug, wg = run(
            "final_rest",
            functools.partial(
                final_kernel, (own,) * 3 + (wide,) + (own,) * 2, (own,) * 3 + (hidden,) + (own,) * 2
            ),
            [like((shard, width), f32)] * 3
            + [like((shard, 4 * hidden), f32)]
            + [like((shard, width), f32)] * 2,
            [info],
            rest_own,
        )
        return (
            mixed.reshape(tokens.shape),
            tokens_grad.reshape(tokens.shape),
            qg,
            kg,
            vg,
            ug,
            wg,
            gg,
            pg,
            ng.T,
        )

    return body


def solution(mesh):
    items, seqs = mesh.shape["items"], mesh.shape["seq"]
    parts = jax.sharding.Mesh(mesh.devices.reshape(items, seqs // 4, 4), AXES)
    act = P("items", ("group", "member"), None)
    row = P(AXES, None)
    col = P(None, AXES)
    return jax.shard_map(
        make_body(items, seqs),
        mesh=parts,
        in_specs=(act, P()) + (row,) * 7 + (col, act),
        out_specs=(act, act) + (row,) * 7 + (col,),
        check_vma=False,
    )
```

profile of v0, /device:TPU:0, one launch (start us, length us, event | category | flops | bytes accessed | tf_op | source)
XLA Modules:
  0.0 274.3 jit_solution(11893718448755978878)
XLA Ops:
  1.3 3.1 %pack.1 = (bf16[32,3584]{1,0:T(8,128)(2,1)}, bf16[32,3584]{1,0:T(8,128)(2,1)}, bf16[32,3584]{1,0:T(8,128)(2,1)}, bf16[32,3584]{1,0:T(8,128)(2,1)}) custom-call(s32[2]{0:T(128)} %pad_add_fusion.refs_0_.info, bf16[32,1024]{1,0:T(8,128)(2,1)} %q.1, bf16[32,1024]{1,0:T(8,128)(2,1)} %k.1, bf16[32,1024]{1,0:T(8,128)(2,1)} %v.1, bf16[32,1024]{1,0:T(8,128)(2,1)} %u.1, ...), custom_call_target="tpu_custom_call" | custom-call | tf_op jit(solution)/shard_map/pack/pallas_call | solution.py:561
  4.8 2.6 collective-permute-start.1
  11.0 2.1 fusion.5
  14.2 4.4 %collective-permute-done.2 = bf16[32,3584]{1,0:T(8,128)(2,1)S(1)} collective-permute-done((bf16[32,3584]{1,0:T(8,128)(2,1)}, bf16[32,3584]{1,0:T(8,128)(2,1)S(1)}, u32[]{:S(2)}, u32[]{:S(2)}) %collective-permute-start.2) | collective-permute-done | bytes 229408 | tf_op jit(solution)/shard_map/ppermute | solution.py:86
  18.7 1.6 collective-permute-start.7
  20.2 2.6 collective-permute-start.6
  22.8 1.6 collective-permute-start.4
  24.8 1.6 collective-permute-start.9
  26.5 2.0 collective-permute-done.7.refs_1_.refs_8_.refs_17_
  28.5 1.7 collective-permute-start.11
  30.1 7.7 %collective-permute-done.6.refs_3_.refs_7_.refs_16_ = bf16[128,1280]{1,0:T(8,128)(2,1)S(1)} collective-permute-done((bf16[128,1280]{1,0:T(8,128)(2,1)S(1)}, bf16[128,1280]{1,0:T(8,128)(2,1)S(1)}, u32[]{:S(2)}, u32[]{:S(2)}) %collective-permute-start.6) | collective-permute-done | bytes 327712 | tf_op jit(solution)/shard_map/ppermute | solution.py:86
  37.9 1.5 collective-permute-start.10
  40.2 2.1 collective-permute-done.4.refs_4_.refs_2_.refs_6_
  42.3 1.5 collective-permute-start.15
  45.6 3.8 %collective-permute-done.10.refs_11_.refs_20_ = bf16[128,1280]{1,0:T(8,128)(2,1)S(1)} collective-permute-done((bf16[128,1280]{1,0:T(8,128)(2,1)S(1)}, bf16[128,1280]{1,0:T(8,128)(2,1)S(1)}, u32[]{:S(2)}, u32[]{:S(2)}) %collective-permute-start.10) | collective-permute-done | bytes 327712 | tf_op jit(solution)/shard_map/ppermute | solution.py:86
  50.9 16.8 %collective-permute-done.12.refs_13_.refs_22_ = bf16[128,1280]{1,0:T(8,128)(2,1)S(1)} collective-permute-done((bf16[128,1280]{1,0:T(8,128)(2,1)S(1)}, bf16[128,1280]{1,0:T(8,128)(2,1)S(1)}, u32[]{:S(2)}, u32[]{:S(2)}) %collective-permute-start.12) | collective-permute-done | bytes 327712 | tf_op jit(solution)/shard_map/ppermute | solution.py:86
  67.7 3.6 %collective-permute-done.13.refs_18_.refs_0_ = bf16[128,2304]{1,0:T(8,128)(2,1)S(1)} collective-permute-done((bf16[128,2304]{1,0:T(8,128)(2,1)S(1)}, bf16[128,2304]{1,0:T(8,128)(2,1)S(1)}, u32[]{:S(2)}, u32[]{:S(2)}) %collective-permute-start.13) | collective-permute-done | bytes 589856 | tf_op jit(solution)/shard_map/ppermute | solution.py:86
  71.7 3.9 %project.1 = (f32[4,256,256]{2,1,0:T(8,128)S(1)}, f32[4,256,256]{2,1,0:T(8,128)S(1)}, f32[4,256,256]{2,1,0:T(8,128)S(1)}, bf16[4,256,256]{2,1,0:T(8,128)(2,1)S(1...) custom-call(s32[2]{0:T(128)S(1)} %copy-done.3, ...), custom_call_target="tpu_custom_call" | custom-call | flops 2147483648 | bytes 13238272 | tf_op jit(solution)/shard_map/project/pallas_call | solution.py:51
  75.9 1.6 collective-permute-start.24
  78.0 5.1 %collective-permute-start.16 = (f32[2,128,128]{2,1,0:T(8,128)S(1)}, f32[2,128,128]{2,1,0:T(8,128)S(1)}, u32[]{:S(2)}, u32[]{:S(2)}) collective-permute-start(f32[2,128,128]{2,1,0:T(8,128)S(1)} %get-tuple-element.126), channel_id=1, source_target_pairs={{0,4},{1,5},{2,6},{3,7},{8,12},{9,13},{10,14},{11,15},{16,20},{17,... | collective-permute-start | bytes 393224 | tf_op jit(solution)/shard_map/ppermute | solution.py:100
  84.2 5.2 %collective-permute-done.16.refs_3_ = f32[2,128,128]{2,1,0:T(8,128)S(1)} collective-permute-done((f32[2,128,128]{2,1,0:T(8,128)S(1)}, f32[2,128,128]{2,1,0:T(8,128)S(1)}, u32[]{:S(2)}, u32[]{:S(2)}) %collective-permute-start.16) | collective-permute-done | bytes 131104 | tf_op jit(solution)/shard_map/ppermute | solution.py:100
  93.0 1.9 collective-permute-start.31
  94.9 2.5 collective-permute-done.19.refs_4_
  98.4 1.7 mid.1
  100.2 1.4 collective-permute-start.29
  102.2 1.4 collective-permute-start.28
  103.6 7.9 %collective-permute-done.31.refs_0_ = bf16[256,1024]{1,0:T(8,128)(2,1)S(1)} collective-permute-done((bf16[256,1024]{1,0:T(8,128)(2,1)S(1)}, bf16[256,1024]{1,0:T(8,128)(2,1)S(1)}, u32[]{:S(2)}, u32[]{:S(2)}) %collective-permute-start.31) | collective-permute-done | bytes 524320 | tf_op jit(solution)/shard_map/ppermute | solution.py:86
  111.5 10.3 %collective-permute-done.29.refs_0_.refs_2_ = bf16[256,1024]{1,0:T(8,128)(2,1)S(1)} collective-permute-done((bf16[256,1024]{1,0:T(8,128)(2,1)S(1)}, bf16[256,1024]{1,0:T(8,128)(2,1)S(1)}, u32[]{:S(2)}, u32[]{:S(2)}) %collective-permute-start.29) | collective-permute-done | bytes 524320 | tf_op jit(solution)/shard_map/ppermute | solution.py:86
  121.8 1.9 collective-permute-done.30.refs_1_.refs_3_
  123.7 5.1 %ffn2.1 = (bf16[256,768]{1,0:T(8,128)(2,1)S(1)}, bf16[256,768]{1,0:T(8,128)(2,1)S(1)}, bf16[256,768]{1,0:T(8,128)(2,1)S(1)}, f32[256,1024]{1,0:T(8,128)S(1)}, bf...) custom-call(bf16[256,1024]{1,0:T(8,128)(2,1)S(1)} %collective-permut, ...), custom_call_target="tpu_custom_call" | custom-call | tf_op jit(solution)/shard_map/ffn2/pallas_call | solution.py:51
  132.3 5.1 %ffn0.1 = (bf16[256,768]{1,0:T(8,128)(2,1)S(1)}, bf16[256,768]{1,0:T(8,128)(2,1)S(1)}, bf16[256,768]{1,0:T(8,128)(2,1)S(1)}, f32[256,1024]{1,0:T(8,128)S(1)}, bf...) custom-call(bf16[256,1024]{1,0:T(8,128)(2,1)S(1)} %get-tuple-element, ...), custom_call_target="tpu_custom_call" | custom-call | tf_op jit(solution)/shard_map/ffn0/pallas_call | solution.py:51
  137.6 17.6 %hidden_grad.1 = (bf16[2,128,1536]{2,1,0:T(8,128)(2,1)S(1)}, bf16[128,1536]{1,0:T(8,128)(2,1)S(1)}, bf16[128,1536]{1,0:T(8,128)(2,1)S(1)}, bf16[2,128,1536]{2,1,...) custom-call(bf16[256,1024]{1,0:T(8,128)(2,1)S(1)} %get-tuple-element.140.refs_0_, ...), custom_call_target="tpu_custom_call" | custom-call | tf_op jit(solution)/shard_map/hidden_grad/pallas_call | solution.py:51
  155.3 2.3 mid_back.1
  157.5 1.3 out_grad.1
  159.9 1.4 collective-permute-start.43
  163.1 1.8 ffn_out.1
  165.0 2.6 collective-permute-done.40.refs_4_
  167.6 2.0 collective-permute-done.41.refs_5_
  169.6 1.8 back_state.1
  172.3 6.5 %collective-permute-done.45.refs_1_.refs_4_ = bf16[2,128,1536]{2,1,0:T(8,128)(2,1)S(1)} collective-permute-done((bf16[2,128,1536]{2,1,0:T(8,128)(2,1)S(1)}, bf16[2,128,1536]{2,1,0:T(8,128)(2,1)S(1)}, u32[]{:S(2)}, u32[]{:S(2)}) %collective-permute-start.45) | collective-permute-done | bytes 786464 | tf_op jit(solution)/shard_map/ppermute | solution.py:86
  179.0 1.6 collective-permute-start.46
  182.5 2.5 back_local.1
  185.0 2.3 collective-permute-done.57.refs_15_
  187.4 2.7 down_side.1
  190.7 1.4 collective-permute-start.61
  192.4 2.4 collective-permute-start.59
  194.9 4.1 %back_final.1 = (bf16[4,256,1024]{2,1,0:T(8,128)(2,1)S(1)}, f32[256,1024]{1,0:T(8,128)S(1)}, bf16[256,1024]{1,0:T(8,128)(2,1)S(1)}, f32[256,1024]{1,0:T(8,128)S(1)}, bf16[256,1024]{1,0:T(8,128)(2,1)S(1)}) custom-call(s32[2]{0:T(128)S(1)} %copy-done.3, f32[2,4]{1,0:T(2,128)S(1)} %multiply_exponential_fusion.2.refs_1_, ...), custom_call_target="tpu_custom_call" | custom-call | flops 2147483648 | bytes 16646144 | tf_op jit(solution)/shard_map/back_final/pallas_call | solution.py:51
  199.0 1.9 attn_grad.1
  201.6 11.8 %collective-permute-done.59.refs_3_.refs_2_ = bf16[128,1536]{1,0:T(8,128)(2,1)S(1)} collective-permute-done((bf16[128,1536]{1,0:T(8,128)(2,1)S(1)}, bf16[128,1536]{1,0:T(8,128)(2,1)S(1)}, u32[]{:S(2)}, u32[]{:S(2)}) %collective-permute-start.59) | collective-permute-done | bytes 393248 | tf_op jit(solution)/shard_map/ppermute | solution.py:86
  213.4 1.5 collective-permute-start.50
  216.4 8.9 %collective-permute-done.50.refs_1_ = bf16[2,128,768]{2,1,0:T(8,128)(2,1)S(1)} collective-permute-done((bf16[2,128,768]{2,1,0:T(8,128)(2,1)S(1)}, bf16[2,128,768]{2,1,0:T(8,128)(2,1)S(1)}, u32[]{:S(2)}, u32[]{:S(2)}) %collective-permute-start.50) | collective-permute-done | bytes 393248 | tf_op jit(solution)/shard_map/ppermute | solution.py:86
  225.4 1.6 collective-permute-start.53
  227.0 5.3 %collective-permute-done.62.refs_5_ = bf16[128,1280]{1,0:T(8,128)(2,1)S(1)} collective-permute-done((bf16[128,1280]{1,0:T(8,128)(2,1)S(1)}, bf16[128,1280]{1,0:T(8,128)(2,1)S(1)}, u32[]{:S(2)}, u32[]{:S(2)}) %collective-permute-start.62) | collective-permute-done | bytes 327712 | tf_op jit(solution)/shard_map/ppermute | solution.py:86
  233.4 2.2 collective-permute-done.53.refs_5_
  235.6 2.4 collective-permute-done.51.refs_2_
  238.2 3.3 %collective-permute-start.54 = (bf16[128,768]{1,0:T(8,128)(2,1)S(1)}, bf16[128,768]{1,0:T(8,128)(2,1)S(1)}, u32[]{:S(2)}, u32[]{:S(2)}) collective-permute-start(bf16[128,768]{1,0:T(8,128)(2,1)S(1)} %get-tuple-element.195), channel_id=1, source_target_pairs={{0,4},{1,5},{2,6},{3,7},{4,0},{5,1},{6,2},{7,3},{8,12},{9,13},{10,... | collective-permute-start | bytes 589832 | tf_op jit(solution)/shard_map/ppermute | solution.py:86
  242.2 15.6 %collective-permute-done.54.refs_2_ = bf16[128,768]{1,0:T(8,128)(2,1)S(1)} collective-permute-done((bf16[128,768]{1,0:T(8,128)(2,1)S(1)}, bf16[128,768]{1,0:T(8,128)(2,1)S(1)}, u32[]{:S(2)}, u32[]{:S(2)}) %collective-permute-start.54) | collective-permute-done | bytes 196640 | tf_op jit(solution)/shard_map/ppermute | solution.py:86
  257.8 2.9 %collective-permute-start.68 = (bf16[32,1536]{1,0:T(8,128)(2,1)S(1)}, bf16[32,1536]{1,0:T(8,128)(2,1)S(1)}, u32[]{:S(2)}, u32[]{:S(2)}) collective-permute-start(bf16[32,1536]{1,0:T(8,128)(2,1)S(1)} %get-tuple-element.225), channel_id=1, source_target_pairs={{0,2},{1,3},{2,0},{3,1},{4,6},{5,7},{6,4},{7,5},{8,10},{9,11},{10,... | collective-permute-start | bytes 294920 | tf_op jit(solution)/shard_map/ppermute | solution.py:86
  261.6 1.8 collective-permute-done.68.refs_3_
  263.4 2.5 collective-permute-start.65
  266.9 1.8 mixed.1
  268.6 1.5 final_hidden.1
  270.2 2.3 first_back.1
  272.5 1.6 final_rest.1
  (158 shorter events, 34.2 us)
Async XLA Ops:
  4.3 8.8 %collective-permute-start = (bf16[32,3584]{1,0:T(8,128)(2,1)}, bf16[32,3584]{1,0:T(8,128)(2,1)S(1)}, u32[]{:S(2)}, u32[]{:S(2)}) collective-permute-start(bf16[32,3584]{1,0:T(8,128)(2,1)} %get-tuple-element.122), channel_id=1, source_target_pairs={{0,1},{1,0},{2,3},{3,2},{4,5},{5,4},{6,7},{7,6},{8,9},{9,8},{10,11... | collective-permute-start | bytes 688136 | tf_op jit(solution)/shard_map/ppermute | solution.py:86
  4.8 9.3 %collective-permute-start.1 = (bf16[32,3584]{1,0:T(8,128)(2,1)}, bf16[32,3584]{1,0:T(8,128)(2,1)S(1)}, u32[]{:S(2)}, u32[]{:S(2)}) collective-permute-start(bf16[32,3584]{1,0:T(8,128)(2,1)} %get-tuple-element.123), channel_id=1, source_target_pairs={{0,2},{1,3},{2,0},{3,1},{4,6},{5,7},{6,4},{7,5},{8,10},{9,11},{10,... | collective-permute-start | bytes 688136 | tf_op jit(solution)/shard_map/ppermute | solution.py:86
  7.5 11.1 %collective-permute-start.2 = (bf16[32,3584]{1,0:T(8,128)(2,1)}, bf16[32,3584]{1,0:T(8,128)(2,1)S(1)}, u32[]{:S(2)}, u32[]{:S(2)}) collective-permute-start(bf16[32,3584]{1,0:T(8,128)(2,1)} %get-tuple-element.124), channel_id=1, source_target_pairs={{0,3},{1,2},{2,1},{3,0},{4,7},{5,6},{6,5},{7,4},{8,11},{9,10},{10,... | collective-permute-start | bytes 688136 | tf_op jit(solution)/shard_map/ppermute | solution.py:86
  18.7 9.8 %collective-permute-start.7 = (bf16[128,1280]{1,0:T(8,128)(2,1)S(1)}, bf16[128,1280]{1,0:T(8,128)(2,1)S(1)}, u32[]{:S(2)}, u32[]{:S(2)}) collective-permute-start(bf16[128,1280]{1,0:T(8,128)(2,1)S(1)} %maximum_select_fusion.3.refs_1_.refs_6_.refs_15_), channel_id=1, source_target_pairs={{0,8},{1,9},{2,10},{3,11},{4,12},{5,13},{6,14},{7,15},{8,0},{9,1},... | collective-permute-start | bytes 983048 | tf_op jit(solution)/shard_map/ppermute | solution.py:86
  20.2 17.6 %collective-permute-start.6 = (bf16[128,1280]{1,0:T(8,128)(2,1)S(1)}, bf16[128,1280]{1,0:T(8,128)(2,1)S(1)}, u32[]{:S(2)}, u32[]{:S(2)}) collective-permute-start(bf16[128,1280]{1,0:T(8,128)(2,1)S(1)} %maximum_select_fusion.3.refs_1_.refs_6_.refs_15_), channel_id=1, source_target_pairs={{0,4},{1,5},{2,6},{3,7},{4,0},{5,1},{6,2},{7,3},{8,12},{9,13},{10,... | collective-permute-start | bytes 983048 | tf_op jit(solution)/shard_map/ppermute | solution.py:86
  22.8 19.5 %collective-permute-start.4 = (bf16[256,1024]{1,0:T(8,128)(2,1)S(1)}, bf16[256,1024]{1,0:T(8,128)(2,1)S(1)}, u32[]{:S(2)}, u32[]{:S(2)}) collective-permute-start(bf16[256,1024]{1,0:T(8,128)(2,1)S(1)} %tie.8.refs_2_.refs_0_.refs_4_), channel_id=1, source_target_pairs={{0,2},{1,3},{2,0},{3,1},{4,6},{5,7},{6,4},{7,5},{8,10},{9,11},{10,... | collective-permute-start | bytes 1572872 | tf_op jit(solution)/shard_map/ppermute | solution.py:86
  24.4 19.4 %collective-permute-start.3 = (bf16[256,1024]{1,0:T(8,128)(2,1)S(1)}, bf16[256,1024]{1,0:T(8,128)(2,1)S(1)}, u32[]{:S(2)}, u32[]{:S(2)}) collective-permute-start(bf16[256,1024]{1,0:T(8,128)(2,1)S(1)} %tie.8.refs_2_.refs_0_.refs_4_), channel_id=1, source_target_pairs={{0,1},{1,0},{2,3},{3,2},{4,5},{5,4},{6,7},{7,6},{8,9},{9,8},{10,11... | collective-permute-start | bytes 1572872 | tf_op jit(solution)/shard_map/ppermute | solution.py:86
  24.8 14.7 %collective-permute-start.9 = (bf16[128,1280]{1,0:T(8,128)(2,1)S(1)}, bf16[128,1280]{1,0:T(8,128)(2,1)S(1)}, u32[]{:S(2)}, u32[]{:S(2)}) collective-permute-start(bf16[128,1280]{1,0:T(8,128)(2,1)S(1)} %maximum_select_fusion.3.refs_1_.refs_6_.refs_15_), channel_id=1, source_target_pairs={{0,16},{1,17},{2,18},{3,19},{4,20},{5,21},{6,22},{7,23},{8,24},{9,... | collective-permute-start | bytes 983048 | tf_op jit(solution)/shard_map/ppermute | solution.py:86
  28.5 15.9 %collective-permute-start.11 = (bf16[128,1280]{1,0:T(8,128)(2,1)S(1)}, bf16[128,1280]{1,0:T(8,128)(2,1)S(1)}, u32[]{:S(2)}, u32[]{:S(2)}) collective-permute-start(bf16[128,1280]{1,0:T(8,128)(2,1)S(1)} %collective-permute-done.7.refs_1_.refs_8_.refs_17_), channel_id=1, source_target_pairs={{0,16},{1,17},{2,18},{3,19},{4,20},{5,21},{6,22},{7,23},{8,24},{9,... | collective-permute-start | bytes 983048 | tf_op jit(solution)/shard_map/ppermute | solution.py:86
  37.9 11.6 %collective-permute-start.10 = (bf16[128,1280]{1,0:T(8,128)(2,1)S(1)}, bf16[128,1280]{1,0:T(8,128)(2,1)S(1)}, u32[]{:S(2)}, u32[]{:S(2)}) collective-permute-start(bf16[128,1280]{1,0:T(8,128)(2,1)S(1)} %collective-permute-done.6.refs_3_.refs_7_.refs_16_), channel_id=1, source_target_pairs={{0,16},{1,17},{2,18},{3,19},{4,20},{5,21},{6,22},{7,23},{8,24},{9,... | collective-permute-start | bytes 983048 | tf_op jit(solution)/shard_map/ppermute | solution.py:86
  39.6 10.7 %collective-permute-start.8 = (bf16[128,1280]{1,0:T(8,128)(2,1)S(1)}, bf16[128,1280]{1,0:T(8,128)(2,1)S(1)}, u32[]{:S(2)}, u32[]{:S(2)}) collective-permute-start(bf16[128,1280]{1,0:T(8,128)(2,1)S(1)} %collective-permute-done.6.refs_3_.refs_7_.refs_16_), channel_id=1, source_target_pairs={{0,8},{1,9},{2,10},{3,11},{4,12},{5,13},{6,14},{7,15},{8,0},{9,1},... | collective-permute-start | bytes 983048 | tf_op jit(solution)/shard_map/ppermute | solution.py:86
  42.3 25.4 %collective-permute-start.15 = (bf16[128,2304]{1,0:T(8,128)(2,1)S(1)}, bf16[128,2304]{1,0:T(8,128)(2,1)S(1)}, u32[]{:S(2)}, u32[]{:S(2)}) collective-permute-start(bf16[128,2304]{1,0:T(8,128)(2,1)S(1)} %tie.9.refs_4_), channel_id=1, source_target_pairs={{0,16},{1,17},{2,18},{3,19},{4,20},{5,21},{6,22},{7,23},{8,24},{9,... | collective-permute-start | bytes 1769480 | tf_op jit(solution)/shard_map/ppermute | solution.py:86
  43.8 23.9 %collective-permute-start.14 = (bf16[128,2304]{1,0:T(8,128)(2,1)S(1)}, bf16[128,2304]{1,0:T(8,128)(2,1)S(1)}, u32[]{:S(2)}, u32[]{:S(2)}) collective-permute-start(bf16[128,2304]{1,0:T(8,128)(2,1)S(1)} %tie.9.refs_4_), channel_id=1, source_target_pairs={{0,8},{1,9},{2,10},{3,11},{4,12},{5,13},{6,14},{7,15},{8,0},{9,1},... | collective-permute-start | bytes 1769480 | tf_op jit(solution)/shard_map/ppermute | solution.py:86
  44.3 27.0 %collective-permute-start.13 = (bf16[128,2304]{1,0:T(8,128)(2,1)S(1)}, bf16[128,2304]{1,0:T(8,128)(2,1)S(1)}, u32[]{:S(2)}, u32[]{:S(2)}) collective-permute-start(bf16[128,2304]{1,0:T(8,128)(2,1)S(1)} %tie.9.refs_4_), channel_id=1, source_target_pairs={{0,4},{1,5},{2,6},{3,7},{4,0},{5,1},{6,2},{7,3},{8,12},{9,13},{10,... | collective-permute-start | bytes 1769480 | tf_op jit(solution)/shard_map/ppermute | solution.py:86
  49.4 18.3 %collective-permute-start.5 = (bf16[256,1024]{1,0:T(8,128)(2,1)S(1)}, bf16[256,1024]{1,0:T(8,128)(2,1)S(1)}, u32[]{:S(2)}, u32[]{:S(2)}) collective-permute-start(bf16[256,1024]{1,0:T(8,128)(2,1)S(1)} %collective-permute-done.4.refs_4_.refs_2_.refs_6_), channel_id=1, source_target_pairs={{0,1},{1,0},{2,3},{3,2},{4,5},{5,4},{6,7},{7,6},{8,9},{9,8},{10,11... | collective-permute-start | bytes 1572872 | tf_op jit(solution)/shard_map/ppermute | solution.py:86
  50.3 17.4 %collective-permute-start.12 = (bf16[128,1280]{1,0:T(8,128)(2,1)S(1)}, bf16[128,1280]{1,0:T(8,128)(2,1)S(1)}, u32[]{:S(2)}, u32[]{:S(2)}) collective-permute-start(bf16[128,1280]{1,0:T(8,128)(2,1)S(1)} %collective-permute-done.10.refs_11_.refs_20_), channel_id=1, source_target_pairs={{0,8},{1,9},{2,10},{3,11},{4,12},{5,13},{6,14},{7,15},{8,0},{9,1},... | collective-permute-start | bytes 983048 | tf_op jit(solution)/shard_map/ppermute | solution.py:86
  75.5 14.9 %collective-permute-start.21 = (bf16[1024,256]{1,0:T(8,128)(2,1)S(1)}, bf16[1024,256]{1,0:T(8,128)(2,1)S(1)}, u32[]{:S(2)}, u32[]{:S(2)}) collective-permute-start(bf16[1024,256]{1,0:T(8,128)(2,1)S(1)} %get-tuple-element.133.refs_6_), channel_id=1, source_target_pairs={{0,2},{1,3},{2,0},{3,1},{4,6},{5,7},{6,4},{7,5},{8,10},{9,11},{10,... | collective-permute-start | bytes 1572872 | tf_op jit(solution)/shard_map/ppermute | solution.py:86
  75.6 13.8 %collective-permute-start.17 = (bf16[1024,256]{1,0:T(8,128)(2,1)S(1)}, bf16[1024,256]{1,0:T(8,128)(2,1)S(1)}, u32[]{:S(2)}, u32[]{:S(2)}) collective-permute-start(bf16[1024,256]{1,0:T(8,128)(2,1)S(1)} %get-tuple-element.133.refs_6_), channel_id=1, source_target_pairs={{0,1},{1,0},{2,3},{3,2},{4,5},{5,4},{6,7},{7,6},{8,9},{9,8},{10,11... | collective-permute-start | bytes 1572872 | tf_op jit(solution)/shard_map/ppermute | solution.py:86
  75.9 15.8 %collective-permute-start.24 = (bf16[128,2304]{1,0:T(8,128)(2,1)S(1)}, bf16[128,2304]{1,0:T(8,128)(2,1)S(1)}, u32[]{:S(2)}, u32[]{:S(2)}) collective-permute-start(bf16[128,2304]{1,0:T(8,128)(2,1)S(1)} %tie.11.refs_5_), channel_id=1, source_target_pairs={{0,8},{1,9},{2,10},{3,11},{4,12},{5,13},{6,14},{7,15},{8,0},{9,1},... | collective-permute-start | bytes 1769480 | tf_op jit(solution)/shard_map/ppermute | solution.py:86
  77.5 15.5 %collective-permute-start.23 = (bf16[128,2304]{1,0:T(8,128)(2,1)S(1)}, bf16[128,2304]{1,0:T(8,128)(2,1)S(1)}, u32[]{:S(2)}, u32[]{:S(2)}) collective-permute-start(bf16[128,2304]{1,0:T(8,128)(2,1)S(1)} %tie.11.refs_5_), channel_id=1, source_target_pairs={{0,16},{1,17},{2,18},{3,19},{4,20},{5,21},{6,22},{7,23},{8,24},{9,... | collective-permute-start | bytes 1769480 | tf_op jit(solution)/shard_map/ppermute | solution.py:86
  78.0 11.4 %collective-permute-start.16 = (f32[2,128,128]{2,1,0:T(8,128)S(1)}, f32[2,128,128]{2,1,0:T(8,128)S(1)}, u32[]{:S(2)}, u32[]{:S(2)}) collective-permute-start(f32[2,128,128]{2,1,0:T(8,128)S(1)} %get-tuple-element.126), channel_id=1, source_target_pairs={{0,4},{1,5},{2,6},{3,7},{8,12},{9,13},{10,14},{11,15},{16,20},{17,... | collective-permute-start | bytes 393224 | tf_op jit(solution)/shard_map/ppermute | solution.py:100
  90.5 8.0 %collective-permute-start.22 = (bf16[1024,256]{1,0:T(8,128)(2,1)S(1)}, bf16[1024,256]{1,0:T(8,128)(2,1)S(1)}, u32[]{:S(2)}, u32[]{:S(2)}) collective-permute-start(bf16[1024,256]{1,0:T(8,128)(2,1)S(1)} %tie.10.refs_8_), channel_id=1, source_target_pairs={{0,1},{1,0},{2,3},{3,2},{4,5},{5,4},{6,7},{7,6},{8,9},{9,8},{10,11... | collective-permute-start | bytes 1572872 | tf_op jit(solution)/shard_map/ppermute | solution.py:86
  91.0 6.4 %collective-permute-start.19 = (bf16[256,256]{1,0:T(8,128)(2,1)S(1)}, bf16[256,256]{1,0:T(8,128)(2,1)S(1)}, u32[]{:S(2)}, u32[]{:S(2)}) collective-permute-start(bf16[256,256]{1,0:T(8,128)(2,1)S(1)} %get-tuple-element.136), channel_id=1, source_target_pairs={{0,2},{1,3},{2,0},{3,1},{4,6},{5,7},{6,4},{7,5},{8,10},{9,11},{10,... | collective-permute-start | bytes 393224 | tf_op jit(solution)/shard_map/ppermute | solution.py:86
  91.7 6.7 %collective-permute-start.20 = (bf16[256,256]{1,0:T(8,128)(2,1)S(1)}, bf16[256,256]{1,0:T(8,128)(2,1)S(1)}, u32[]{:S(2)}, u32[]{:S(2)}) collective-permute-start(bf16[256,256]{1,0:T(8,128)(2,1)S(1)} %get-tuple-element.137), channel_id=1, source_target_pairs={{0,3},{1,2},{2,1},{3,0},{4,7},{5,6},{6,5},{7,4},{8,11},{9,10},{10,... | collective-permute-start | bytes 393224 | tf_op jit(solution)/shard_map/ppermute | solution.py:86
  93.0 18.5 %collective-permute-start.31 = (bf16[256,1024]{1,0:T(8,128)(2,1)S(1)}, bf16[256,1024]{1,0:T(8,128)(2,1)S(1)}, u32[]{:S(2)}, u32[]{:S(2)}) collective-permute-start(bf16[256,1024]{1,0:T(8,128)(2,1)S(1)} %tie.12.refs_2_.refs_0_), channel_id=1, source_target_pairs={{0,2},{1,3},{2,0},{3,1},{4,6},{5,7},{6,4},{7,5},{8,10},{9,11},{10,... | collective-permute-start | bytes 1572872 | tf_op jit(solution)/shard_map/ppermute | solution.py:86
  100.2 21.6 %collective-permute-start.29 = (bf16[256,1024]{1,0:T(8,128)(2,1)S(1)}, bf16[256,1024]{1,0:T(8,128)(2,1)S(1)}, u32[]{:S(2)}, u32[]{:S(2)}) collective-permute-start(bf16[256,1024]{1,0:T(8,128)(2,1)S(1)} %get-tuple-element.140.refs_0_), channel_id=1, source_target_pairs={{0,2},{1,3},{2,0},{3,1},{4,6},{5,7},{6,4},{7,5},{8,10},{9,11},{10,... | collective-permute-start | bytes 1572872 | tf_op jit(solution)/shard_map/ppermute | solution.py:86
  101.6 20.2 %collective-permute-start.27 = (bf16[128,2304]{1,0:T(8,128)(2,1)S(1)}, bf16[128,2304]{1,0:T(8,128)(2,1)S(1)}, u32[]{:S(2)}, u32[]{:S(2)}) collective-permute-start(bf16[128,2304]{1,0:T(8,128)(2,1)S(1)} %tie.13.refs_6_), channel_id=1, source_target_pairs={{0,16},{1,17},{2,18},{3,19},{4,20},{5,21},{6,22},{7,23},{8,24},{9,... | collective-permute-start | bytes 1769480 | tf_op jit(solution)/shard_map/ppermute | solution.py:86
  102.2 19.6 %collective-permute-start.28 = (bf16[128,2304]{1,0:T(8,128)(2,1)S(1)}, bf16[128,2304]{1,0:T(8,128)(2,1)S(1)}, u32[]{:S(2)}, u32[]{:S(2)}) collective-permute-start(bf16[128,2304]{1,0:T(8,128)(2,1)S(1)} %tie.14.refs_9_), channel_id=1, source_target_pairs={{0,8},{1,9},{2,10},{3,11},{4,12},{5,13},{6,14},{7,15},{8,0},{9,1},... | collective-permute-start | bytes 1769480 | tf_op jit(solution)/shard_map/ppermute | solution.py:86
  111.5 10.4 %collective-permute-start.32 = (bf16[256,1024]{1,0:T(8,128)(2,1)S(1)}, bf16[256,1024]{1,0:T(8,128)(2,1)S(1)}, u32[]{:S(2)}, u32[]{:S(2)}) collective-permute-start(bf16[256,1024]{1,0:T(8,128)(2,1)S(1)} %tie.15.refs_2_), channel_id=1, source_target_pairs={{0,1},{1,0},{2,3},{3,2},{4,5},{5,4},{6,7},{7,6},{8,9},{9,8},{10,11... | collective-permute-start | bytes 1572872 | tf_op jit(solution)/shard_map/ppermute | solution.py:86
  130.9 24.3 %collective-permute-start.38 = (bf16[256,1024]{1,0:T(8,128)(2,1)S(1)}, bf16[256,1024]{1,0:T(8,128)(2,1)S(1)}, u32[]{:S(2)}, u32[]{:S(2)}) collective-permute-start(bf16[256,1024]{1,0:T(8,128)(2,1)S(1)} %add.92.refs_12_), channel_id=1, source_target_pairs={{0,2},{1,3},{2,0},{3,1},{4,6},{5,7},{6,4},{7,5},{8,10},{9,11},{10,... | collective-permute-start | bytes 1572872 | tf_op jit(solution)/shard_map/ppermute | solution.py:86
  137.4 17.8 %collective-permute-start.37 = (bf16[256,1024]{1,0:T(8,128)(2,1)S(1)}, bf16[256,1024]{1,0:T(8,128)(2,1)S(1)}, u32[]{:S(2)}, u32[]{:S(2)}) collective-permute-start(bf16[256,1024]{1,0:T(8,128)(2,1)S(1)} %get-tuple-element.153), channel_id=1, source_target_pairs={{0,1},{1,0},{2,3},{3,2},{4,5},{5,4},{6,7},{7,6},{8,9},{9,8},{10,11... | collective-permute-start | bytes 1572872 | tf_op jit(solution)/shard_map/ppermute | solution.py:86
  158.8 12.6 %collective-permute-start.56 = (bf16[1024,256]{1,0:T(8,128)(2,1)S(1)}, bf16[1024,256]{1,0:T(8,128)(2,1)S(1)}, u32[]{:S(2)}, u32[]{:S(2)}) collective-permute-start(bf16[1024,256]{1,0:T(8,128)(2,1)S(1)} %get-tuple-element.201), channel_id=1, source_target_pairs={{0,1},{1,0},{2,3},{3,2},{4,5},{5,4},{6,7},{7,6},{8,9},{9,8},{10,11... | collective-permute-start | bytes 1572872 | tf_op jit(solution)/shard_map/ppermute | solution.py:86
  159.3 19.6 %collective-permute-start.45 = (bf16[2,128,1536]{2,1,0:T(8,128)(2,1)S(1)}, bf16[2,128,1536]{2,1,0:T(8,128)(2,1)S(1)}, u32[]{:S(2)}, u32[]{:S(2)}) collective-permute-start(bf16[2,128,1536]{2,1,0:T(8,128)(2,1)S(1)} %get-tuple-element.182), channel_id=1, source_target_pairs={{0,16},{1,17},{2,18},{3,19},{4,20},{5,21},{6,22},{7,23},{8,24},{9,... | collective-permute-start | bytes 2359304 | tf_op jit(solution)/shard_map/ppermute | solution.py:86
  159.9 20.6 %collective-permute-start.43 = (bf16[2,128,1536]{2,1,0:T(8,128)(2,1)S(1)}, bf16[2,128,1536]{2,1,0:T(8,128)(2,1)S(1)}, u32[]{:S(2)}, u32[]{:S(2)}) collective-permute-start(bf16[2,128,1536]{2,1,0:T(8,128)(2,1)S(1)} %get-tuple-element.162.refs_10_), channel_id=1, source_target_pairs={{0,8},{1,9},{2,10},{3,11},{4,12},{5,13},{6,14},{7,15},{8,0},{9,1},... | collective-permute-start | bytes 2359304 | tf_op jit(solution)/shard_map/ppermute | solution.py:86
  161.3 6.3 %collective-permute-start.40 = (bf16[256,256]{1,0:T(8,128)(2,1)S(1)}, bf16[256,256]{1,0:T(8,128)(2,1)S(1)}, u32[]{:S(2)}, u32[]{:S(2)}) collective-permute-start(bf16[256,256]{1,0:T(8,128)(2,1)S(1)} %get-tuple-element.165), channel_id=1, source_target_pairs={{0,2},{1,3},{2,0},{3,1},{4,6},{5,7},{6,4},{7,5},{8,10},{9,11},{10,... | collective-permute-start | bytes 393224 | tf_op jit(solution)/shard_map/ppermute | solution.py:86
  162.6 7.0 %collective-permute-start.41 = (bf16[256,256]{1,0:T(8,128)(2,1)S(1)}, bf16[256,256]{1,0:T(8,128)(2,1)S(1)}, u32[]{:S(2)}, u32[]{:S(2)}) collective-permute-start(bf16[256,256]{1,0:T(8,128)(2,1)S(1)} %get-tuple-element.166), channel_id=1, source_target_pairs={{0,3},{1,2},{2,1},{3,0},{4,7},{5,6},{6,5},{7,4},{8,11},{9,10},{10,... | collective-permute-start | bytes 393224 | tf_op jit(solution)/shard_map/ppermute | solution.py:86
  167.6 17.4 %collective-permute-start.55 = (bf16[1024,256]{1,0:T(8,128)(2,1)S(1)}, bf16[1024,256]{1,0:T(8,128)(2,1)S(1)}, u32[]{:S(2)}, u32[]{:S(2)}) collective-permute-start(bf16[1024,256]{1,0:T(8,128)(2,1)S(1)} %get-tuple-element.199), channel_id=1, source_target_pairs={{0,1},{1,0},{2,3},{3,2},{4,5},{5,4},{6,7},{7,6},{8,9},{9,8},{10,11... | collective-permute-start | bytes 1572872 | tf_op jit(solution)/shard_map/ppermute | solution.py:86
  171.6 15.8 %collective-permute-start.57 = (bf16[1024,256]{1,0:T(8,128)(2,1)S(1)}, bf16[1024,256]{1,0:T(8,128)(2,1)S(1)}, u32[]{:S(2)}, u32[]{:S(2)}) collective-permute-start(bf16[1024,256]{1,0:T(8,128)(2,1)S(1)} %add.95), channel_id=1, source_target_pairs={{0,2},{1,3},{2,0},{3,1},{4,6},{5,7},{6,4},{7,5},{8,10},{9,11},{10,... | collective-permute-start | bytes 1572872 | tf_op jit(solution)/shard_map/ppermute | solution.py:86
  179.0 13.2 %collective-permute-start.46 = (bf16[128,1536]{1,0:T(8,128)(2,1)S(1)}, bf16[128,1536]{1,0:T(8,128)(2,1)S(1)}, u32[]{:S(2)}, u32[]{:S(2)}) collective-permute-start(bf16[128,1536]{1,0:T(8,128)(2,1)S(1)} %next.7), channel_id=1, source_target_pairs={{0,8},{1,9},{2,10},{3,11},{4,12},{5,13},{6,14},{7,15},{8,0},{9,1},... | collective-permute-start | bytes 1179656 | tf_op jit(solution)/shard_map/ppermute | solution.py:86
  180.6 11.5 %collective-permute-start.44 = (bf16[128,1536]{1,0:T(8,128)(2,1)S(1)}, bf16[128,1536]{1,0:T(8,128)(2,1)S(1)}, u32[]{:S(2)}, u32[]{:S(2)}) collective-permute-start(bf16[128,1536]{1,0:T(8,128)(2,1)S(1)} %next.6), channel_id=1, source_target_pairs={{0,16},{1,17},{2,18},{3,19},{4,20},{5,21},{6,22},{7,23},{8,24},{9,... | collective-permute-start | bytes 1179656 | tf_op jit(solution)/shard_map/ppermute | solution.py:86
  181.2 13.7 %collective-permute-start.42 = (f32[2,128,128]{2,1,0:T(8,128)S(1)}, f32[2,128,128]{2,1,0:T(8,128)S(1)}, u32[]{:S(2)}, u32[]{:S(2)}) collective-permute-start(f32[2,128,128]{2,1,0:T(8,128)S(1)} %get-tuple-element.168), channel_id=1, source_target_pairs={{4,0},{5,1},{6,2},{7,3},{12,8},{13,9},{14,10},{15,11},{20,16},{21,... | collective-permute-start | bytes 393224 | tf_op jit(solution)/shard_map/ppermute | solution.py:100
  190.0 24.8 %collective-permute-start.58 = (bf16[2,128,1280]{2,1,0:T(8,128)(2,1)S(1)}, bf16[2,128,1280]{2,1,0:T(8,128)(2,1)S(1)}, u32[]{:S(2)}, u32[]{:S(2)}) collective-permute-start(bf16[2,128,1280]{2,1,0:T(8,128)(2,1)S(1)} %get-tuple-element.203), channel_id=1, source_target_pairs={{0,8},{1,9},{2,10},{3,11},{4,12},{5,13},{6,14},{7,15},{8,0},{9,1},... | collective-permute-start | bytes 1966088 | tf_op jit(solution)/shard_map/ppermute | solution.py:86
  190.7 24.2 %collective-permute-start.61 = (bf16[2,128,1280]{2,1,0:T(8,128)(2,1)S(1)}, bf16[2,128,1280]{2,1,0:T(8,128)(2,1)S(1)}, u32[]{:S(2)}, u32[]{:S(2)}) collective-permute-start(bf16[2,128,1280]{2,1,0:T(8,128)(2,1)S(1)} %get-tuple-element.209), channel_id=1, source_target_pairs={{0,16},{1,17},{2,18},{3,19},{4,20},{5,21},{6,22},{7,23},{8,24},{9,... | collective-permute-start | bytes 1966088 | tf_op jit(solution)/shard_map/ppermute | solution.py:86
  192.2 23.4 %collective-permute-start.35 = (bf16[256,1024]{1,0:T(8,128)(2,1)S(1)}, bf16[256,1024]{1,0:T(8,128)(2,1)S(1)}, u32[]{:S(2)}, u32[]{:S(2)}) collective-permute-start(bf16[256,1024]{1,0:T(8,128)(2,1)S(1)} %get-tuple-element.151), channel_id=1, source_target_pairs={{0,1},{1,0},{2,3},{3,2},{4,5},{5,4},{6,7},{7,6},{8,9},{9,8},{10,11... | collective-permute-start | bytes 1572872 | tf_op jit(solution)/shard_map/ppermute | solution.py:86
  192.4 20.9 %collective-permute-start.59 = (bf16[128,1536]{1,0:T(8,128)(2,1)S(1)}, bf16[128,1536]{1,0:T(8,128)(2,1)S(1)}, u32[]{:S(2)}, u32[]{:S(2)}) collective-permute-start(bf16[128,1536]{1,0:T(8,128)(2,1)S(1)} %get-tuple-element.207), channel_id=1, source_target_pairs={{0,4},{1,5},{2,6},{3,7},{4,0},{5,1},{6,2},{7,3},{8,12},{9,13},{10,... | collective-permute-start | bytes 1179656 | tf_op jit(solution)/shard_map/ppermute | solution.py:86
  200.9 15.4 %collective-permute-start.52 = (bf16[2,128,768]{2,1,0:T(8,128)(2,1)S(1)}, bf16[2,128,768]{2,1,0:T(8,128)(2,1)S(1)}, u32[]{:S(2)}, u32[]{:S(2)}) collective-permute-start(bf16[2,128,768]{2,1,0:T(8,128)(2,1)S(1)} %get-tuple-element.192), channel_id=1, source_target_pairs={{0,16},{1,17},{2,18},{3,19},{4,20},{5,21},{6,22},{7,23},{8,24},{9,... | collective-permute-start | bytes 1179656 | tf_op jit(solution)/shard_map/ppermute | solution.py:86
  213.4 12.0 %collective-permute-start.50 = (bf16[2,128,768]{2,1,0:T(8,128)(2,1)S(1)}, bf16[2,128,768]{2,1,0:T(8,128)(2,1)S(1)}, u32[]{:S(2)}, u32[]{:S(2)}) collective-permute-start(bf16[2,128,768]{2,1,0:T(8,128)(2,1)S(1)} %get-tuple-element.183.refs_5_.refs_2_), channel_id=1, source_target_pairs={{0,8},{1,9},{2,10},{3,11},{4,12},{5,13},{6,14},{7,15},{8,0},{9,1},... | collective-permute-start | bytes 1179656 | tf_op jit(solution)/shard_map/ppermute | solution.py:86
  214.9 18.3 %collective-permute-start.48 = (bf16[256,1024]{1,0:T(8,128)(2,1)S(1)}, bf16[256,1024]{1,0:T(8,128)(2,1)S(1)}, u32[]{:S(2)}, u32[]{:S(2)}) collective-permute-start(bf16[256,1024]{1,0:T(8,128)(2,1)S(1)} %get-tuple-element.188), channel_id=1, source_target_pairs={{0,1},{1,0},{2,3},{3,2},{4,5},{5,4},{6,7},{7,6},{8,9},{9,8},{10,11... | collective-permute-start | bytes 1572872 | tf_op jit(solution)/shard_map/ppermute | solution.py:86
  214.9 10.4 %collective-permute-start.60 = (bf16[128,1280]{1,0:T(8,128)(2,1)S(1)}, bf16[128,1280]{1,0:T(8,128)(2,1)S(1)}, u32[]{:S(2)}, u32[]{:S(2)}) collective-permute-start(bf16[128,1280]{1,0:T(8,128)(2,1)S(1)} %next.10), channel_id=1, source_target_pairs={{0,16},{1,17},{2,18},{3,19},{4,20},{5,21},{6,22},{7,23},{8,24},{9,... | collective-permute-start | bytes 983048 | tf_op jit(solution)/shard_map/ppermute | solution.py:86
  215.6 16.7 %collective-permute-start.62 = (bf16[128,1280]{1,0:T(8,128)(2,1)S(1)}, bf16[128,1280]{1,0:T(8,128)(2,1)S(1)}, u32[]{:S(2)}, u32[]{:S(2)}) collective-permute-start(bf16[128,1280]{1,0:T(8,128)(2,1)S(1)} %next.11), channel_id=1, source_target_pairs={{0,8},{1,9},{2,10},{3,11},{4,12},{5,13},{6,14},{7,15},{8,0},{9,1},... | collective-permute-start | bytes 983048 | tf_op jit(solution)/shard_map/ppermute | solution.py:86
  216.3 21.9 %collective-permute-start.34 = (bf16[256,1024]{1,0:T(8,128)(2,1)S(1)}, bf16[256,1024]{1,0:T(8,128)(2,1)S(1)}, u32[]{:S(2)}, u32[]{:S(2)}) collective-permute-start(bf16[256,1024]{1,0:T(8,128)(2,1)S(1)} %get-tuple-element.149), channel_id=1, source_target_pairs={{0,1},{1,0},{2,3},{3,2},{4,5},{5,4},{6,7},{7,6},{8,9},{9,8},{10,11... | collective-permute-start | bytes 1572872 | tf_op jit(solution)/shard_map/ppermute | solution.py:86
  225.3 16.8 %collective-permute-start.36 = (bf16[256,1024]{1,0:T(8,128)(2,1)S(1)}, bf16[256,1024]{1,0:T(8,128)(2,1)S(1)}, u32[]{:S(2)}, u32[]{:S(2)}) collective-permute-start(bf16[256,1024]{1,0:T(8,128)(2,1)S(1)} %add.93), channel_id=1, source_target_pairs={{0,2},{1,3},{2,0},{3,1},{4,6},{5,7},{6,4},{7,5},{8,10},{9,11},{10,... | collective-permute-start | bytes 1572872 | tf_op jit(solution)/shard_map/ppermute | solution.py:86
  225.4 10.2 %collective-permute-start.53 = (bf16[128,768]{1,0:T(8,128)(2,1)S(1)}, bf16[128,768]{1,0:T(8,128)(2,1)S(1)}, u32[]{:S(2)}, u32[]{:S(2)}) collective-permute-start(bf16[128,768]{1,0:T(8,128)(2,1)S(1)} %next.9), channel_id=1, source_target_pairs={{0,8},{1,9},{2,10},{3,11},{4,12},{5,13},{6,14},{7,15},{8,0},{9,1},... | collective-permute-start | bytes 589832 | tf_op jit(solution)/shard_map/ppermute | solution.py:86
  232.4 5.7 %collective-permute-start.51 = (bf16[128,768]{1,0:T(8,128)(2,1)S(1)}, bf16[128,768]{1,0:T(8,128)(2,1)S(1)}, u32[]{:S(2)}, u32[]{:S(2)}) collective-permute-start(bf16[128,768]{1,0:T(8,128)(2,1)S(1)} %next.8), channel_id=1, source_target_pairs={{0,16},{1,17},{2,18},{3,19},{4,20},{5,21},{6,22},{7,23},{8,24},{9,... | collective-permute-start | bytes 589832 | tf_op jit(solution)/shard_map/ppermute | solution.py:86
  233.2 27.5 %collective-permute-start.63 = (bf16[128,1280]{1,0:T(8,128)(2,1)S(1)}, bf16[128,1280]{1,0:T(8,128)(2,1)S(1)}, u32[]{:S(2)}, u32[]{:S(2)}) collective-permute-start(bf16[128,1280]{1,0:T(8,128)(2,1)S(1)} %get-tuple-element.212), channel_id=1, source_target_pairs={{0,4},{1,5},{2,6},{3,7},{4,0},{5,1},{6,2},{7,3},{8,12},{9,13},{10,... | collective-permute-start | bytes 983048 | tf_op jit(solution)/shard_map/ppermute | solution.py:86
  235.6 34.6 %collective-permute-start.47 = (bf16[256,1024]{1,0:T(8,128)(2,1)S(1)}, bf16[256,1024]{1,0:T(8,128)(2,1)S(1)}, u32[]{:S(2)}, u32[]{:S(2)}) collective-permute-start(bf16[256,1024]{1,0:T(8,128)(2,1)S(1)} %get-tuple-element.186), channel_id=1, source_target_pairs={{0,1},{1,0},{2,3},{3,2},{4,5},{5,4},{6,7},{7,6},{8,9},{9,8},{10,11... | collective-permute-start | bytes 1572872 | tf_op jit(solution)/shard_map/ppermute | solution.py:86
  238.0 32.1 %collective-permute-start.49 = (bf16[256,1024]{1,0:T(8,128)(2,1)S(1)}, bf16[256,1024]{1,0:T(8,128)(2,1)S(1)}, u32[]{:S(2)}, u32[]{:S(2)}) collective-permute-start(bf16[256,1024]{1,0:T(8,128)(2,1)S(1)} %add.94), channel_id=1, source_target_pairs={{0,2},{1,3},{2,0},{3,1},{4,6},{5,7},{6,4},{7,5},{8,10},{9,11},{10,... | collective-permute-start | bytes 1572872 | tf_op jit(solution)/shard_map/ppermute | solution.py:86
  238.2 19.6 %collective-permute-start.54 = (bf16[128,768]{1,0:T(8,128)(2,1)S(1)}, bf16[128,768]{1,0:T(8,128)(2,1)S(1)}, u32[]{:S(2)}, u32[]{:S(2)}) collective-permute-start(bf16[128,768]{1,0:T(8,128)(2,1)S(1)} %get-tuple-element.195), channel_id=1, source_target_pairs={{0,4},{1,5},{2,6},{3,7},{4,0},{5,1},{6,2},{7,3},{8,12},{9,13},{10,... | collective-permute-start | bytes 589832 | tf_op jit(solution)/shard_map/ppermute | solution.py:86
  242.1 19.2 %collective-permute-start.67 = (bf16[32,1536]{1,0:T(8,128)(2,1)S(1)}, bf16[32,1536]{1,0:T(8,128)(2,1)S(1)}, u32[]{:S(2)}, u32[]{:S(2)}) collective-permute-start(bf16[32,1536]{1,0:T(8,128)(2,1)S(1)} %get-tuple-element.224), channel_id=1, source_target_pairs={{0,1},{1,0},{2,3},{3,2},{4,5},{5,4},{6,7},{7,6},{8,9},{9,8},{10,11... | collective-permute-start | bytes 294920 | tf_op jit(solution)/shard_map/ppermute | solution.py:86
  257.8 5.6 %collective-permute-start.68 = (bf16[32,1536]{1,0:T(8,128)(2,1)S(1)}, bf16[32,1536]{1,0:T(8,128)(2,1)S(1)}, u32[]{:S(2)}, u32[]{:S(2)}) collective-permute-start(bf16[32,1536]{1,0:T(8,128)(2,1)S(1)} %get-tuple-element.225), channel_id=1, source_target_pairs={{0,2},{1,3},{2,0},{3,1},{4,6},{5,7},{6,4},{7,5},{8,10},{9,11},{10,... | collective-permute-start | bytes 294920 | tf_op jit(solution)/shard_map/ppermute | solution.py:86
  260.7 5.1 %collective-permute-start.69 = (bf16[32,1536]{1,0:T(8,128)(2,1)S(1)}, bf16[32,1536]{1,0:T(8,128)(2,1)S(1)}, u32[]{:S(2)}, u32[]{:S(2)}) collective-permute-start(bf16[32,1536]{1,0:T(8,128)(2,1)S(1)} %get-tuple-element.226), channel_id=1, source_target_pairs={{0,3},{1,2},{2,1},{3,0},{4,7},{5,6},{6,5},{7,4},{8,11},{9,10},{10,... | collective-permute-start | bytes 294920 | tf_op jit(solution)/shard_map/ppermute | solution.py:86
  261.4 11.1 %collective-permute-start.64 = (bf16[32,2048]{1,0:T(8,128)(2,1)S(1)}, bf16[32,2048]{1,0:T(8,128)(2,1)S(1)}, u32[]{:S(2)}, u32[]{:S(2)}) collective-permute-start(bf16[32,2048]{1,0:T(8,128)(2,1)S(1)} %get-tuple-element.214), channel_id=1, source_target_pairs={{0,1},{1,0},{2,3},{3,2},{4,5},{5,4},{6,7},{7,6},{8,9},{9,8},{10,11... | collective-permute-start | bytes 393224 | tf_op jit(solution)/shard_map/ppermute | solution.py:86
  263.4 9.1 %collective-permute-start.65 = (bf16[32,2048]{1,0:T(8,128)(2,1)S(1)}, bf16[32,2048]{1,0:T(8,128)(2,1)S(1)}, u32[]{:S(2)}, u32[]{:S(2)}) collective-permute-start(bf16[32,2048]{1,0:T(8,128)(2,1)S(1)} %get-tuple-element.215), channel_id=1, source_target_pairs={{0,2},{1,3},{2,0},{3,1},{4,6},{5,7},{6,4},{7,5},{8,10},{9,11},{10,... | collective-permute-start | bytes 393224 | tf_op jit(solution)/shard_map/ppermute | solution.py:86
  265.8 6.6 %collective-permute-start.66 = (bf16[32,2048]{1,0:T(8,128)(2,1)S(1)}, bf16[32,2048]{1,0:T(8,128)(2,1)S(1)}, u32[]{:S(2)}, u32[]{:S(2)}) collective-permute-start(bf16[32,2048]{1,0:T(8,128)(2,1)S(1)} %get-tuple-element.216), channel_id=1, source_target_pairs={{0,3},{1,2},{2,1},{3,0},{4,7},{5,6},{6,5},{7,4},{8,11},{9,10},{10,... | collective-permute-start | bytes 393224 | tf_op jit(solution)/shard_map/ppermute | solution.py:86
  (11 other events, 76.2 us)
where the time goes:
time: 276 us; the launch traced here: 274 us
  waiting for transfers between devices  136 us (49%)
  Pallas kernels  67.9 us (25%)
  starting transfers between devices  62 us (22%)
  other arithmetic  4.01 us (1%)
    ppermute x68, waiting for transfers between devices, swap(): return lax.ppermute(v, AXES, [(d, d ^ mask) for d in range(self.count)])  131 us
    pallas_call x35, Pallas kernels, run(): pl.pallas_call(body, out_shape=list(outs), in_specs=[pl.BlockSpec(memory_...  64.8 us
    ppermute x68, starting transfers between devices, swap(): return lax.ppermute(v, AXES, [(d, d ^ mask) for d in range(self.count)])  55.6 us
    ppermute x2, starting transfers between devices, group_shift(): return lax.ppermute(v, AXES, pairs)  6.39 us
  transfers between devices with their start and end apart: 70, of which 31 were waited for; matrix products, arithmetic and copies ran while one was open for 2% of the time, Pallas kernels for 18%

commit v1 on v0

--- a/solution.py
+++ b/solution.py
@@ -14,6 +14,7 @@
 bf16 = jnp.bfloat16
 MIB = 1024 * 1024
 VM = (12, 16, 16, 16)
+WEIGHT = {}
 
 
 def mm(a, b):
@@ -40,7 +41,7 @@
     return jax.ShapeDtypeStruct(tuple(shape), dtype)
 
 
-def run(name, kernel, outs, scalars, arrays, scratch=(), flops=0, vmem=10, after=()):
+def run(name, kernel, outs, scalars, arrays, scratch=(), flops=0, vmem=10, after=(), alias=None):
     ins = list(scalars) + list(arrays) + list(after)
     used, held = len(scalars) + len(arrays), len(after)
 
@@ -48,6 +49,7 @@
         kernel(*refs[:used], *refs[used + held :])
 
     size = sum(v.size * v.dtype.itemsize for v in list(arrays) + list(outs)) if flops else 0
+    size, flops = (int(v * WEIGHT.get(name, 1)) for v in (size, flops))
     return pl.pallas_call(
         body,
         out_shape=list(outs),
@@ -56,6 +58,7 @@
         + [pl.BlockSpec(memory_space=pl.ANY)] * held,
         out_specs=[pl.BlockSpec(memory_space=pltpu.VMEM)] * len(outs),
         scratch_shapes=list(scratch),
+        input_output_aliases=alias or {},
         compiler_params=pltpu.CompilerParams(vmem_limit_bytes=vmem * MIB),
         cost_estimate=pl.CostEstimate(flops=flops, bytes_accessed=size, transcendentals=0),
         name=name,
@@ -138,7 +141,7 @@
 
 
 def pack_kernel(own, hidden, wide, info, q, k, v, u, o, g, up, dn, *refs):
-    outs, small, large, sems = refs[:4], refs[4], refs[5], refs[6]
+    outs, wides, small, large, sems = refs[:4], refs[4:8], refs[8], refs[9], refs[10]
     copies = [
         pltpu.make_async_copy(ref, small.at[n], sems.at[n]) for n, ref in enumerate((q, k, v, u, o))
     ] + [pltpu.make_async_copy(ref, large.at[n], sems.at[5 + n]) for n, ref in enumerate((g, up, dn))]
@@ -161,8 +164,7 @@
                         v = jnp.concatenate(
                             [v, jnp.zeros((v.shape[0], wide - hidden), v.dtype)], 1
                         )
-                    lo = 5 * own + n * wide
-                    outs[d][:, lo : lo + wide] = v
+                    wides[d][:, n * wide : (n + 1) * wide] = v
 
 
 def prep_kernel(count, block, info, x, c, h_out, c_out, scr):
@@ -279,7 +281,7 @@
 def ffn_out_kernel(wide, h0, h1, h2, h3, *refs):
     w, outs = refs[:-4], refs[-4:]
     for d, h in enumerate((h0, h1, h2, h3)):
-        outs[d][...] = mm_nt(h[...], columns(w, 2 * wide, 3 * wide)).astype(outs[d].dtype)
+        outs[d][1] = mm_nt(h[...], columns(w, 2 * wide, 3 * wide)).astype(outs[d].dtype)
 
 
 def store_grads(outs, items, groups, rows, lanes, value):
@@ -306,15 +308,13 @@
 
 
 def down_side_kernel(items, groups, rows, wide, own, *refs):
-    c, h, hd, du, og, outs = refs[:4], refs[4:8], refs[8:12], refs[12], refs[13:16], refs[16:]
+    c, h, hd, dq, du, outs = refs[:4], refs[4:8], refs[8:12], refs[12], refs[13], refs[14:]
     left = jnp.concatenate([r[...] for r in c], 0)
     value = mm_tn(left, jnp.concatenate([r[...] for r in hd], 0))
     store_grads(outs, items, groups, rows, slice(0, wide), value)
     left = jnp.concatenate([r[...] for r in h], 0)
-    value = mm_tn(left, jnp.concatenate([du[d] for d in range(4)], 0))
-    store_grads(outs, items, groups, rows, slice(wide, wide + own), value)
-    value = og[0][...].astype(f32) + og[1][...].astype(f32) + og[2][...].astype(f32)
-    store_grads(outs, items, groups, rows, slice(wide + own, wide + 2 * own), value)
+    right = jnp.concatenate([jnp.concatenate([dq[d], du[d]], 1) for d in range(4)], 0)
+    store_grads(outs, items, groups, rows, slice(wide, wide + 2 * own), mm_tn(left, right))
 
 
 def next_kernel(keep2, got, out):
@@ -407,19 +407,23 @@
         total[n] = state
 
 
-def back_local_kernel(own, size, da, v, w, q, k, plow, mask, qd, dq, dk, dv):
+def back_local_kernel(own, size, da, v, w, q, k, plow, mask, qd, q0, cosine, sine, dq, dk, dv):
     for d in range(4):
         for n in range(own // size):
             lanes = slice(n * size, (n + 1) * size)
             a = da[d, :, lanes]
             ds = (mm_nt(a, v[d, :, lanes]) * mask[n]).astype(bf16)
-            dq[d, :, lanes] = mm(ds, k[d, :, lanes]) + mm_nt(a, plow[d, n]) * qd[n]
+            g = mm(ds, k[d, :, lanes]) + mm_nt(a, plow[d, n]) * qd[n]
+            z = q0[d, :, lanes]
+            s = jax.nn.sigmoid(z)
+            g = turn(g, cosine[d], -sine[d]) * s * (1.0 + z * (1.0 - s))
+            dq[d, :, lanes] = g.astype(bf16)
             dk[d, :, lanes] = mm_tn(ds, q[d, :, lanes])
             dv[d, :, lanes] = mm_tn(w[d, n], a)
 
 
-def back_final_kernel(nw, own, size, info, fac, suffix, after, v, ks, du, dq, dk, dv, q0, k0, cosine, sine, kd, *refs):
-    w, outs = refs[:nw], refs[nw:]
+def back_final_kernel(nw, own, size, info, fac, suffix, after, v, ks, du, dq, dk, dv, k0, cosine, sine, kd, *refs):
+    w, outs = refs[:nw], refs[nw + 4 :]
     grads = outs[0]
     parts = outs[1:]
     member = info[0]
@@ -430,28 +434,27 @@
             low = (suffix[b, n] + fac[n, 3 - b] * after[n]).astype(bf16)
             dka = dk[d, :, lanes] + mm_nt(v[d, :, lanes], low) * kd[n]
             dvv = dv[d, :, lanes] + mm(ks[d, :, lanes], low)
-            z = q0[d, :, lanes]
-            s = jax.nn.sigmoid(z)
-            g = turn(dq[d, :, lanes], cosine[d], -sine[d]) * s * (1.0 + z * (1.0 - s))
-            grads[d, :, n * size : (n + 1) * size] = g.astype(bf16)
             z = k0[d, :, lanes]
             s = jax.nn.sigmoid(z)
             g = turn(dka, cosine[d], -sine[d]) * s * (1.0 + z * (1.0 - s))
             grads[d, :, own + n * size : own + (n + 1) * size] = g.astype(bf16)
             grads[d, :, 2 * own + n * size : 2 * own + (n + 1) * size] = dvv.astype(bf16)
+        grads[d, :, :own] = dq[d]
         grads[d, :, 3 * own :] = du[d]
         weights = jnp.concatenate([r[:, : 4 * own] for r in w], 0)
-        parts[d][...] = mm_nt(grads[d], weights).astype(parts[d].dtype)
-
-
-def attn_grad_kernel(items, groups, rows, wide, h0, h1, h2, h3, grads, *outs):
+        parts[d][0] = mm_nt(grads[d], weights).astype(parts[d].dtype)
+
+
+def attn_grad_kernel(items, groups, rows, own, h0, h1, h2, h3, grads, o0, o1, o2, *outs):
     left = jnp.concatenate([h0[...], h1[...], h2[...], h3[...]], 0)
-    value = mm_tn(left, jnp.concatenate([grads[d][:, :wide] for d in range(4)], 0))
-    store_grads(outs, items, groups, rows, slice(0, wide), value)
+    value = mm_tn(left, jnp.concatenate([grads[d][:, own : 3 * own] for d in range(4)], 0))
+    store_grads(outs, items, groups, rows, slice(0, 2 * own), value)
+    value = o0[...].astype(f32) + o1[...].astype(f32) + o2[...].astype(f32)
+    store_grads(outs, items, groups, rows, slice(2 * own, 3 * own), value)
 
 
 def first_back_kernel(count, block, info, x, dy, a0, a1, a2, out, scr):
-    scr[...] = a0[...] + a1[...].astype(f32) + a2[...].astype(f32)
+    scr[...] = a0[0] + a1[0].astype(f32) + a2[0].astype(f32)
     grad = blocks_of(scr, count, block, info[1])
     v = x[...].astype(f32)
     scale = norm_factor(v)
@@ -459,7 +462,7 @@
 
 
 def mixed_kernel(count, block, info, y, a0, a1, a2, out, scr):
-    scr[...] = a0[...] + a1[...].astype(f32) + a2[...].astype(f32)
+    scr[...] = a0[1] + a1[1].astype(f32) + a2[1].astype(f32)
     out[...] = (y[...] + blocks_of(scr, count, block, info[1])).astype(bf16)
 
 
@@ -478,7 +481,7 @@
                     lo += wide
 
 
-def scatter_split(at, info, aligned, sums):
+def scatter_split(at, info, aligned, sums, after=()):
     if aligned:
         rows = sums[0][0].shape[0] // 4
         cols = sum(v[0].shape[1] for v in sums)
@@ -488,6 +491,7 @@
             [like((rows, cols), f32)] + [like((rows, cols), bf16)] * 3,
             [info],
             [v for group in sums for v in group],
+            after=after,
         )
     else:
         total = jnp.concatenate([sum(v.astype(f32) for v in group) for group in sums], 1)
@@ -560,10 +564,10 @@
         half = groups // 2
         packed = pl.pallas_call(
             functools.partial(pack_kernel, own, hidden, wide),
-            out_shape=[like((shard, 5 * own + 3 * wide), bf16)] * 4,
+            out_shape=[like((shard, 5 * own), bf16)] * 4 + [like((shard, 3 * wide), bf16)] * 4,
             in_specs=[pl.BlockSpec(memory_space=pltpu.SMEM)]
             + [pl.BlockSpec(memory_space=pltpu.HBM)] * 8,
-            out_specs=[pl.BlockSpec(memory_space=pltpu.VMEM)] * 4,
+            out_specs=[pl.BlockSpec(memory_space=pltpu.VMEM)] * 8,
             scratch_shapes=[
                 pltpu.VMEM((5, shard, width), bf16),
                 pltpu.VMEM((3, shard, 4 * hidden), bf16),
@@ -583,9 +587,8 @@
             up_weight,
             down_weight.T,
         )
-        packed = at.exchange(packed)
-        aw = at.in_order([v[:, : 5 * own] for v in packed])
-        fw = at.in_order([v[:, 5 * own :] for v in packed])
+        aw = at.in_order(at.exchange(packed[:4]))
+        fw = at.in_order(at.exchange(packed[4:]))
         near = [aw] + [at.group_swap(aw, k) for k in range(1, groups)]
 
 
@@ -753,14 +756,15 @@
             return [at.item_swap(outs[0], 1), at.item_swap(outs[3], 2)]
 
         def second_hop(outs, got, after=()):
-            res = []
+            res, sent = [], []
             for p, two in ((0, 2), (1, 1)):
                 keep2, keep0 = outs[3 * p + 1 : 3 * p + 3]
                 (v,) = run(
                     "next", next_kernel, [like(keep2.shape, bf16)], [], [keep2, got[p]], after=after
                 )
                 res += [keep0, got[p], at.item_swap(v, two)]
-            return res
+                sent.append(v)
+            return res, sent
 
         def third_hop(parts, after=()):
             cols = parts[0].shape[1]
@@ -801,16 +805,17 @@
             after=[hidden_outs[0]],
         )
         dz = at.exchange(dz)
-        ffn_parts = run(
+        two_acts = [like((2, rows, width), t) for t in (f32, bf16, f32, bf16)]
+        ffn_parts = [None] * 4
+        ffn_parts[:] = run(
             "ffn_out",
             functools.partial(ffn_out_kernel, wide),
-            [act(f32), act(), act(f32), act()],
+            two_acts,
             [],
             hd + ffn_w,
             flops=8 * rows * width * wide,
             vmem=VM[3],
         )
-        out_sums = at.collect(*ffn_parts)
 
         og = run(
             "out_grad",
@@ -818,7 +823,7 @@
             [like((width, own), f32), like((width, own), bf16)] * 2,
             [info],
             [zp, do],
-            flops=2 * rows * width * width,
+            after=[],
         )
 
         du, da, suffix, gtotal = run(
@@ -829,18 +834,20 @@
             dz + [attn, u, qs],
             [scratch_states],
             flops=8 * rows * size * own,
-            after=[ffn_parts[0]],
+            after=[ffn_parts[0], og[0]],
         )
         after = carried(gtotal, -1)
-        og = at.collect(*og, after=[du])
-        hidden_parts = second_hop(hidden_outs, hidden_got, [du])
+        og_added, og_far = at.collect_far(og[2], og[3], after=[])
+        og = [og[0], at.swap(og[1], 1), og_far]
+        hidden_parts, hidden_sent = second_hop(hidden_outs, hidden_got, [du])
         dq, dk, dv = run(
             "back_local",
             functools.partial(back_local_kernel, own, size),
-            [blk(f32)] * 3,
+            [blk(bf16), blk(f32), blk(f32)],
             [],
-            [da, v, w, q, k, plow, mask, query_decay],
+            [da, v, w, q, k, plow, mask, query_decay, q0, cosine, sine],
             flops=40 * rows * rows * own,
+            after=hidden_sent,
         )
         if aligned:
             ds_outs = run(
@@ -848,57 +855,66 @@
                 functools.partial(down_side_kernel, items, groups, block, wide, own),
                 grad_outs(wide + 2 * own),
                 [],
-                cots + h1 + hd + [du] + og,
+                cots + h1 + hd + [dq, du],
                 flops=8 * rows * width * (wide + own),
                 vmem=VM[2],
-                after=[dq],
             )
         else:
             hh, cc = jnp.concatenate(h1, 0), jnp.concatenate(cots, 0)
             both = [
                 mm_tn(cc, jnp.concatenate(hd, 0)),
+                mm_tn(hh, dq.reshape(4 * rows, own)),
                 mm_tn(hh, du.reshape(4 * rows, own)),
-                sum(v.astype(f32) for v in og),
             ]
             ds_outs = halves(jnp.concatenate(both, 1))
         ds_got = first_hop(ds_outs)
+        hidden_sums = third_hop(hidden_parts)
         grads, *part = run(
             "back_final",
             functools.partial(back_final_kernel, nw, own, size),
-            [like((4, rows, 4 * own), bf16), act(f32), act(), act(f32), act()],
+            [like((4, rows, 4 * own), bf16)] + two_acts,
             [info, fac],
-            [suffix, after, v, ks, du, dq, dk, dv, q0, k0, cosine, sine, key_decay] + attn_w,
+            [suffix, after, v, ks, du, dq, dk, dv, k0, cosine, sine, key_decay] + attn_w + ffn_parts,
             flops=8 * rows * width * 4 * own,
             vmem=VM[0],
-        )
+            after=[],
+            alias={14 + nw + d: 1 + d for d in range(4)},
+        )
+        part_got1, part_got3 = at.swap(part[1], 1), at.swap(part[3], 1)
         if aligned:
             attn_outs = run(
                 "attn_grad",
-                functools.partial(attn_grad_kernel, items, groups, block, 3 * own),
+                functools.partial(attn_grad_kernel, items, groups, block, own),
                 grad_outs(3 * own),
                 [],
-                h1 + [grads],
+                h1 + [grads] + og,
                 flops=6 * rows * width * 4 * own,
                 vmem=VM[2],
-                after=[hidden_parts[2], hidden_parts[5]],
+                after=[hidden_sums[0], part_got1, part_got3],
             )
         else:
-            attn_outs = halves(mm_tn(hh, grads[:, :, : 3 * own].reshape(4 * rows, 3 * own)))
+            both = [
+                mm_tn(hh, grads[:, :, own : 3 * own].reshape(4 * rows, 2 * own)),
+                sum(v.astype(f32) for v in og),
+            ]
+            attn_outs = halves(jnp.concatenate(both, 1))
         attn_got = first_hop(attn_outs)
-        in_sums = at.collect(*part)
-        hidden_sums = third_hop(hidden_parts)
-        ds_sums = third_hop(second_hop(ds_outs, ds_got, [attn_outs[0], hidden_sums[-1]]))
-        attn_sums = third_hop(second_hop(attn_outs, attn_got))
+        ds_parts, ds_sent = second_hop(ds_outs, ds_got, [attn_outs[0], hidden_sums[-1]])
+        attn_parts, attn_sent = second_hop(attn_outs, attn_got, [])
+        ds_sums = third_hop(ds_parts, [])
+        attn_sums = third_hop(attn_parts, [])
+        (both,) = run("add", add_kernel, [two_acts[1]], [], [part[2], part_got3], after=[hidden_sums[0]])
+        in_sums = [part[0], part_got1, at.swap(both, 2)]
         hidden_own = scatter_split(at, info, aligned, [hidden_sums])
-        rest_own = scatter_split(at, info, aligned, [attn_sums, ds_sums])
         (mixed,) = run(
             "mixed",
             functools.partial(mixed_kernel, kcount, kblock),
             [act()],
             [info],
-            [y] + out_sums,
+            [y] + in_sums,
             [pltpu.VMEM((rows, width), f32)],
-            after=[attn_outs[0]],
+            flops=1,
+            after=[],
         )
         tokens_grad = run(
             "first_back",
@@ -907,6 +923,7 @@
             [info],
             [x, dy] + in_sums,
             [pltpu.VMEM((rows, width), f32)],
+            flops=1,
         )[0]
         gg, pg = run(
             "final_hidden",
@@ -914,8 +931,10 @@
             [like((shard, 4 * hidden), f32)] * 2,
             [info],
             hidden_own,
-        )
-        qg, kg, vg, ng, ug, wg = run(
+            flops=1,
+        )
+        rest_own = scatter_split(at, info, aligned, [attn_sums, ds_sums], [mixed, tokens_grad, gg])
+        kg, vg, wg, ng, qg, ug = run(
             "final_rest",
             functools.partial(
                 final_kernel, (own,) * 3 + (wide,) + (own,) * 2, (own,) * 3 + (hidden,) + (own,) * 2
@@ -925,6 +944,7 @@
             + [like((shard, width), f32)] * 2,
             [info],
             rest_own,
+            after=[],
         )
         return (
             mixed.reshape(tokens.shape),

time: 276 us -> 264 us (0.957)
  waiting for transfers between devices: 136 us -> 126 us
    ppermute x68, waiting for transfers between devices: 131 us -> 117 us  [swap(): return lax.ppermute(v, AXES, [(d, d ^ mask) for d in range(self.count)])]
    ppermute x2, waiting for transfers between devices: 5.18 us -> 8.95 us  [group_shift(): return lax.ppermute(v, AXES, pairs)]
    pallas_call x35 -> x34, Pallas kernels: 64.8 us -> 65 us  [run(): pl.pallas_call(body, out_shape=list(outs), in_specs=[pl.BlockSpec(memory_...]
  transfers between devices with their start and end apart: 70 -> 70, of which waited for: 31 -> 35; matrix products, arithmetic and copies ran while one was open for 2% -> 1% of each run, Pallas kernels for 18% -> 20%
where the time goes in v1:
time: 264 us; the launch traced here: 263 us
  waiting for transfers between devices  126 us (48%)
  Pallas kernels  68.2 us (26%)
  starting transfers between devices  62.2 us (24%)
  other arithmetic  4.02 us (2%)
    ppermute x68, waiting for transfers between devices, swap(): return lax.ppermute(v, AXES, [(d, d ^ mask) for d in range(self.count)])  117 us
    pallas_call x34, Pallas kernels, run(): pl.pallas_call(body, out_shape=list(outs), in_specs=[pl.BlockSpec(memory_...  65 us
    ppermute x68, starting transfers between devices, swap(): return lax.ppermute(v, AXES, [(d, d ^ mask) for d in range(self.count)])  55.6 us
    ppermute x2, waiting for transfers between devices, group_shift(): return lax.ppermute(v, AXES, pairs)  8.95 us
    ppermute x2, starting transfers between devices, group_shift(): return lax.ppermute(v, AXES, pairs)  6.55 us
  transfers between devices with their start and end apart: 70, of which 35 were waited for; matrix products, arithmetic and copies ran while one was open for 1% of the time, Pallas kernels for 20%

profile of v1, /device:TPU:0, one launch (start us, length us, event | category | flops | bytes accessed | tf_op | source)
XLA Modules:
  0.0 263.3 jit_solution(4785146880122758695)
XLA Ops:
  1.2 3.2 %pack.1 = (bf16[32,1280]{1,0:T(8,128)(2,1)}, bf16[32,1280]{1,0:T(8,128)(2,1)}, bf16[32,1280]{1,0:T(8,128)(2,1)}, bf16[32,1280]{1,0:T(8,128)(2,1)}, bf16[32,2304]...) custom-call(s32[2]{0:T(128)} %pad_add_fusion.refs_0_.info, ...), custom_call_target="tpu_custom_call" | custom-call | tf_op jit(solution)/shard_map/pack/pallas_call | solution.py:565
  5.0 2.6 %collective-permute-start.1 = (bf16[32,1280]{1,0:T(8,128)(2,1)}, bf16[32,1280]{1,0:T(8,128)(2,1)S(1)}, u32[]{:S(2)}, u32[]{:S(2)}) collective-permute-start(bf16[32,1280]{1,0:T(8,128)(2,1)} %get-tuple-element.127), channel_id=1, source_target_pairs={{0,2},{1,3},{2,0},{3,1},{4,6},{5,7},{6,4},{7,5},{8,10},{9,11},{10,... | collective-permute-start | bytes 245768 | tf_op jit(solution)/shard_map/ppermute | solution.py:89
  7.8 1.9 collective-permute-start.14
  9.9 2.1 fusion.5
  13.4 1.6 collective-permute-start.7
  15.0 2.6 collective-permute-start.6
  17.5 1.5 collective-permute-start.4
  19.5 2.6 collective-permute-done.15
  22.1 1.5 collective-permute-start.9
  23.6 1.5 collective-permute-start.11
  25.1 7.8 %collective-permute-done.6.refs_3_.refs_7_.refs_15_ = bf16[128,1280]{1,0:T(8,128)(2,1)S(1)} collective-permute-done((bf16[128,1280]{1,0:T(8,128)(2,1)S(1)}, bf16[128,1280]{1,0:T(8,128)(2,1)S(1)}, u32[]{:S(2)}, u32[]{:S(2)}) %collective-permute-start.6) | collective-permute-done | bytes 327712 | tf_op jit(solution)/shard_map/ppermute | solution.py:89
  32.9 1.5 collective-permute-start.10
  35.2 2.4 collective-permute-done.4.refs_4_.refs_2_.refs_6_
  37.7 1.5 collective-permute-start.18
  39.2 1.5 collective-permute-start.17
  40.7 2.6 %collective-permute-start.16 = (bf16[128,2304]{1,0:T(8,128)(2,1)S(1)}, bf16[128,2304]{1,0:T(8,128)(2,1)S(1)}, u32[]{:S(2)}, u32[]{:S(2)}) collective-permute-start(bf16[128,2304]{1,0:T(8,128)(2,1)S(1)} %tie.9.refs_4_), channel_id=1, source_target_pairs={{0,4},{1,5},{2,6},{3,7},{4,0},{5,1},{6,2},{7,3},{8,12},{9,13},{10,... | collective-permute-start | bytes 1769480 | tf_op jit(solution)/shard_map/ppermute | solution.py:89
  43.3 3.4 %collective-permute-done.10.refs_11_.refs_19_ = bf16[128,1280]{1,0:T(8,128)(2,1)S(1)} collective-permute-done((bf16[128,1280]{1,0:T(8,128)(2,1)S(1)}, bf16[128,1280]{1,0:T(8,128)(2,1)S(1)}, u32[]{:S(2)}, u32[]{:S(2)}) %collective-permute-start.10) | collective-permute-done | bytes 327712 | tf_op jit(solution)/shard_map/ppermute | solution.py:89
  46.8 2.5 collective-permute-start.12
  49.3 13.7 %collective-permute-done.12.refs_13_.refs_21_ = bf16[128,1280]{1,0:T(8,128)(2,1)S(1)} collective-permute-done((bf16[128,1280]{1,0:T(8,128)(2,1)S(1)}, bf16[128,1280]{1,0:T(8,128)(2,1)S(1)}, u32[]{:S(2)}, u32[]{:S(2)}) %collective-permute-start.12) | collective-permute-done | bytes 327712 | tf_op jit(solution)/shard_map/ppermute | solution.py:89
  63.1 5.8 %collective-permute-done.16.refs_18_.refs_0_ = bf16[128,2304]{1,0:T(8,128)(2,1)S(1)} collective-permute-done((bf16[128,2304]{1,0:T(8,128)(2,1)S(1)}, bf16[128,2304]{1,0:T(8,128)(2,1)S(1)}, u32[]{:S(2)}, u32[]{:S(2)}) %collective-permute-start.16) | collective-permute-done | bytes 589856 | tf_op jit(solution)/shard_map/ppermute | solution.py:89
  69.2 3.9 %project.1 = (f32[4,256,256]{2,1,0:T(8,128)S(1)}, f32[4,256,256]{2,1,0:T(8,128)S(1)}, f32[4,256,256]{2,1,0:T(8,128)S(1)}, bf16[4,256,256]{2,1,0:T(8,128)(2,1)S(1...) custom-call(s32[2]{0:T(128)S(1)} %copy-done.5, ...), custom_call_target="tpu_custom_call" | custom-call | flops 2147483648 | bytes 13238272 | tf_op jit(solution)/shard_map/project/pallas_call | solution.py:53
  75.1 5.3 %collective-permute-start.19 = (f32[2,128,128]{2,1,0:T(8,128)S(1)}, f32[2,128,128]{2,1,0:T(8,128)S(1)}, u32[]{:S(2)}, u32[]{:S(2)}) collective-permute-start(f32[2,128,128]{2,1,0:T(8,128)S(1)} %get-tuple-element.134), channel_id=1, source_target_pairs={{0,4},{1,5},{2,6},{3,7},{8,12},{9,13},{10,14},{11,15},{16,20},{17,... | collective-permute-start | bytes 393224 | tf_op jit(solution)/shard_map/ppermute | solution.py:103
  81.5 5.7 %collective-permute-done.19.refs_3_ = f32[2,128,128]{2,1,0:T(8,128)S(1)} collective-permute-done((f32[2,128,128]{2,1,0:T(8,128)S(1)}, f32[2,128,128]{2,1,0:T(8,128)S(1)}, u32[]{:S(2)}, u32[]{:S(2)}) %collective-permute-start.19) | collective-permute-done | bytes 131104 | tf_op jit(solution)/shard_map/ppermute | solution.py:103
  91.7 3.5 %collective-permute-done.22.refs_4_ = bf16[256,256]{1,0:T(8,128)(2,1)S(1)} collective-permute-done((bf16[256,256]{1,0:T(8,128)(2,1)S(1)}, bf16[256,256]{1,0:T(8,128)(2,1)S(1)}, u32[]{:S(2)}, u32[]{:S(2)}) %collective-permute-start.22) | collective-permute-done | bytes 131104 | tf_op jit(solution)/shard_map/ppermute | solution.py:89
  96.3 1.7 mid.1
  98.0 1.4 collective-permute-start.32
  99.9 1.5 collective-permute-start.31
  101.4 7.9 %collective-permute-done.34.refs_0_ = bf16[256,1024]{1,0:T(8,128)(2,1)S(1)} collective-permute-done((bf16[256,1024]{1,0:T(8,128)(2,1)S(1)}, bf16[256,1024]{1,0:T(8,128)(2,1)S(1)}, u32[]{:S(2)}, u32[]{:S(2)}) %collective-permute-start.34) | collective-permute-done | bytes 524320 | tf_op jit(solution)/shard_map/ppermute | solution.py:89
  109.2 10.4 %collective-permute-done.32.refs_0_.refs_2_ = bf16[256,1024]{1,0:T(8,128)(2,1)S(1)} collective-permute-done((bf16[256,1024]{1,0:T(8,128)(2,1)S(1)}, bf16[256,1024]{1,0:T(8,128)(2,1)S(1)}, u32[]{:S(2)}, u32[]{:S(2)}) %collective-permute-start.32) | collective-permute-done | bytes 524320 | tf_op jit(solution)/shard_map/ppermute | solution.py:89
  119.6 1.9 collective-permute-done.33.refs_1_.refs_3_
  121.5 5.1 %ffn2.1 = (bf16[256,768]{1,0:T(8,128)(2,1)S(1)}, bf16[256,768]{1,0:T(8,128)(2,1)S(1)}, bf16[256,768]{1,0:T(8,128)(2,1)S(1)}, f32[256,1024]{1,0:T(8,128)S(1)}, bf...) custom-call(bf16[256,1024]{1,0:T(8,128)(2,1)S(1)} %collective-permut, ...), custom_call_target="tpu_custom_call" | custom-call | tf_op jit(solution)/shard_map/ffn2/pallas_call | solution.py:53
  130.1 5.1 %ffn0.1 = (bf16[256,768]{1,0:T(8,128)(2,1)S(1)}, bf16[256,768]{1,0:T(8,128)(2,1)S(1)}, bf16[256,768]{1,0:T(8,128)(2,1)S(1)}, f32[256,1024]{1,0:T(8,128)S(1)}, bf...) custom-call(bf16[256,1024]{1,0:T(8,128)(2,1)S(1)} %get-tuple-element, ...), custom_call_target="tpu_custom_call" | custom-call | tf_op jit(solution)/shard_map/ffn0/pallas_call | solution.py:53
  135.4 17.6 %hidden_grad.1 = (bf16[2,128,1536]{2,1,0:T(8,128)(2,1)S(1)}, bf16[128,1536]{1,0:T(8,128)(2,1)S(1)}, bf16[128,1536]{1,0:T(8,128)(2,1)S(1)}, bf16[2,128,1536]{2,1,...) custom-call(bf16[256,1024]{1,0:T(8,128)(2,1)S(1)} %get-tuple-element.148.refs_0_, ...), custom_call_target="tpu_custom_call" | custom-call | tf_op jit(solution)/shard_map/hidden_grad/pallas_call | solution.py:53
  153.6 1.5 collective-permute-start.43
  155.1 2.2 mid_back.1
  159.3 1.8 ffn_out.1
  162.4 1.4 collective-permute-done.40.refs_4_
  163.8 1.9 collective-permute-done.41.refs_5_
  165.7 1.8 back_state.1
  169.6 3.3 %collective-permute-done.44.refs_1_.refs_4_ = bf16[2,128,1536]{2,1,0:T(8,128)(2,1)S(1)} collective-permute-done((bf16[2,128,1536]{2,1,0:T(8,128)(2,1)S(1)}, bf16[2,128,1536]{2,1,0:T(8,128)(2,1)S(1)}, u32[]{:S(2)}, u32[]{:S(2)}) %collective-permute-start.44) | collective-permute-done | bytes 786464 | tf_op jit(solution)/shard_map/ppermute | solution.py:89
  173.2 2.8 %back_local.1 = (bf16[4,256,256]{2,1,0:T(8,128)(2,1)S(1)}, f32[4,256,256]{2,1,0:T(8,128)S(1)}, f32[4,256,256]{2,1,0:T(8,128)S(1)}) custom-call(bf16[4,256,256]{2,1,0:T(8,128)(2,1)S(1)} %get-tuple-element.179.refs_0_, bf16[4,256,256]{2,1,0:T(8,128)(2,1)S(1)} %get-tuple-element.138.refs_2_.refs_1_.refs_4_, ...), custom_call_target="tpu_custom_call" | custom-call | flops 671088640 | bytes 8912896 | tf_op jit(solution)/shard_map/back_local/pallas_call | solution.py:53
  176.0 3.3 %collective-permute-done.42.refs_3_ = f32[2,128,128]{2,1,0:T(8,128)S(1)} collective-permute-done((f32[2,128,128]{2,1,0:T(8,128)S(1)}, f32[2,128,128]{2,1,0:T(8,128)S(1)}, u32[]{:S(2)}, u32[]{:S(2)}) %collective-permute-start.42) | collective-permute-done | bytes 131104 | tf_op jit(solution)/shard_map/ppermute | solution.py:103
  179.2 4.0 %back_final.1 = (bf16[4,256,1024]{2,1,0:T(8,128)(2,1)S(1)}, f32[2,256,1024]{2,1,0:T(8,128)S(1)}, bf16[2,256,1024]{2,1,0:T(8,128)(2,1)S(1)}, f32[2,256,1024]{2,1,0:T(8,128)S(1)}, bf16[2,256,1024]{2,1,0:T(8,128)(2,1)S(1)}) custom-call(s32[2]{0:T(128)S(1)} %copy-done.5, ...), custom_call_target="tpu_custom_call", output_to_operand_aliasing={{1}: (22, {}), {2}: (23, {}), {3}: (24, {}), {4}: (25, {})} | custom-call | flops 2147483648 | bytes 24510464 | tf_op jit(solution)/shard_map/back_final/pallas_call | solution.py:53
  186.0 3.0 %down_side.1 = (bf16[2,128,1280]{2,1,0:T(8,128)(2,1)S(1)}, bf16[128,1280]{1,0:T(8,128)(2,1)S(1)}, bf16[128,1280]{1,0:T(8,128)(2,1)S(1)}, bf16[2,128,1280]{2,1,0:...) custom-call(bf16[256,1024]{1,0:T(8,128)(2,1)S(1)} %tie.12.refs_2_.refs_0_, ...), custom_call_target="tpu_custom_call" | custom-call | flops 2147483648 | bytes 9437184 | tf_op jit(solution)/shard_map/down_side/pallas_call | solution.py:53
  189.0 5.9 %collective-permute-done.47.refs_2_ = bf16[128,1536]{1,0:T(8,128)(2,1)S(1)} collective-permute-done((bf16[128,1536]{1,0:T(8,128)(2,1)S(1)}, bf16[128,1536]{1,0:T(8,128)(2,1)S(1)}, u32[]{:S(2)}, u32[]{:S(2)}) %collective-permute-start.47) | collective-permute-done | bytes 393248 | tf_op jit(solution)/shard_map/ppermute | solution.py:89
  195.5 1.5 collective-permute-start.61
  198.0 1.4 collective-permute-done.52.refs_7_
  200.2 1.6 attn_grad.1
  201.9 8.9 %collective-permute-done.58.refs_1_ = bf16[2,128,1280]{2,1,0:T(8,128)(2,1)S(1)} collective-permute-done((bf16[2,128,1280]{2,1,0:T(8,128)(2,1)S(1)}, bf16[2,128,1280]{2,1,0:T(8,128)(2,1)S(1)}, u32[]{:S(2)}, u32[]{:S(2)}) %collective-permute-start.58) | collective-permute-done | bytes 655392 | tf_op jit(solution)/shard_map/ppermute | solution.py:89
  211.3 4.3 %collective-permute-done.59.refs_3_.refs_2_ = bf16[128,1536]{1,0:T(8,128)(2,1)S(1)} collective-permute-done((bf16[128,1536]{1,0:T(8,128)(2,1)S(1)}, bf16[128,1536]{1,0:T(8,128)(2,1)S(1)}, u32[]{:S(2)}, u32[]{:S(2)}) %collective-permute-start.59) | collective-permute-done | bytes 393248 | tf_op jit(solution)/shard_map/ppermute | solution.py:89
  217.7 3.6 %collective-permute-done.55.refs_1_.refs_4_ = bf16[2,128,768]{2,1,0:T(8,128)(2,1)S(1)} collective-permute-done((bf16[2,128,768]{2,1,0:T(8,128)(2,1)S(1)}, bf16[2,128,768]{2,1,0:T(8,128)(2,1)S(1)}, u32[]{:S(2)}, u32[]{:S(2)}) %collective-permute-start.55) | collective-permute-done | bytes 393248 | tf_op jit(solution)/shard_map/ppermute | solution.py:89
  221.4 1.8 collective-permute-start.56
  224.1 4.2 %collective-permute-done.60.refs_2_ = bf16[128,1280]{1,0:T(8,128)(2,1)S(1)} collective-permute-done((bf16[128,1280]{1,0:T(8,128)(2,1)S(1)}, bf16[128,1280]{1,0:T(8,128)(2,1)S(1)}, u32[]{:S(2)}, u32[]{:S(2)}) %collective-permute-start.60) | collective-permute-done | bytes 327712 | tf_op jit(solution)/shard_map/ppermute | solution.py:89
  231.5 1.9 collective-permute-start.57
  233.4 1.5 collective-permute-start.66
  235.0 7.6 %collective-permute-done.65.refs_3_ = bf16[32,1536]{1,0:T(8,128)(2,1)S(1)} collective-permute-done((bf16[32,1536]{1,0:T(8,128)(2,1)S(1)}, bf16[32,1536]{1,0:T(8,128)(2,1)S(1)}, u32[]{:S(2)}, u32[]{:S(2)}) %collective-permute-start.65) | collective-permute-done | bytes 98336 | tf_op jit(solution)/shard_map/ppermute | solution.py:89
  243.6 1.5 final_hidden.1
  245.1 1.8 mixed.1.refs_5_
  246.9 2.3 first_back.1.refs_6_
  249.2 2.1 collective-permute-done.57.refs_2_
  253.5 1.6 collective-permute-start.69
  255.1 4.5 %collective-permute-done.68.refs_3_ = bf16[32,2048]{1,0:T(8,128)(2,1)S(1)} collective-permute-done((bf16[32,2048]{1,0:T(8,128)(2,1)S(1)}, bf16[32,2048]{1,0:T(8,128)(2,1)S(1)}, u32[]{:S(2)}, u32[]{:S(2)}) %collective-permute-start.68) | collective-permute-done | bytes 131104 | tf_op jit(solution)/shard_map/ppermute | solution.py:89
  259.6 1.9 collective-permute-done.69.refs_4_
  261.5 1.6 final_rest.1
  (159 shorter events, 38.7 us)
Async XLA Ops:
  4.5 8.7 %collective-permute-start = (bf16[32,1280]{1,0:T(8,128)(2,1)}, bf16[32,1280]{1,0:T(8,128)(2,1)S(1)}, u32[]{:S(2)}, u32[]{:S(2)}) collective-permute-start(bf16[32,1280]{1,0:T(8,128)(2,1)} %get-tuple-element.126), channel_id=1, source_target_pairs={{0,1},{1,0},{2,3},{3,2},{4,5},{5,4},{6,7},{7,6},{8,9},{9,8},{10,11... | collective-permute-start | bytes 245768 | tf_op jit(solution)/shard_map/ppermute | solution.py:89
  5.0 8.3 %collective-permute-start.1 = (bf16[32,1280]{1,0:T(8,128)(2,1)}, bf16[32,1280]{1,0:T(8,128)(2,1)S(1)}, u32[]{:S(2)}, u32[]{:S(2)}) collective-permute-start(bf16[32,1280]{1,0:T(8,128)(2,1)} %get-tuple-element.127), channel_id=1, source_target_pairs={{0,2},{1,3},{2,0},{3,1},{4,6},{5,7},{6,4},{7,5},{8,10},{9,11},{10,... | collective-permute-start | bytes 245768 | tf_op jit(solution)/shard_map/ppermute | solution.py:89
  7.6 5.6 %collective-permute-start.2 = (bf16[32,1280]{1,0:T(8,128)(2,1)}, bf16[32,1280]{1,0:T(8,128)(2,1)S(1)}, u32[]{:S(2)}, u32[]{:S(2)}) collective-permute-start(bf16[32,1280]{1,0:T(8,128)(2,1)} %get-tuple-element.128), channel_id=1, source_target_pairs={{0,3},{1,2},{2,1},{3,0},{4,7},{5,6},{6,5},{7,4},{8,11},{9,10},{10,... | collective-permute-start | bytes 245768 | tf_op jit(solution)/shard_map/ppermute | solution.py:89
  7.7 9.9 %collective-permute-start.13 = (bf16[32,2304]{1,0:T(8,128)(2,1)}, bf16[32,2304]{1,0:T(8,128)(2,1)S(1)}, u32[]{:S(2)}, u32[]{:S(2)}) collective-permute-start(bf16[32,2304]{1,0:T(8,128)(2,1)} %get-tuple-element.130), channel_id=1, source_target_pairs={{0,1},{1,0},{2,3},{3,2},{4,5},{5,4},{6,7},{7,6},{8,9},{9,8},{10,11... | collective-permute-start | bytes 442376 | tf_op jit(solution)/shard_map/ppermute | solution.py:89
  7.8 11.2 %collective-permute-start.14 = (bf16[32,2304]{1,0:T(8,128)(2,1)}, bf16[32,2304]{1,0:T(8,128)(2,1)S(1)}, u32[]{:S(2)}, u32[]{:S(2)}) collective-permute-start(bf16[32,2304]{1,0:T(8,128)(2,1)} %get-tuple-element.131), channel_id=1, source_target_pairs={{0,2},{1,3},{2,0},{3,1},{4,6},{5,7},{6,4},{7,5},{8,10},{9,11},{10,... | collective-permute-start | bytes 442376 | tf_op jit(solution)/shard_map/ppermute | solution.py:89
  13.2 8.9 %collective-permute-start.15 = (bf16[32,2304]{1,0:T(8,128)(2,1)S(1)}, bf16[32,2304]{1,0:T(8,128)(2,1)S(1)}, u32[]{:S(2)}, u32[]{:S(2)}) collective-permute-start(bf16[32,2304]{1,0:T(8,128)(2,1)S(1)} %copy-done.8), channel_id=1, source_target_pairs={{0,3},{1,2},{2,1},{3,0},{4,7},{5,6},{6,5},{7,4},{8,11},{9,10},{10,... | collective-permute-start | bytes 442376 | tf_op jit(solution)/shard_map/ppermute | solution.py:89
  13.4 10.2 %collective-permute-start.7 = (bf16[128,1280]{1,0:T(8,128)(2,1)S(1)}, bf16[128,1280]{1,0:T(8,128)(2,1)S(1)}, u32[]{:S(2)}, u32[]{:S(2)}) collective-permute-start(bf16[128,1280]{1,0:T(8,128)(2,1)S(1)} %maximum_select_fusion.3.refs_1_.refs_6_.refs_14_), channel_id=1, source_target_pairs={{0,8},{1,9},{2,10},{3,11},{4,12},{5,13},{6,14},{7,15},{8,0},{9,1},... | collective-permute-start | bytes 983048 | tf_op jit(solution)/shard_map/ppermute | solution.py:89
  15.0 17.9 %collective-permute-start.6 = (bf16[128,1280]{1,0:T(8,128)(2,1)S(1)}, bf16[128,1280]{1,0:T(8,128)(2,1)S(1)}, u32[]{:S(2)}, u32[]{:S(2)}) collective-permute-start(bf16[128,1280]{1,0:T(8,128)(2,1)S(1)} %maximum_select_fusion.3.refs_1_.refs_6_.refs_14_), channel_id=1, source_target_pairs={{0,4},{1,5},{2,6},{3,7},{4,0},{5,1},{6,2},{7,3},{8,12},{9,13},{10,... | collective-permute-start | bytes 983048 | tf_op jit(solution)/shard_map/ppermute | solution.py:89
  17.5 20.1 %collective-permute-start.4 = (bf16[256,1024]{1,0:T(8,128)(2,1)S(1)}, bf16[256,1024]{1,0:T(8,128)(2,1)S(1)}, u32[]{:S(2)}, u32[]{:S(2)}) collective-permute-start(bf16[256,1024]{1,0:T(8,128)(2,1)S(1)} %tie.8.refs_2_.refs_0_.refs_4_), channel_id=1, source_target_pairs={{0,2},{1,3},{2,0},{3,1},{4,6},{5,7},{6,4},{7,5},{8,10},{9,11},{10,... | collective-permute-start | bytes 1572872 | tf_op jit(solution)/shard_map/ppermute | solution.py:89
  19.0 20.1 %collective-permute-start.3 = (bf16[256,1024]{1,0:T(8,128)(2,1)S(1)}, bf16[256,1024]{1,0:T(8,128)(2,1)S(1)}, u32[]{:S(2)}, u32[]{:S(2)}) collective-permute-start(bf16[256,1024]{1,0:T(8,128)(2,1)S(1)} %tie.8.refs_2_.refs_0_.refs_4_), channel_id=1, source_target_pairs={{0,1},{1,0},{2,3},{3,2},{4,5},{5,4},{6,7},{7,6},{8,9},{9,8},{10,11... | collective-permute-start | bytes 1572872 | tf_op jit(solution)/shard_map/ppermute | solution.py:89
  22.1 12.5 %collective-permute-start.9 = (bf16[128,1280]{1,0:T(8,128)(2,1)S(1)}, bf16[128,1280]{1,0:T(8,128)(2,1)S(1)}, u32[]{:S(2)}, u32[]{:S(2)}) collective-permute-start(bf16[128,1280]{1,0:T(8,128)(2,1)S(1)} %maximum_select_fusion.3.refs_1_.refs_6_.refs_14_), channel_id=1, source_target_pairs={{0,16},{1,17},{2,18},{3,19},{4,20},{5,21},{6,22},{7,23},{8,24},{9,... | collective-permute-start | bytes 983048 | tf_op jit(solution)/shard_map/ppermute | solution.py:89
  23.6 17.1 %collective-permute-start.11 = (bf16[128,1280]{1,0:T(8,128)(2,1)S(1)}, bf16[128,1280]{1,0:T(8,128)(2,1)S(1)}, u32[]{:S(2)}, u32[]{:S(2)}) collective-permute-start(bf16[128,1280]{1,0:T(8,128)(2,1)S(1)} %collective-permute-done.7.refs_1_.refs_8_.refs_16_), channel_id=1, source_target_pairs={{0,16},{1,17},{2,18},{3,19},{4,20},{5,21},{6,22},{7,23},{8,24},{9,... | collective-permute-start | bytes 983048 | tf_op jit(solution)/shard_map/ppermute | solution.py:89
  32.9 13.8 %collective-permute-start.10 = (bf16[128,1280]{1,0:T(8,128)(2,1)S(1)}, bf16[128,1280]{1,0:T(8,128)(2,1)S(1)}, u32[]{:S(2)}, u32[]{:S(2)}) collective-permute-start(bf16[128,1280]{1,0:T(8,128)(2,1)S(1)} %collective-permute-done.6.refs_3_.refs_7_.refs_15_), channel_id=1, source_target_pairs={{0,16},{1,17},{2,18},{3,19},{4,20},{5,21},{6,22},{7,23},{8,24},{9,... | collective-permute-start | bytes 983048 | tf_op jit(solution)/shard_map/ppermute | solution.py:89
  34.6 12.1 %collective-permute-start.8 = (bf16[128,1280]{1,0:T(8,128)(2,1)S(1)}, bf16[128,1280]{1,0:T(8,128)(2,1)S(1)}, u32[]{:S(2)}, u32[]{:S(2)}) collective-permute-start(bf16[128,1280]{1,0:T(8,128)(2,1)S(1)} %collective-permute-done.6.refs_3_.refs_7_.refs_15_), channel_id=1, source_target_pairs={{0,8},{1,9},{2,10},{3,11},{4,12},{5,13},{6,14},{7,15},{8,0},{9,1},... | collective-permute-start | bytes 983048 | tf_op jit(solution)/shard_map/ppermute | solution.py:89
  37.7 25.4 %collective-permute-start.18 = (bf16[128,2304]{1,0:T(8,128)(2,1)S(1)}, bf16[128,2304]{1,0:T(8,128)(2,1)S(1)}, u32[]{:S(2)}, u32[]{:S(2)}) collective-permute-start(bf16[128,2304]{1,0:T(8,128)(2,1)S(1)} %tie.9.refs_4_), channel_id=1, source_target_pairs={{0,16},{1,17},{2,18},{3,19},{4,20},{5,21},{6,22},{7,23},{8,24},{9,... | collective-permute-start | bytes 1769480 | tf_op jit(solution)/shard_map/ppermute | solution.py:89
  39.2 23.9 %collective-permute-start.17 = (bf16[128,2304]{1,0:T(8,128)(2,1)S(1)}, bf16[128,2304]{1,0:T(8,128)(2,1)S(1)}, u32[]{:S(2)}, u32[]{:S(2)}) collective-permute-start(bf16[128,2304]{1,0:T(8,128)(2,1)S(1)} %tie.9.refs_4_), channel_id=1, source_target_pairs={{0,8},{1,9},{2,10},{3,11},{4,12},{5,13},{6,14},{7,15},{8,0},{9,1},... | collective-permute-start | bytes 1769480 | tf_op jit(solution)/shard_map/ppermute | solution.py:89
  40.7 28.3 %collective-permute-start.16 = (bf16[128,2304]{1,0:T(8,128)(2,1)S(1)}, bf16[128,2304]{1,0:T(8,128)(2,1)S(1)}, u32[]{:S(2)}, u32[]{:S(2)}) collective-permute-start(bf16[128,2304]{1,0:T(8,128)(2,1)S(1)} %tie.9.refs_4_), channel_id=1, source_target_pairs={{0,4},{1,5},{2,6},{3,7},{4,0},{5,1},{6,2},{7,3},{8,12},{9,13},{10,... | collective-permute-start | bytes 1769480 | tf_op jit(solution)/shard_map/ppermute | solution.py:89
  46.7 16.4 %collective-permute-start.5 = (bf16[256,1024]{1,0:T(8,128)(2,1)S(1)}, bf16[256,1024]{1,0:T(8,128)(2,1)S(1)}, u32[]{:S(2)}, u32[]{:S(2)}) collective-permute-start(bf16[256,1024]{1,0:T(8,128)(2,1)S(1)} %collective-permute-done.4.refs_4_.refs_2_.refs_6_), channel_id=1, source_target_pairs={{0,1},{1,0},{2,3},{3,2},{4,5},{5,4},{6,7},{7,6},{8,9},{9,8},{10,11... | collective-permute-start | bytes 1572872 | tf_op jit(solution)/shard_map/ppermute | solution.py:89
  46.8 16.3 %collective-permute-start.12 = (bf16[128,1280]{1,0:T(8,128)(2,1)S(1)}, bf16[128,1280]{1,0:T(8,128)(2,1)S(1)}, u32[]{:S(2)}, u32[]{:S(2)}) collective-permute-start(bf16[128,1280]{1,0:T(8,128)(2,1)S(1)} %collective-permute-done.10.refs_11_.refs_19_), channel_id=1, source_target_pairs={{0,8},{1,9},{2,10},{3,11},{4,12},{5,13},{6,14},{7,15},{8,0},{9,1},... | collective-permute-start | bytes 983048 | tf_op jit(solution)/shard_map/ppermute | solution.py:89
  73.1 15.1 %collective-permute-start.24 = (bf16[1024,256]{1,0:T(8,128)(2,1)S(1)}, bf16[1024,256]{1,0:T(8,128)(2,1)S(1)}, u32[]{:S(2)}, u32[]{:S(2)}) collective-permute-start(bf16[1024,256]{1,0:T(8,128)(2,1)S(1)} %get-tuple-element.141.refs_6_), channel_id=1, source_target_pairs={{0,2},{1,3},{2,0},{3,1},{4,6},{5,7},{6,4},{7,5},{8,10},{9,11},{10,... | collective-permute-start | bytes 1572872 | tf_op jit(solution)/shard_map/ppermute | solution.py:89
  73.3 13.8 %collective-permute-start.20 = (bf16[1024,256]{1,0:T(8,128)(2,1)S(1)}, bf16[1024,256]{1,0:T(8,128)(2,1)S(1)}, u32[]{:S(2)}, u32[]{:S(2)}) collective-permute-start(bf16[1024,256]{1,0:T(8,128)(2,1)S(1)} %get-tuple-element.141.refs_6_), channel_id=1, source_target_pairs={{0,1},{1,0},{2,3},{3,2},{4,5},{5,4},{6,7},{7,6},{8,9},{9,8},{10,11... | collective-permute-start | bytes 1572872 | tf_op jit(solution)/shard_map/ppermute | solution.py:89
  73.5 15.8 %collective-permute-start.27 = (bf16[128,2304]{1,0:T(8,128)(2,1)S(1)}, bf16[128,2304]{1,0:T(8,128)(2,1)S(1)}, u32[]{:S(2)}, u32[]{:S(2)}) collective-permute-start(bf16[128,2304]{1,0:T(8,128)(2,1)S(1)} %tie.11.refs_5_), channel_id=1, source_target_pairs={{0,8},{1,9},{2,10},{3,11},{4,12},{5,13},{6,14},{7,15},{8,0},{9,1},... | collective-permute-start | bytes 1769480 | tf_op jit(solution)/shard_map/ppermute | solution.py:89
  74.3 16.3 %collective-permute-start.26 = (bf16[128,2304]{1,0:T(8,128)(2,1)S(1)}, bf16[128,2304]{1,0:T(8,128)(2,1)S(1)}, u32[]{:S(2)}, u32[]{:S(2)}) collective-permute-start(bf16[128,2304]{1,0:T(8,128)(2,1)S(1)} %tie.11.refs_5_), channel_id=1, source_target_pairs={{0,16},{1,17},{2,18},{3,19},{4,20},{5,21},{6,22},{7,23},{8,24},{9,... | collective-permute-start | bytes 1769480 | tf_op jit(solution)/shard_map/ppermute | solution.py:89
  75.1 12.0 %collective-permute-start.19 = (f32[2,128,128]{2,1,0:T(8,128)S(1)}, f32[2,128,128]{2,1,0:T(8,128)S(1)}, u32[]{:S(2)}, u32[]{:S(2)}) collective-permute-start(f32[2,128,128]{2,1,0:T(8,128)S(1)} %get-tuple-element.134), channel_id=1, source_target_pairs={{0,4},{1,5},{2,6},{3,7},{8,12},{9,13},{10,14},{11,15},{16,20},{17,... | collective-permute-start | bytes 393224 | tf_op jit(solution)/shard_map/ppermute | solution.py:103
  88.3 8.0 %collective-permute-start.25 = (bf16[1024,256]{1,0:T(8,128)(2,1)S(1)}, bf16[1024,256]{1,0:T(8,128)(2,1)S(1)}, u32[]{:S(2)}, u32[]{:S(2)}) collective-permute-start(bf16[1024,256]{1,0:T(8,128)(2,1)S(1)} %tie.10.refs_8_), channel_id=1, source_target_pairs={{0,1},{1,0},{2,3},{3,2},{4,5},{5,4},{6,7},{7,6},{8,9},{9,8},{10,11... | collective-permute-start | bytes 1572872 | tf_op jit(solution)/shard_map/ppermute | solution.py:89
  88.3 3.4 %collective-permute-start.21 = (bf16[256,256]{1,0:T(8,128)(2,1)S(1)}, bf16[256,256]{1,0:T(8,128)(2,1)S(1)}, u32[]{:S(2)}, u32[]{:S(2)}) collective-permute-start(bf16[256,256]{1,0:T(8,128)(2,1)S(1)} %get-tuple-element.143), channel_id=1, source_target_pairs={{0,1},{1,0},{2,3},{3,2},{4,5},{5,4},{6,7},{7,6},{8,9},{9,8},{10,11... | collective-permute-start | bytes 393224 | tf_op jit(solution)/shard_map/ppermute | solution.py:89
  88.8 6.4 %collective-permute-start.22 = (bf16[256,256]{1,0:T(8,128)(2,1)S(1)}, bf16[256,256]{1,0:T(8,128)(2,1)S(1)}, u32[]{:S(2)}, u32[]{:S(2)}) collective-permute-start(bf16[256,256]{1,0:T(8,128)(2,1)S(1)} %get-tuple-element.144), channel_id=1, source_target_pairs={{0,2},{1,3},{2,0},{3,1},{4,6},{5,7},{6,4},{7,5},{8,10},{9,11},{10,... | collective-permute-start | bytes 393224 | tf_op jit(solution)/shard_map/ppermute | solution.py:89
  89.3 6.9 %collective-permute-start.23 = (bf16[256,256]{1,0:T(8,128)(2,1)S(1)}, bf16[256,256]{1,0:T(8,128)(2,1)S(1)}, u32[]{:S(2)}, u32[]{:S(2)}) collective-permute-start(bf16[256,256]{1,0:T(8,128)(2,1)S(1)} %get-tuple-element.145), channel_id=1, source_target_pairs={{0,3},{1,2},{2,1},{3,0},{4,7},{5,6},{6,5},{7,4},{8,11},{9,10},{10,... | collective-permute-start | bytes 393224 | tf_op jit(solution)/shard_map/ppermute | solution.py:89
  90.6 18.7 %collective-permute-start.34 = (bf16[256,1024]{1,0:T(8,128)(2,1)S(1)}, bf16[256,1024]{1,0:T(8,128)(2,1)S(1)}, u32[]{:S(2)}, u32[]{:S(2)}) collective-permute-start(bf16[256,1024]{1,0:T(8,128)(2,1)S(1)} %tie.12.refs_2_.refs_0_), channel_id=1, source_target_pairs={{0,2},{1,3},{2,0},{3,1},{4,6},{5,7},{6,4},{7,5},{8,10},{9,11},{10,... | collective-permute-start | bytes 1572872 | tf_op jit(solution)/shard_map/ppermute | solution.py:89
  98.0 21.6 %collective-permute-start.32 = (bf16[256,1024]{1,0:T(8,128)(2,1)S(1)}, bf16[256,1024]{1,0:T(8,128)(2,1)S(1)}, u32[]{:S(2)}, u32[]{:S(2)}) collective-permute-start(bf16[256,1024]{1,0:T(8,128)(2,1)S(1)} %get-tuple-element.148.refs_0_), channel_id=1, source_target_pairs={{0,2},{1,3},{2,0},{3,1},{4,6},{5,7},{6,4},{7,5},{8,10},{9,11},{10,... | collective-permute-start | bytes 1572872 | tf_op jit(solution)/shard_map/ppermute | solution.py:89
  99.4 20.2 %collective-permute-start.30 = (bf16[128,2304]{1,0:T(8,128)(2,1)S(1)}, bf16[128,2304]{1,0:T(8,128)(2,1)S(1)}, u32[]{:S(2)}, u32[]{:S(2)}) collective-permute-start(bf16[128,2304]{1,0:T(8,128)(2,1)S(1)} %tie.13.refs_6_), channel_id=1, source_target_pairs={{0,16},{1,17},{2,18},{3,19},{4,20},{5,21},{6,22},{7,23},{8,24},{9,... | collective-permute-start | bytes 1769480 | tf_op jit(solution)/shard_map/ppermute | solution.py:89
  99.9 19.7 %collective-permute-start.31 = (bf16[128,2304]{1,0:T(8,128)(2,1)S(1)}, bf16[128,2304]{1,0:T(8,128)(2,1)S(1)}, u32[]{:S(2)}, u32[]{:S(2)}) collective-permute-start(bf16[128,2304]{1,0:T(8,128)(2,1)S(1)} %tie.14.refs_9_), channel_id=1, source_target_pairs={{0,8},{1,9},{2,10},{3,11},{4,12},{5,13},{6,14},{7,15},{8,0},{9,1},... | collective-permute-start | bytes 1769480 | tf_op jit(solution)/shard_map/ppermute | solution.py:89
  109.2 10.4 %collective-permute-start.35 = (bf16[256,1024]{1,0:T(8,128)(2,1)S(1)}, bf16[256,1024]{1,0:T(8,128)(2,1)S(1)}, u32[]{:S(2)}, u32[]{:S(2)}) collective-permute-start(bf16[256,1024]{1,0:T(8,128)(2,1)S(1)} %tie.15.refs_2_), channel_id=1, source_target_pairs={{0,1},{1,0},{2,3},{3,2},{4,5},{5,4},{6,7},{7,6},{8,9},{9,8},{10,11... | collective-permute-start | bytes 1572872 | tf_op jit(solution)/shard_map/ppermute | solution.py:89
  128.7 26.4 %collective-permute-start.38 = (bf16[256,1024]{1,0:T(8,128)(2,1)S(1)}, bf16[256,1024]{1,0:T(8,128)(2,1)S(1)}, u32[]{:S(2)}, u32[]{:S(2)}) collective-permute-start(bf16[256,1024]{1,0:T(8,128)(2,1)S(1)} %add.91.refs_12_), channel_id=1, source_target_pairs={{0,2},{1,3},{2,0},{3,1},{4,6},{5,7},{6,4},{7,5},{8,10},{9,11},{10,... | collective-permute-start | bytes 1572872 | tf_op jit(solution)/shard_map/ppermute | solution.py:89
  135.2 19.9 %collective-permute-start.37 = (bf16[256,1024]{1,0:T(8,128)(2,1)S(1)}, bf16[256,1024]{1,0:T(8,128)(2,1)S(1)}, u32[]{:S(2)}, u32[]{:S(2)}) collective-permute-start(bf16[256,1024]{1,0:T(8,128)(2,1)S(1)} %get-tuple-element.153), channel_id=1, source_target_pairs={{0,1},{1,0},{2,3},{3,2},{4,5},{5,4},{6,7},{7,6},{8,9},{9,8},{10,11... | collective-permute-start | bytes 1572872 | tf_op jit(solution)/shard_map/ppermute | solution.py:89
  153.0 19.9 %collective-permute-start.44 = (bf16[2,128,1536]{2,1,0:T(8,128)(2,1)S(1)}, bf16[2,128,1536]{2,1,0:T(8,128)(2,1)S(1)}, u32[]{:S(2)}, u32[]{:S(2)}) collective-permute-start(bf16[2,128,1536]{2,1,0:T(8,128)(2,1)S(1)} %get-tuple-element.185), channel_id=1, source_target_pairs={{0,16},{1,17},{2,18},{3,19},{4,20},{5,21},{6,22},{7,23},{8,24},{9,... | collective-permute-start | bytes 2359304 | tf_op jit(solution)/shard_map/ppermute | solution.py:89
  153.6 19.5 %collective-permute-start.43 = (bf16[2,128,1536]{2,1,0:T(8,128)(2,1)S(1)}, bf16[2,128,1536]{2,1,0:T(8,128)(2,1)S(1)}, u32[]{:S(2)}, u32[]{:S(2)}) collective-permute-start(bf16[2,128,1536]{2,1,0:T(8,128)(2,1)S(1)} %get-tuple-element.162.refs_10_), channel_id=1, source_target_pairs={{0,8},{1,9},{2,10},{3,11},{4,12},{5,13},{6,14},{7,15},{8,0},{9,1},... | collective-permute-start | bytes 2359304 | tf_op jit(solution)/shard_map/ppermute | solution.py:89
  157.4 5.1 %collective-permute-start.39 = (bf16[256,256]{1,0:T(8,128)(2,1)S(1)}, bf16[256,256]{1,0:T(8,128)(2,1)S(1)}, u32[]{:S(2)}, u32[]{:S(2)}) collective-permute-start(bf16[256,256]{1,0:T(8,128)(2,1)S(1)} %get-tuple-element.164), channel_id=1, source_target_pairs={{0,1},{1,0},{2,3},{3,2},{4,5},{5,4},{6,7},{7,6},{8,9},{9,8},{10,11... | collective-permute-start | bytes 393224 | tf_op jit(solution)/shard_map/ppermute | solution.py:89
  157.4 6.4 %collective-permute-start.40 = (bf16[256,256]{1,0:T(8,128)(2,1)S(1)}, bf16[256,256]{1,0:T(8,128)(2,1)S(1)}, u32[]{:S(2)}, u32[]{:S(2)}) collective-permute-start(bf16[256,256]{1,0:T(8,128)(2,1)S(1)} %get-tuple-element.165), channel_id=1, source_target_pairs={{0,2},{1,3},{2,0},{3,1},{4,6},{5,7},{6,4},{7,5},{8,10},{9,11},{10,... | collective-permute-start | bytes 393224 | tf_op jit(solution)/shard_map/ppermute | solution.py:89
  158.1 7.6 %collective-permute-start.41 = (bf16[256,256]{1,0:T(8,128)(2,1)S(1)}, bf16[256,256]{1,0:T(8,128)(2,1)S(1)}, u32[]{:S(2)}, u32[]{:S(2)}) collective-permute-start(bf16[256,256]{1,0:T(8,128)(2,1)S(1)} %get-tuple-element.166), channel_id=1, source_target_pairs={{0,3},{1,2},{2,1},{3,0},{4,7},{5,6},{6,5},{7,4},{8,11},{9,10},{10,... | collective-permute-start | bytes 393224 | tf_op jit(solution)/shard_map/ppermute | solution.py:89
  167.5 11.7 %collective-permute-start.42 = (f32[2,128,128]{2,1,0:T(8,128)S(1)}, f32[2,128,128]{2,1,0:T(8,128)S(1)}, u32[]{:S(2)}, u32[]{:S(2)}) collective-permute-start(f32[2,128,128]{2,1,0:T(8,128)S(1)} %get-tuple-element.176), channel_id=1, source_target_pairs={{4,0},{5,1},{6,2},{7,3},{12,8},{13,9},{14,10},{15,11},{20,16},{21,... | collective-permute-start | bytes 393224 | tf_op jit(solution)/shard_map/ppermute | solution.py:103
  168.8 17.1 %collective-permute-start.50 = (bf16[1024,256]{1,0:T(8,128)(2,1)S(1)}, bf16[1024,256]{1,0:T(8,128)(2,1)S(1)}, u32[]{:S(2)}, u32[]{:S(2)}) collective-permute-start(bf16[1024,256]{1,0:T(8,128)(2,1)S(1)} %get-tuple-element.202), channel_id=1, source_target_pairs={{0,1},{1,0},{2,3},{3,2},{4,5},{5,4},{6,7},{7,6},{8,9},{9,8},{10,11... | collective-permute-start | bytes 1572872 | tf_op jit(solution)/shard_map/ppermute | solution.py:89
  169.5 15.2 %collective-permute-start.51 = (bf16[1024,256]{1,0:T(8,128)(2,1)S(1)}, bf16[1024,256]{1,0:T(8,128)(2,1)S(1)}, u32[]{:S(2)}, u32[]{:S(2)}) collective-permute-start(bf16[1024,256]{1,0:T(8,128)(2,1)S(1)} %get-tuple-element.204), channel_id=1, source_target_pairs={{0,1},{1,0},{2,3},{3,2},{4,5},{5,4},{6,7},{7,6},{8,9},{9,8},{10,11... | collective-permute-start | bytes 1572872 | tf_op jit(solution)/shard_map/ppermute | solution.py:89
  183.2 14.0 %collective-permute-start.46 = (bf16[2,256,1024]{2,1,0:T(8,128)(2,1)S(1)}, bf16[2,256,1024]{2,1,0:T(8,128)(2,1)S(1)}, u32[]{:S(2)}, u32[]{:S(2)}) collective-permute-start(bf16[2,256,1024]{2,1,0:T(8,128)(2,1)S(1)} %get-tuple-element.196), channel_id=1, source_target_pairs={{0,1},{1,0},{2,3},{3,2},{4,5},{5,4},{6,7},{7,6},{8,9},{9,8},{10,11... | collective-permute-start | bytes 3145736 | tf_op jit(solution)/shard_map/ppermute | solution.py:89
  183.3 16.9 %collective-permute-start.45 = (bf16[2,256,1024]{2,1,0:T(8,128)(2,1)S(1)}, bf16[2,256,1024]{2,1,0:T(8,128)(2,1)S(1)}, u32[]{:S(2)}, u32[]{:S(2)}) collective-permute-start(bf16[2,256,1024]{2,1,0:T(8,128)(2,1)S(1)} %get-tuple-element.194), channel_id=1, source_target_pairs={{0,1},{1,0},{2,3},{3,2},{4,5},{5,4},{6,7},{7,6},{8,9},{9,8},{10,11... | collective-permute-start | bytes 3145736 | tf_op jit(solution)/shard_map/ppermute | solution.py:89
  183.8 11.1 %collective-permute-start.47 = (bf16[128,1536]{1,0:T(8,128)(2,1)S(1)}, bf16[128,1536]{1,0:T(8,128)(2,1)S(1)}, u32[]{:S(2)}, u32[]{:S(2)}) collective-permute-start(bf16[128,1536]{1,0:T(8,128)(2,1)S(1)} %next.6.refs_11_), channel_id=1, source_target_pairs={{0,16},{1,17},{2,18},{3,19},{4,20},{5,21},{6,22},{7,23},{8,24},{9,... | collective-permute-start | bytes 1179656 | tf_op jit(solution)/shard_map/ppermute | solution.py:89
  184.7 10.8 %collective-permute-start.48 = (bf16[128,1536]{1,0:T(8,128)(2,1)S(1)}, bf16[128,1536]{1,0:T(8,128)(2,1)S(1)}, u32[]{:S(2)}, u32[]{:S(2)}) collective-permute-start(bf16[128,1536]{1,0:T(8,128)(2,1)S(1)} %next.7.refs_12_), channel_id=1, source_target_pairs={{0,8},{1,9},{2,10},{3,11},{4,12},{5,13},{6,14},{7,15},{8,0},{9,1},... | collective-permute-start | bytes 1179656 | tf_op jit(solution)/shard_map/ppermute | solution.py:89
  186.0 13.4 %collective-permute-start.52 = (bf16[1024,256]{1,0:T(8,128)(2,1)S(1)}, bf16[1024,256]{1,0:T(8,128)(2,1)S(1)}, u32[]{:S(2)}, u32[]{:S(2)}) collective-permute-start(bf16[1024,256]{1,0:T(8,128)(2,1)S(1)} %add.93), channel_id=1, source_target_pairs={{0,2},{1,3},{2,0},{3,1},{4,6},{5,7},{6,4},{7,5},{8,10},{9,11},{10,... | collective-permute-start | bytes 1572872 | tf_op jit(solution)/shard_map/ppermute | solution.py:89
  194.9 15.9 %collective-permute-start.58 = (bf16[2,128,1280]{2,1,0:T(8,128)(2,1)S(1)}, bf16[2,128,1280]{2,1,0:T(8,128)(2,1)S(1)}, u32[]{:S(2)}, u32[]{:S(2)}) collective-permute-start(bf16[2,128,1280]{2,1,0:T(8,128)(2,1)S(1)} %get-tuple-element.214), channel_id=1, source_target_pairs={{0,8},{1,9},{2,10},{3,11},{4,12},{5,13},{6,14},{7,15},{8,0},{9,1},... | collective-permute-start | bytes 1966088 | tf_op jit(solution)/shard_map/ppermute | solution.py:89
  195.5 21.1 %collective-permute-start.61 = (bf16[2,128,1280]{2,1,0:T(8,128)(2,1)S(1)}, bf16[2,128,1280]{2,1,0:T(8,128)(2,1)S(1)}, u32[]{:S(2)}, u32[]{:S(2)}) collective-permute-start(bf16[2,128,1280]{2,1,0:T(8,128)(2,1)S(1)} %get-tuple-element.218), channel_id=1, source_target_pairs={{0,16},{1,17},{2,18},{3,19},{4,20},{5,21},{6,22},{7,23},{8,24},{9,... | collective-permute-start | bytes 1966088 | tf_op jit(solution)/shard_map/ppermute | solution.py:89
  197.2 18.4 %collective-permute-start.59 = (bf16[128,1536]{1,0:T(8,128)(2,1)S(1)}, bf16[128,1536]{1,0:T(8,128)(2,1)S(1)}, u32[]{:S(2)}, u32[]{:S(2)}) collective-permute-start(bf16[128,1536]{1,0:T(8,128)(2,1)S(1)} %get-tuple-element.216), channel_id=1, source_target_pairs={{0,4},{1,5},{2,6},{3,7},{4,0},{5,1},{6,2},{7,3},{8,12},{9,13},{10,... | collective-permute-start | bytes 1179656 | tf_op jit(solution)/shard_map/ppermute | solution.py:89
  199.4 45.8 %collective-permute-start.49 = (bf16[2,256,1024]{2,1,0:T(8,128)(2,1)S(1)}, bf16[2,256,1024]{2,1,0:T(8,128)(2,1)S(1)}, u32[]{:S(2)}, u32[]{:S(2)}) collective-permute-start(bf16[2,256,1024]{2,1,0:T(8,128)(2,1)S(1)} %add.92), channel_id=1, source_target_pairs={{0,2},{1,3},{2,0},{3,1},{4,6},{5,7},{6,4},{7,5},{8,10},{9,11},{10,... | collective-permute-start | bytes 3145736 | tf_op jit(solution)/shard_map/ppermute | solution.py:89
  201.8 19.5 %collective-permute-start.55 = (bf16[2,128,768]{2,1,0:T(8,128)(2,1)S(1)}, bf16[2,128,768]{2,1,0:T(8,128)(2,1)S(1)}, u32[]{:S(2)}, u32[]{:S(2)}) collective-permute-start(bf16[2,128,768]{2,1,0:T(8,128)(2,1)S(1)} %get-tuple-element.209), channel_id=1, source_target_pairs={{0,16},{1,17},{2,18},{3,19},{4,20},{5,21},{6,22},{7,23},{8,24},{9,... | collective-permute-start | bytes 1179656 | tf_op jit(solution)/shard_map/ppermute | solution.py:89
  210.8 12.4 %collective-permute-start.53 = (bf16[2,128,768]{2,1,0:T(8,128)(2,1)S(1)}, bf16[2,128,768]{2,1,0:T(8,128)(2,1)S(1)}, u32[]{:S(2)}, u32[]{:S(2)}) collective-permute-start(bf16[2,128,768]{2,1,0:T(8,128)(2,1)S(1)} %get-tuple-element.206.refs_2_), channel_id=1, source_target_pairs={{0,8},{1,9},{2,10},{3,11},{4,12},{5,13},{6,14},{7,15},{8,0},{9,1},... | collective-permute-start | bytes 1179656 | tf_op jit(solution)/shard_map/ppermute | solution.py:89
  215.7 12.7 %collective-permute-start.60 = (bf16[128,1280]{1,0:T(8,128)(2,1)S(1)}, bf16[128,1280]{1,0:T(8,128)(2,1)S(1)}, u32[]{:S(2)}, u32[]{:S(2)}) collective-permute-start(bf16[128,1280]{1,0:T(8,128)(2,1)S(1)} %next.10), channel_id=1, source_target_pairs={{0,16},{1,17},{2,18},{3,19},{4,20},{5,21},{6,22},{7,23},{8,24},{9,... | collective-permute-start | bytes 983048 | tf_op jit(solution)/shard_map/ppermute | solution.py:89
  216.7 12.6 %collective-permute-start.62 = (bf16[128,1280]{1,0:T(8,128)(2,1)S(1)}, bf16[128,1280]{1,0:T(8,128)(2,1)S(1)}, u32[]{:S(2)}, u32[]{:S(2)}) collective-permute-start(bf16[128,1280]{1,0:T(8,128)(2,1)S(1)} %next.11), channel_id=1, source_target_pairs={{0,8},{1,9},{2,10},{3,11},{4,12},{5,13},{6,14},{7,15},{8,0},{9,1},... | collective-permute-start | bytes 983048 | tf_op jit(solution)/shard_map/ppermute | solution.py:89
  221.4 10.0 %collective-permute-start.56 = (bf16[128,768]{1,0:T(8,128)(2,1)S(1)}, bf16[128,768]{1,0:T(8,128)(2,1)S(1)}, u32[]{:S(2)}, u32[]{:S(2)}) collective-permute-start(bf16[128,768]{1,0:T(8,128)(2,1)S(1)} %next.9), channel_id=1, source_target_pairs={{0,8},{1,9},{2,10},{3,11},{4,12},{5,13},{6,14},{7,15},{8,0},{9,1},... | collective-permute-start | bytes 589832 | tf_op jit(solution)/shard_map/ppermute | solution.py:89
  223.2 8.2 %collective-permute-start.54 = (bf16[128,768]{1,0:T(8,128)(2,1)S(1)}, bf16[128,768]{1,0:T(8,128)(2,1)S(1)}, u32[]{:S(2)}, u32[]{:S(2)}) collective-permute-start(bf16[128,768]{1,0:T(8,128)(2,1)S(1)} %next.8), channel_id=1, source_target_pairs={{0,16},{1,17},{2,18},{3,19},{4,20},{5,21},{6,22},{7,23},{8,24},{9,... | collective-permute-start | bytes 589832 | tf_op jit(solution)/shard_map/ppermute | solution.py:89
  229.5 19.7 %collective-permute-start.63 = (bf16[128,1280]{1,0:T(8,128)(2,1)S(1)}, bf16[128,1280]{1,0:T(8,128)(2,1)S(1)}, u32[]{:S(2)}, u32[]{:S(2)}) collective-permute-start(bf16[128,1280]{1,0:T(8,128)(2,1)S(1)} %get-tuple-element.221), channel_id=1, source_target_pairs={{0,4},{1,5},{2,6},{3,7},{4,0},{5,1},{6,2},{7,3},{8,12},{9,13},{10,... | collective-permute-start | bytes 983048 | tf_op jit(solution)/shard_map/ppermute | solution.py:89
  231.5 19.8 %collective-permute-start.57 = (bf16[128,768]{1,0:T(8,128)(2,1)S(1)}, bf16[128,768]{1,0:T(8,128)(2,1)S(1)}, u32[]{:S(2)}, u32[]{:S(2)}) collective-permute-start(bf16[128,768]{1,0:T(8,128)(2,1)S(1)} %get-tuple-element.212), channel_id=1, source_target_pairs={{0,4},{1,5},{2,6},{3,7},{4,0},{5,1},{6,2},{7,3},{8,12},{9,13},{10,... | collective-permute-start | bytes 589832 | tf_op jit(solution)/shard_map/ppermute | solution.py:89
  233.4 9.2 %collective-permute-start.65 = (bf16[32,1536]{1,0:T(8,128)(2,1)S(1)}, bf16[32,1536]{1,0:T(8,128)(2,1)S(1)}, u32[]{:S(2)}, u32[]{:S(2)}) collective-permute-start(bf16[32,1536]{1,0:T(8,128)(2,1)S(1)} %get-tuple-element.224), channel_id=1, source_target_pairs={{0,2},{1,3},{2,0},{3,1},{4,6},{5,7},{6,4},{7,5},{8,10},{9,11},{10,... | collective-permute-start | bytes 294920 | tf_op jit(solution)/shard_map/ppermute | solution.py:89
  233.4 10.2 %collective-permute-start.66 = (bf16[32,1536]{1,0:T(8,128)(2,1)S(1)}, bf16[32,1536]{1,0:T(8,128)(2,1)S(1)}, u32[]{:S(2)}, u32[]{:S(2)}) collective-permute-start(bf16[32,1536]{1,0:T(8,128)(2,1)S(1)} %get-tuple-element.225), channel_id=1, source_target_pairs={{0,3},{1,2},{2,1},{3,0},{4,7},{5,6},{6,5},{7,4},{8,11},{9,10},{10,... | collective-permute-start | bytes 294920 | tf_op jit(solution)/shard_map/ppermute | solution.py:89
  253.2 6.4 %collective-permute-start.68 = (bf16[32,2048]{1,0:T(8,128)(2,1)S(1)}, bf16[32,2048]{1,0:T(8,128)(2,1)S(1)}, u32[]{:S(2)}, u32[]{:S(2)}) collective-permute-start(bf16[32,2048]{1,0:T(8,128)(2,1)S(1)} %get-tuple-element.229), channel_id=1, source_target_pairs={{0,2},{1,3},{2,0},{3,1},{4,6},{5,7},{6,4},{7,5},{8,10},{9,11},{10,... | collective-permute-start | bytes 393224 | tf_op jit(solution)/shard_map/ppermute | solution.py:89
  253.5 8.0 %collective-permute-start.69 = (bf16[32,2048]{1,0:T(8,128)(2,1)S(1)}, bf16[32,2048]{1,0:T(8,128)(2,1)S(1)}, u32[]{:S(2)}, u32[]{:S(2)}) collective-permute-start(bf16[32,2048]{1,0:T(8,128)(2,1)S(1)} %get-tuple-element.230), channel_id=1, source_target_pairs={{0,3},{1,2},{2,1},{3,0},{4,7},{5,6},{6,5},{7,4},{8,11},{9,10},{10,... | collective-permute-start | bytes 393224 | tf_op jit(solution)/shard_map/ppermute | solution.py:89
  (16 other events, 89.2 us)

commit v2 on v1

--- a/solution.py
+++ b/solution.py
@@ -14,7 +14,6 @@
 bf16 = jnp.bfloat16
 MIB = 1024 * 1024
 VM = (12, 16, 16, 16)
-WEIGHT = {}
 
 
 def mm(a, b):
@@ -49,7 +48,6 @@
         kernel(*refs[:used], *refs[used + held :])
 
     size = sum(v.size * v.dtype.itemsize for v in list(arrays) + list(outs)) if flops else 0
-    size, flops = (int(v * WEIGHT.get(name, 1)) for v in (size, flops))
     return pl.pallas_call(
         body,
         out_shape=list(outs),
@@ -618,6 +616,8 @@
         h1 = [h1_own, at.swap(h1_own, 1), h1_far, at.swap(h1_far, 1)]
         far_f = [fw] + [at.group_swap(fw, k) for k in range(1, groups)]
         ffn_p = [sides(far_f[k], k) for k in range(half)]
+        cot_own = tie(cot_own, attn_p[-1][1], attn_p[-1][2])
+        cot_far = at.swap(cot_own, 2)
         early = far_f[1:] + [v for got in ffn_p for v in got.values()]
         attn_w = arrange([near[k] if i == 0 else attn_p[k][i] for i in range(items) for k in range(groups)])
         nw = len(attn_w)
@@ -670,8 +670,6 @@
         before = carried(total, 1)
         out_far = at.swap(out_w, 2)
         out_core = at.swap(out_w, 1)
-        cot_own = tie(cot_own, prefix)
-        cot_far = at.swap(cot_own, 2)
         w, intra = run(
             "scores",
             functools.partial(scores_kernel, own, size),
@@ -687,7 +685,7 @@
             [info, fac],
             [prefix, before, qs, intra, u],
             flops=8 * rows * size * own,
-            after=[out_core],
+            after=[out_core, cot_far],
         )
         z = at.exchange(z)
         out_far = tie(out_far, attn)
@@ -826,6 +824,8 @@
             after=[],
         )
 
+        og_added, og_far = at.collect_far(og[2], og[3], after=[])
+        og = [og[0], at.swap(og[1], 1), og_far]
         du, da, suffix, gtotal = run(
             "back_state",
             functools.partial(back_state_kernel, own, size),
@@ -834,11 +834,9 @@
             dz + [attn, u, qs],
             [scratch_states],
             flops=8 * rows * size * own,
-            after=[ffn_parts[0], og[0]],
+            after=[ffn_parts[0], og_added],
         )
         after = carried(gtotal, -1)
-        og_added, og_far = at.collect_far(og[2], og[3], after=[])
-        og = [og[0], at.swap(og[1], 1), og_far]
         hidden_parts, hidden_sent = second_hop(hidden_outs, hidden_got, [du])
         dq, dk, dv = run(
             "back_local",
@@ -877,7 +875,7 @@
             [suffix, after, v, ks, du, dq, dk, dv, k0, cosine, sine, key_decay] + attn_w + ffn_parts,
             flops=8 * rows * width * 4 * own,
             vmem=VM[0],
-            after=[],
+            after=[hidden_sums[0], ds_outs[0], og_far],
             alias={14 + nw + d: 1 + d for d in range(4)},
         )
         part_got1, part_got3 = at.swap(part[1], 1), at.swap(part[3], 1)
@@ -933,7 +931,7 @@
             hidden_own,
             flops=1,
         )
-        rest_own = scatter_split(at, info, aligned, [attn_sums, ds_sums], [mixed, tokens_grad, gg])
+        rest_own = scatter_split(at, info, aligned, [attn_sums, ds_sums], [gg, mixed])
         kg, vg, wg, ng, qg, ug = run(
             "final_rest",
             functools.partial(

time: 264 us -> 261 us (0.989)
  waiting for transfers between devices: 126 us -> 120 us
  starting transfers between devices: 62.2 us -> 65.5 us
    ppermute x68, starting transfers between devices: 55.6 us -> 61.1 us  [swap(): return lax.ppermute(v, AXES, [(d, d ^ mask) for d in range(self.count)])]
    ppermute x2, waiting for transfers between devices: 8.95 us -> 5.42 us  [group_shift(): return lax.ppermute(v, AXES, pairs)]
  transfers between devices with their start and end apart: 70 -> 70, of which waited for: 35 -> 37; matrix products, arithmetic and copies ran while one was open for 1% -> 1% of each run, Pallas kernels for 20% -> 20%
where the time goes in v2:
time: 261 us
  waiting for transfers between devices  120 us (46%)
  Pallas kernels  68.1 us (26%)
  starting transfers between devices  65.5 us (25%)
  other arithmetic  4.02 us (2%)
    ppermute x68, waiting for transfers between devices, swap(): return lax.ppermute(v, AXES, [(d, d ^ mask) for d in range(self.count)])  115 us
    pallas_call x34, Pallas kernels, run(): pl.pallas_call(body, out_shape=list(outs), in_specs=[pl.BlockSpec(memory_...  64.9 us
    ppermute x68, starting transfers between devices, swap(): return lax.ppermute(v, AXES, [(d, d ^ mask) for d in range(self.count)])  61.1 us
    ppermute x2, waiting for transfers between devices, group_shift(): return lax.ppermute(v, AXES, pairs)  5.42 us
  transfers between devices with their start and end apart: 70, of which 37 were waited for; matrix products, arithmetic and copies ran while one was open for 1% of the time, Pallas kernels for 20%

profile of v2, /device:TPU:0, one launch (start us, length us, event | category | flops | bytes accessed | tf_op | source)
XLA Modules:
  0.0 260.6 jit_solution(1823292151049332726)
XLA Ops:
  1.2 3.2 %pack.1 = (bf16[32,1280]{1,0:T(8,128)(2,1)}, bf16[32,1280]{1,0:T(8,128)(2,1)}, bf16[32,1280]{1,0:T(8,128)(2,1)}, bf16[32,1280]{1,0:T(8,128)(2,1)}, bf16[32,2304]...) custom-call(s32[2]{0:T(128)} %pad_add_fusion.refs_0_.info, ...), custom_call_target="tpu_custom_call" | custom-call | tf_op jit(solution)/shard_map/pack/pallas_call | solution.py:563
  5.0 2.6 %collective-permute-start.1 = (bf16[32,1280]{1,0:T(8,128)(2,1)}, bf16[32,1280]{1,0:T(8,128)(2,1)S(1)}, u32[]{:S(2)}, u32[]{:S(2)}) collective-permute-start(bf16[32,1280]{1,0:T(8,128)(2,1)} %get-tuple-element.127), channel_id=1, source_target_pairs={{0,2},{1,3},{2,0},{3,1},{4,6},{5,7},{6,4},{7,5},{8,10},{9,11},{10,... | collective-permute-start | bytes 245768 | tf_op jit(solution)/shard_map/ppermute | solution.py:87
  7.8 1.9 collective-permute-start.14
  9.9 2.1 fusion.5
  13.4 1.6 collective-permute-start.7
  15.0 2.6 collective-permute-start.6
  17.5 1.5 collective-permute-start.4
  19.5 2.6 %collective-permute-done.15 = bf16[32,2304]{1,0:T(8,128)(2,1)S(1)} collective-permute-done((bf16[32,2304]{1,0:T(8,128)(2,1)S(1)}, bf16[32,2304]{1,0:T(8,128)(2,1)S(1)}, u32[]{:S(2)}, u32[]{:S(2)}) %collective-permute-start.15) | collective-permute-done | bytes 147488 | tf_op jit(solution)/shard_map/ppermute | solution.py:87
  22.1 1.5 collective-permute-start.9
  23.6 1.5 collective-permute-start.11
  25.1 7.8 %collective-permute-done.6.refs_3_.refs_7_.refs_15_ = bf16[128,1280]{1,0:T(8,128)(2,1)S(1)} collective-permute-done((bf16[128,1280]{1,0:T(8,128)(2,1)S(1)}, bf16[128,1280]{1,0:T(8,128)(2,1)S(1)}, u32[]{:S(2)}, u32[]{:S(2)}) %collective-permute-start.6) | collective-permute-done | bytes 327712 | tf_op jit(solution)/shard_map/ppermute | solution.py:87
  32.9 1.5 collective-permute-start.10
  35.2 2.4 collective-permute-done.4.refs_4_.refs_6_.refs_2_
  37.7 1.5 collective-permute-start.18
  39.2 1.5 collective-permute-start.17
  40.7 2.6 %collective-permute-start.16 = (bf16[128,2304]{1,0:T(8,128)(2,1)S(1)}, bf16[128,2304]{1,0:T(8,128)(2,1)S(1)}, u32[]{:S(2)}, u32[]{:S(2)}) collective-permute-start(bf16[128,2304]{1,0:T(8,128)(2,1)S(1)} %tie.9.refs_4_), channel_id=1, source_target_pairs={{0,4},{1,5},{2,6},{3,7},{4,0},{5,1},{6,2},{7,3},{8,12},{9,13},{10,... | collective-permute-start | bytes 1769480 | tf_op jit(solution)/shard_map/ppermute | solution.py:87
  43.3 3.4 %collective-permute-done.10.refs_11_.refs_2_.refs_19_ = bf16[128,1280]{1,0:T(8,128)(2,1)S(1)} collective-permute-done((bf16[128,1280]{1,0:T(8,128)(2,1)S(1)}, bf16[128,1280]{1,0:T(8,128)(2,1)S(1)}, u32[]{:S(2)}, u32[]{:S(2)}) %collective-permute-start.10) | collective-permute-done | bytes 327712 | tf_op jit(solution)/shard_map/ppermute | solution.py:87
  46.8 2.5 collective-permute-start.12
  49.3 13.7 %collective-permute-done.12.refs_13_.refs_21_ = bf16[128,1280]{1,0:T(8,128)(2,1)S(1)} collective-permute-done((bf16[128,1280]{1,0:T(8,128)(2,1)S(1)}, bf16[128,1280]{1,0:T(8,128)(2,1)S(1)}, u32[]{:S(2)}, u32[]{:S(2)}) %collective-permute-start.12) | collective-permute-done | bytes 327712 | tf_op jit(solution)/shard_map/ppermute | solution.py:87
  64.1 4.9 %collective-permute-done.16.refs_18_.refs_0_ = bf16[128,2304]{1,0:T(8,128)(2,1)S(1)} collective-permute-done((bf16[128,2304]{1,0:T(8,128)(2,1)S(1)}, bf16[128,2304]{1,0:T(8,128)(2,1)S(1)}, u32[]{:S(2)}, u32[]{:S(2)}) %collective-permute-start.16) | collective-permute-done | bytes 589856 | tf_op jit(solution)/shard_map/ppermute | solution.py:87
  69.3 3.9 %project.1 = (f32[4,256,256]{2,1,0:T(8,128)S(1)}, f32[4,256,256]{2,1,0:T(8,128)S(1)}, f32[4,256,256]{2,1,0:T(8,128)S(1)}, bf16[4,256,256]{2,1,0:T(8,128)(2,1)S(1...) custom-call(s32[2]{0:T(128)S(1)} %copy-done.4, ...), custom_call_target="tpu_custom_call" | custom-call | flops 2147483648 | bytes 13238272 | tf_op jit(solution)/shard_map/project/pallas_call | solution.py:51
  75.2 5.0 %collective-permute-done.21.refs_8_.refs_0_ = bf16[256,1024]{1,0:T(8,128)(2,1)S(1)} collective-permute-done((bf16[256,1024]{1,0:T(8,128)(2,1)S(1)}, bf16[256,1024]{1,0:T(8,128)(2,1)S(1)}, u32[]{:S(2)}, u32[]{:S(2)}) %collective-permute-start.21) | collective-permute-done | bytes 524320 | tf_op jit(solution)/shard_map/ppermute | solution.py:87
  80.3 3.2 %collective-permute-start.19 = (f32[2,128,128]{2,1,0:T(8,128)S(1)}, f32[2,128,128]{2,1,0:T(8,128)S(1)}, u32[]{:S(2)}, u32[]{:S(2)}) collective-permute-start(f32[2,128,128]{2,1,0:T(8,128)S(1)} %get-tuple-element.134), channel_id=1, source_target_pairs={{0,4},{1,5},{2,6},{3,7},{8,12},{9,13},{10,14},{11,15},{16,20},{17,... | collective-permute-start | bytes 393224 | tf_op jit(solution)/shard_map/ppermute | solution.py:101
  84.6 3.6 %collective-permute-done.19.refs_3_ = f32[2,128,128]{2,1,0:T(8,128)S(1)} collective-permute-done((f32[2,128,128]{2,1,0:T(8,128)S(1)}, f32[2,128,128]{2,1,0:T(8,128)S(1)}, u32[]{:S(2)}, u32[]{:S(2)}) %collective-permute-start.19) | collective-permute-done | bytes 131104 | tf_op jit(solution)/shard_map/ppermute | solution.py:101
  89.3 2.1 collective-permute-done.25.refs_0_
  93.5 4.8 %collective-permute-done.23.refs_4_ = bf16[256,256]{1,0:T(8,128)(2,1)S(1)} collective-permute-done((bf16[256,256]{1,0:T(8,128)(2,1)S(1)}, bf16[256,256]{1,0:T(8,128)(2,1)S(1)}, u32[]{:S(2)}, u32[]{:S(2)}) %collective-permute-start.23) | collective-permute-done | bytes 131104 | tf_op jit(solution)/shard_map/ppermute | solution.py:87
  99.2 1.7 mid.1
  103.5 12.1 %collective-permute-done.33.refs_0_.refs_2_ = bf16[256,1024]{1,0:T(8,128)(2,1)S(1)} collective-permute-done((bf16[256,1024]{1,0:T(8,128)(2,1)S(1)}, bf16[256,1024]{1,0:T(8,128)(2,1)S(1)}, u32[]{:S(2)}, u32[]{:S(2)}) %collective-permute-start.33) | collective-permute-done | bytes 524320 | tf_op jit(solution)/shard_map/ppermute | solution.py:87
  115.6 2.3 collective-permute-done.31.refs_10_
  118.2 5.1 %ffn2.1 = (bf16[256,768]{1,0:T(8,128)(2,1)S(1)}, bf16[256,768]{1,0:T(8,128)(2,1)S(1)}, bf16[256,768]{1,0:T(8,128)(2,1)S(1)}, f32[256,1024]{1,0:T(8,128)S(1)}, bf...) custom-call(bf16[256,1024]{1,0:T(8,128)(2,1)S(1)} %collective-permut, ...), custom_call_target="tpu_custom_call" | custom-call | tf_op jit(solution)/shard_map/ffn2/pallas_call | solution.py:51
  126.7 5.1 %ffn0.1 = (bf16[256,768]{1,0:T(8,128)(2,1)S(1)}, bf16[256,768]{1,0:T(8,128)(2,1)S(1)}, bf16[256,768]{1,0:T(8,128)(2,1)S(1)}, f32[256,1024]{1,0:T(8,128)S(1)}, bf...) custom-call(bf16[256,1024]{1,0:T(8,128)(2,1)S(1)} %get-tuple-element, ...), custom_call_target="tpu_custom_call" | custom-call | tf_op jit(solution)/shard_map/ffn0/pallas_call | solution.py:51
  132.0 17.5 %hidden_grad.1 = (bf16[2,128,1536]{2,1,0:T(8,128)(2,1)S(1)}, bf16[128,1536]{1,0:T(8,128)(2,1)S(1)}, bf16[128,1536]{1,0:T(8,128)(2,1)S(1)}, bf16[2,128,1536]{2,1,...) custom-call(bf16[256,1024]{1,0:T(8,128)(2,1)S(1)} %get-tuple-element.149.refs_0_, ...), custom_call_target="tpu_custom_call" | custom-call | tf_op jit(solution)/shard_map/hidden_grad/pallas_call | solution.py:51
  150.3 1.3 collective-permute-start.45
  151.6 2.3 mid_back.1
  159.2 1.8 ffn_out.1
  163.4 1.8 back_state.1
  165.3 4.1 %collective-permute-done.44.refs_1_ = bf16[2,128,1536]{2,1,0:T(8,128)(2,1)S(1)} collective-permute-done((bf16[2,128,1536]{2,1,0:T(8,128)(2,1)S(1)}, bf16[2,128,1536]{2,1,0:T(8,128)(2,1)S(1)}, u32[]{:S(2)}, u32[]{:S(2)}) %collective-permute-start.44) | collective-permute-done | bytes 786464 | tf_op jit(solution)/shard_map/ppermute | solution.py:87
  169.5 1.6 collective-permute-start.46
  173.0 2.8 %back_local.1 = (bf16[4,256,256]{2,1,0:T(8,128)(2,1)S(1)}, f32[4,256,256]{2,1,0:T(8,128)S(1)}, f32[4,256,256]{2,1,0:T(8,128)S(1)}) custom-call(bf16[4,256,256]{2,1,0:T(8,128)(2,1)S(1)} %get-tuple-element.180.refs_0_, bf16[4,256,256]{2,1,0:T(8,128)(2,1)S(1)} %get-tuple-element.138.refs_2_.refs_1_.refs_4_, ...), custom_call_target="tpu_custom_call" | custom-call | flops 671088640 | bytes 8912896 | tf_op jit(solution)/shard_map/back_local/pallas_call | solution.py:51
  175.8 3.0 %down_side.1 = (bf16[2,128,1280]{2,1,0:T(8,128)(2,1)S(1)}, bf16[128,1280]{1,0:T(8,128)(2,1)S(1)}, bf16[128,1280]{1,0:T(8,128)(2,1)S(1)}, bf16[2,128,1280]{2,1,0:...) custom-call(bf16[256,1024]{1,0:T(8,128)(2,1)S(1)} %tie.10.refs_2_.refs_0_, ...), custom_call_target="tpu_custom_call" | custom-call | flops 2147483648 | bytes 9437184 | tf_op jit(solution)/shard_map/down_side/pallas_call | solution.py:51
  180.1 1.4 collective-permute-done.47.refs_5_
  181.8 1.8 collective-permute-done.43.refs_3_
  183.6 4.0 %back_final.1 = (bf16[4,256,1024]{2,1,0:T(8,128)(2,1)S(1)}, f32[2,256,1024]{2,1,0:T(8,128)S(1)}, bf16[2,256,1024]{2,1,0:T(8,128)(2,1)S(1)}, f32[2,256,1024]{2,1,0:T(8,128)S(1)}, bf16[2,256,1024]{2,1,0:T(8,128)(2,1)S(1)}) custom-call(s32[2]{0:T(128)S(1)} %copy-done.4, ...), custom_call_target="tpu_custom_call", output_to_operand_aliasing={{1}: (22, {}), {2}: (23, {}), {3}: (24, {}), {4}: (25, {})} | custom-call | flops 2147483648 | bytes 24510464 | tf_op jit(solution)/shard_map/back_final/pallas_call | solution.py:51
  188.2 1.5 collective-permute-start.58
  190.3 3.4 %collective-permute-start.59 = (bf16[128,1536]{1,0:T(8,128)(2,1)S(1)}, bf16[128,1536]{1,0:T(8,128)(2,1)S(1)}, u32[]{:S(2)}, u32[]{:S(2)}) collective-permute-start(bf16[128,1536]{1,0:T(8,128)(2,1)S(1)} %get-tuple-element.216), channel_id=1, source_target_pairs={{0,4},{1,5},{2,6},{3,7},{4,0},{5,1},{6,2},{7,3},{8,12},{9,13},{10,... | collective-permute-start | bytes 1179656 | tf_op jit(solution)/shard_map/ppermute | solution.py:87
  194.8 1.6 attn_grad.1
  197.0 8.3 %collective-permute-done.58.refs_1_ = bf16[2,128,1280]{2,1,0:T(8,128)(2,1)S(1)} collective-permute-done((bf16[2,128,1280]{2,1,0:T(8,128)(2,1)S(1)}, bf16[2,128,1280]{2,1,0:T(8,128)(2,1)S(1)}, u32[]{:S(2)}, u32[]{:S(2)}) %collective-permute-start.58) | collective-permute-done | bytes 655392 | tf_op jit(solution)/shard_map/ppermute | solution.py:87
  205.3 1.5 collective-permute-start.53
  206.8 4.8 %collective-permute-done.59.refs_3_.refs_2_ = bf16[128,1536]{1,0:T(8,128)(2,1)S(1)} collective-permute-done((bf16[128,1536]{1,0:T(8,128)(2,1)S(1)}, bf16[128,1536]{1,0:T(8,128)(2,1)S(1)}, u32[]{:S(2)}, u32[]{:S(2)}) %collective-permute-start.59) | collective-permute-done | bytes 393248 | tf_op jit(solution)/shard_map/ppermute | solution.py:87
  213.7 2.1 collective-permute-done.55.refs_1_.refs_4_
  216.0 1.4 collective-permute-done.53.refs_1_
  218.1 4.7 %collective-permute-done.60.refs_2_ = bf16[128,1280]{1,0:T(8,128)(2,1)S(1)} collective-permute-done((bf16[128,1280]{1,0:T(8,128)(2,1)S(1)}, bf16[128,1280]{1,0:T(8,128)(2,1)S(1)}, u32[]{:S(2)}, u32[]{:S(2)}) %collective-permute-start.60) | collective-permute-done | bytes 327712 | tf_op jit(solution)/shard_map/ppermute | solution.py:87
  222.8 1.6 collective-permute-done.62.refs_5_
  224.6 3.4 %collective-permute-start.63 = (bf16[128,1280]{1,0:T(8,128)(2,1)S(1)}, bf16[128,1280]{1,0:T(8,128)(2,1)S(1)}, u32[]{:S(2)}, u32[]{:S(2)}) collective-permute-start(bf16[128,1280]{1,0:T(8,128)(2,1)S(1)} %get-tuple-element.221), channel_id=1, source_target_pairs={{0,4},{1,5},{2,6},{3,7},{4,0},{5,1},{6,2},{7,3},{8,12},{9,13},{10,... | collective-permute-start | bytes 983048 | tf_op jit(solution)/shard_map/ppermute | solution.py:87
  228.9 1.9 collective-permute-start.57
  231.7 8.3 %collective-permute-done.65.refs_3_ = bf16[32,1536]{1,0:T(8,128)(2,1)S(1)} collective-permute-done((bf16[32,1536]{1,0:T(8,128)(2,1)S(1)}, bf16[32,1536]{1,0:T(8,128)(2,1)S(1)}, u32[]{:S(2)}, u32[]{:S(2)}) %collective-permute-start.65) | collective-permute-done | bytes 98336 | tf_op jit(solution)/shard_map/ppermute | solution.py:87
  241.1 1.5 final_hidden.1
  242.6 1.8 mixed.1.refs_6_
  245.0 3.8 %collective-permute-done.57.refs_2_ = bf16[128,768]{1,0:T(8,128)(2,1)S(1)} collective-permute-done((bf16[128,768]{1,0:T(8,128)(2,1)S(1)}, bf16[128,768]{1,0:T(8,128)(2,1)S(1)}, u32[]{:S(2)}, u32[]{:S(2)}) %collective-permute-start.57) | collective-permute-done | bytes 196640 | tf_op jit(solution)/shard_map/ppermute | solution.py:87
  250.7 1.7 collective-permute-start.69
  252.4 2.3 first_back.1
  254.7 2.2 collective-permute-done.68.refs_3_
  256.9 1.9 collective-permute-done.69.refs_4_
  258.8 1.6 final_rest.1
  (157 shorter events, 42.7 us)
Async XLA Ops:
  4.5 8.7 %collective-permute-start = (bf16[32,1280]{1,0:T(8,128)(2,1)}, bf16[32,1280]{1,0:T(8,128)(2,1)S(1)}, u32[]{:S(2)}, u32[]{:S(2)}) collective-permute-start(bf16[32,1280]{1,0:T(8,128)(2,1)} %get-tuple-element.126), channel_id=1, source_target_pairs={{0,1},{1,0},{2,3},{3,2},{4,5},{5,4},{6,7},{7,6},{8,9},{9,8},{10,11... | collective-permute-start | bytes 245768 | tf_op jit(solution)/shard_map/ppermute | solution.py:87
  5.0 8.3 %collective-permute-start.1 = (bf16[32,1280]{1,0:T(8,128)(2,1)}, bf16[32,1280]{1,0:T(8,128)(2,1)S(1)}, u32[]{:S(2)}, u32[]{:S(2)}) collective-permute-start(bf16[32,1280]{1,0:T(8,128)(2,1)} %get-tuple-element.127), channel_id=1, source_target_pairs={{0,2},{1,3},{2,0},{3,1},{4,6},{5,7},{6,4},{7,5},{8,10},{9,11},{10,... | collective-permute-start | bytes 245768 | tf_op jit(solution)/shard_map/ppermute | solution.py:87
  7.6 5.6 %collective-permute-start.2 = (bf16[32,1280]{1,0:T(8,128)(2,1)}, bf16[32,1280]{1,0:T(8,128)(2,1)S(1)}, u32[]{:S(2)}, u32[]{:S(2)}) collective-permute-start(bf16[32,1280]{1,0:T(8,128)(2,1)} %get-tuple-element.128), channel_id=1, source_target_pairs={{0,3},{1,2},{2,1},{3,0},{4,7},{5,6},{6,5},{7,4},{8,11},{9,10},{10,... | collective-permute-start | bytes 245768 | tf_op jit(solution)/shard_map/ppermute | solution.py:87
  7.7 9.9 %collective-permute-start.13 = (bf16[32,2304]{1,0:T(8,128)(2,1)}, bf16[32,2304]{1,0:T(8,128)(2,1)S(1)}, u32[]{:S(2)}, u32[]{:S(2)}) collective-permute-start(bf16[32,2304]{1,0:T(8,128)(2,1)} %get-tuple-element.130), channel_id=1, source_target_pairs={{0,1},{1,0},{2,3},{3,2},{4,5},{5,4},{6,7},{7,6},{8,9},{9,8},{10,11... | collective-permute-start | bytes 442376 | tf_op jit(solution)/shard_map/ppermute | solution.py:87
  7.8 11.2 %collective-permute-start.14 = (bf16[32,2304]{1,0:T(8,128)(2,1)}, bf16[32,2304]{1,0:T(8,128)(2,1)S(1)}, u32[]{:S(2)}, u32[]{:S(2)}) collective-permute-start(bf16[32,2304]{1,0:T(8,128)(2,1)} %get-tuple-element.131), channel_id=1, source_target_pairs={{0,2},{1,3},{2,0},{3,1},{4,6},{5,7},{6,4},{7,5},{8,10},{9,11},{10,... | collective-permute-start | bytes 442376 | tf_op jit(solution)/shard_map/ppermute | solution.py:87
  13.2 8.9 %collective-permute-start.15 = (bf16[32,2304]{1,0:T(8,128)(2,1)S(1)}, bf16[32,2304]{1,0:T(8,128)(2,1)S(1)}, u32[]{:S(2)}, u32[]{:S(2)}) collective-permute-start(bf16[32,2304]{1,0:T(8,128)(2,1)S(1)} %copy-done.7), channel_id=1, source_target_pairs={{0,3},{1,2},{2,1},{3,0},{4,7},{5,6},{6,5},{7,4},{8,11},{9,10},{10,... | collective-permute-start | bytes 442376 | tf_op jit(solution)/shard_map/ppermute | solution.py:87
  13.4 10.2 %collective-permute-start.7 = (bf16[128,1280]{1,0:T(8,128)(2,1)S(1)}, bf16[128,1280]{1,0:T(8,128)(2,1)S(1)}, u32[]{:S(2)}, u32[]{:S(2)}) collective-permute-start(bf16[128,1280]{1,0:T(8,128)(2,1)S(1)} %maximum_select_fusion.3.refs_1_.refs_6_.refs_14_), channel_id=1, source_target_pairs={{0,8},{1,9},{2,10},{3,11},{4,12},{5,13},{6,14},{7,15},{8,0},{9,1},... | collective-permute-start | bytes 983048 | tf_op jit(solution)/shard_map/ppermute | solution.py:87
  15.0 17.9 %collective-permute-start.6 = (bf16[128,1280]{1,0:T(8,128)(2,1)S(1)}, bf16[128,1280]{1,0:T(8,128)(2,1)S(1)}, u32[]{:S(2)}, u32[]{:S(2)}) collective-permute-start(bf16[128,1280]{1,0:T(8,128)(2,1)S(1)} %maximum_select_fusion.3.refs_1_.refs_6_.refs_14_), channel_id=1, source_target_pairs={{0,4},{1,5},{2,6},{3,7},{4,0},{5,1},{6,2},{7,3},{8,12},{9,13},{10,... | collective-permute-start | bytes 983048 | tf_op jit(solution)/shard_map/ppermute | solution.py:87
  17.5 20.1 %collective-permute-start.4 = (bf16[256,1024]{1,0:T(8,128)(2,1)S(1)}, bf16[256,1024]{1,0:T(8,128)(2,1)S(1)}, u32[]{:S(2)}, u32[]{:S(2)}) collective-permute-start(bf16[256,1024]{1,0:T(8,128)(2,1)S(1)} %tie.8.refs_2_.refs_4_.refs_0_), channel_id=1, source_target_pairs={{0,2},{1,3},{2,0},{3,1},{4,6},{5,7},{6,4},{7,5},{8,10},{9,11},{10,... | collective-permute-start | bytes 1572872 | tf_op jit(solution)/shard_map/ppermute | solution.py:87
  19.0 20.1 %collective-permute-start.3 = (bf16[256,1024]{1,0:T(8,128)(2,1)S(1)}, bf16[256,1024]{1,0:T(8,128)(2,1)S(1)}, u32[]{:S(2)}, u32[]{:S(2)}) collective-permute-start(bf16[256,1024]{1,0:T(8,128)(2,1)S(1)} %tie.8.refs_2_.refs_4_.refs_0_), channel_id=1, source_target_pairs={{0,1},{1,0},{2,3},{3,2},{4,5},{5,4},{6,7},{7,6},{8,9},{9,8},{10,11... | collective-permute-start | bytes 1572872 | tf_op jit(solution)/shard_map/ppermute | solution.py:87
  22.1 12.5 %collective-permute-start.9 = (bf16[128,1280]{1,0:T(8,128)(2,1)S(1)}, bf16[128,1280]{1,0:T(8,128)(2,1)S(1)}, u32[]{:S(2)}, u32[]{:S(2)}) collective-permute-start(bf16[128,1280]{1,0:T(8,128)(2,1)S(1)} %maximum_select_fusion.3.refs_1_.refs_6_.refs_14_), channel_id=1, source_target_pairs={{0,16},{1,17},{2,18},{3,19},{4,20},{5,21},{6,22},{7,23},{8,24},{9,... | collective-permute-start | bytes 983048 | tf_op jit(solution)/shard_map/ppermute | solution.py:87
  23.6 17.1 %collective-permute-start.11 = (bf16[128,1280]{1,0:T(8,128)(2,1)S(1)}, bf16[128,1280]{1,0:T(8,128)(2,1)S(1)}, u32[]{:S(2)}, u32[]{:S(2)}) collective-permute-start(bf16[128,1280]{1,0:T(8,128)(2,1)S(1)} %collective-permute-done.7.refs_1_.refs_8_.refs_16_), channel_id=1, source_target_pairs={{0,16},{1,17},{2,18},{3,19},{4,20},{5,21},{6,22},{7,23},{8,24},{9,... | collective-permute-start | bytes 983048 | tf_op jit(solution)/shard_map/ppermute | solution.py:87
  32.9 13.8 %collective-permute-start.10 = (bf16[128,1280]{1,0:T(8,128)(2,1)S(1)}, bf16[128,1280]{1,0:T(8,128)(2,1)S(1)}, u32[]{:S(2)}, u32[]{:S(2)}) collective-permute-start(bf16[128,1280]{1,0:T(8,128)(2,1)S(1)} %collective-permute-done.6.refs_3_.refs_7_.refs_15_), channel_id=1, source_target_pairs={{0,16},{1,17},{2,18},{3,19},{4,20},{5,21},{6,22},{7,23},{8,24},{9,... | collective-permute-start | bytes 983048 | tf_op jit(solution)/shard_map/ppermute | solution.py:87
  34.6 12.1 %collective-permute-start.8 = (bf16[128,1280]{1,0:T(8,128)(2,1)S(1)}, bf16[128,1280]{1,0:T(8,128)(2,1)S(1)}, u32[]{:S(2)}, u32[]{:S(2)}) collective-permute-start(bf16[128,1280]{1,0:T(8,128)(2,1)S(1)} %collective-permute-done.6.refs_3_.refs_7_.refs_15_), channel_id=1, source_target_pairs={{0,8},{1,9},{2,10},{3,11},{4,12},{5,13},{6,14},{7,15},{8,0},{9,1},... | collective-permute-start | bytes 983048 | tf_op jit(solution)/shard_map/ppermute | solution.py:87
  37.7 26.5 %collective-permute-start.18 = (bf16[128,2304]{1,0:T(8,128)(2,1)S(1)}, bf16[128,2304]{1,0:T(8,128)(2,1)S(1)}, u32[]{:S(2)}, u32[]{:S(2)}) collective-permute-start(bf16[128,2304]{1,0:T(8,128)(2,1)S(1)} %tie.9.refs_4_), channel_id=1, source_target_pairs={{0,16},{1,17},{2,18},{3,19},{4,20},{5,21},{6,22},{7,23},{8,24},{9,... | collective-permute-start | bytes 1769480 | tf_op jit(solution)/shard_map/ppermute | solution.py:87
  39.2 25.0 %collective-permute-start.17 = (bf16[128,2304]{1,0:T(8,128)(2,1)S(1)}, bf16[128,2304]{1,0:T(8,128)(2,1)S(1)}, u32[]{:S(2)}, u32[]{:S(2)}) collective-permute-start(bf16[128,2304]{1,0:T(8,128)(2,1)S(1)} %tie.9.refs_4_), channel_id=1, source_target_pairs={{0,8},{1,9},{2,10},{3,11},{4,12},{5,13},{6,14},{7,15},{8,0},{9,1},... | collective-permute-start | bytes 1769480 | tf_op jit(solution)/shard_map/ppermute | solution.py:87
  40.7 28.4 %collective-permute-start.16 = (bf16[128,2304]{1,0:T(8,128)(2,1)S(1)}, bf16[128,2304]{1,0:T(8,128)(2,1)S(1)}, u32[]{:S(2)}, u32[]{:S(2)}) collective-permute-start(bf16[128,2304]{1,0:T(8,128)(2,1)S(1)} %tie.9.refs_4_), channel_id=1, source_target_pairs={{0,4},{1,5},{2,6},{3,7},{4,0},{5,1},{6,2},{7,3},{8,12},{9,13},{10,... | collective-permute-start | bytes 1769480 | tf_op jit(solution)/shard_map/ppermute | solution.py:87
  46.7 17.5 %collective-permute-start.5 = (bf16[256,1024]{1,0:T(8,128)(2,1)S(1)}, bf16[256,1024]{1,0:T(8,128)(2,1)S(1)}, u32[]{:S(2)}, u32[]{:S(2)}) collective-permute-start(bf16[256,1024]{1,0:T(8,128)(2,1)S(1)} %collective-permute-done.4.refs_4_.refs_6_.refs_2_), channel_id=1, source_target_pairs={{0,1},{1,0},{2,3},{3,2},{4,5},{5,4},{6,7},{7,6},{8,9},{9,8},{10,11... | collective-permute-start | bytes 1572872 | tf_op jit(solution)/shard_map/ppermute | solution.py:87
  46.8 16.3 %collective-permute-start.12 = (bf16[128,1280]{1,0:T(8,128)(2,1)S(1)}, bf16[128,1280]{1,0:T(8,128)(2,1)S(1)}, u32[]{:S(2)}, u32[]{:S(2)}) collective-permute-start(bf16[128,1280]{1,0:T(8,128)(2,1)S(1)} %collective-permute-done.10.refs_11_.refs_2_.refs_19_), channel_id=1, source_target_pairs={{0,8},{1,9},{2,10},{3,11},{4,12},{5,13},{6,14},{7,15},{8,0},{9,1},... | collective-permute-start | bytes 983048 | tf_op jit(solution)/shard_map/ppermute | solution.py:87
  63.1 17.2 %collective-permute-start.21 = (bf16[256,1024]{1,0:T(8,128)(2,1)S(1)}, bf16[256,1024]{1,0:T(8,128)(2,1)S(1)}, u32[]{:S(2)}, u32[]{:S(2)}) collective-permute-start(bf16[256,1024]{1,0:T(8,128)(2,1)S(1)} %tie.10.refs_2_.refs_0_), channel_id=1, source_target_pairs={{0,2},{1,3},{2,0},{3,1},{4,6},{5,7},{6,4},{7,5},{8,10},{9,11},{10,... | collective-permute-start | bytes 1572872 | tf_op jit(solution)/shard_map/ppermute | solution.py:87
  73.2 18.2 %collective-permute-start.25 = (bf16[1024,256]{1,0:T(8,128)(2,1)S(1)}, bf16[1024,256]{1,0:T(8,128)(2,1)S(1)}, u32[]{:S(2)}, u32[]{:S(2)}) collective-permute-start(bf16[1024,256]{1,0:T(8,128)(2,1)S(1)} %get-tuple-element.141.refs_6_), channel_id=1, source_target_pairs={{0,2},{1,3},{2,0},{3,1},{4,6},{5,7},{6,4},{7,5},{8,10},{9,11},{10,... | collective-permute-start | bytes 1572872 | tf_op jit(solution)/shard_map/ppermute | solution.py:87
  73.3 14.8 %collective-permute-start.20 = (bf16[1024,256]{1,0:T(8,128)(2,1)S(1)}, bf16[1024,256]{1,0:T(8,128)(2,1)S(1)}, u32[]{:S(2)}, u32[]{:S(2)}) collective-permute-start(bf16[1024,256]{1,0:T(8,128)(2,1)S(1)} %get-tuple-element.141.refs_6_), channel_id=1, source_target_pairs={{0,1},{1,0},{2,3},{3,2},{4,5},{5,4},{6,7},{7,6},{8,9},{9,8},{10,11... | collective-permute-start | bytes 1572872 | tf_op jit(solution)/shard_map/ppermute | solution.py:87
  73.6 19.5 %collective-permute-start.28 = (bf16[128,2304]{1,0:T(8,128)(2,1)S(1)}, bf16[128,2304]{1,0:T(8,128)(2,1)S(1)}, u32[]{:S(2)}, u32[]{:S(2)}) collective-permute-start(bf16[128,2304]{1,0:T(8,128)(2,1)S(1)} %tie.12.refs_5_), channel_id=1, source_target_pairs={{0,8},{1,9},{2,10},{3,11},{4,12},{5,13},{6,14},{7,15},{8,0},{9,1},... | collective-permute-start | bytes 1769480 | tf_op jit(solution)/shard_map/ppermute | solution.py:87
  74.4 18.9 %collective-permute-start.27 = (bf16[128,2304]{1,0:T(8,128)(2,1)S(1)}, bf16[128,2304]{1,0:T(8,128)(2,1)S(1)}, u32[]{:S(2)}, u32[]{:S(2)}) collective-permute-start(bf16[128,2304]{1,0:T(8,128)(2,1)S(1)} %tie.12.refs_5_), channel_id=1, source_target_pairs={{0,16},{1,17},{2,18},{3,19},{4,20},{5,21},{6,22},{7,23},{8,24},{9,... | collective-permute-start | bytes 1769480 | tf_op jit(solution)/shard_map/ppermute | solution.py:87
  80.3 7.9 %collective-permute-start.19 = (f32[2,128,128]{2,1,0:T(8,128)S(1)}, f32[2,128,128]{2,1,0:T(8,128)S(1)}, u32[]{:S(2)}, u32[]{:S(2)}) collective-permute-start(f32[2,128,128]{2,1,0:T(8,128)S(1)} %get-tuple-element.134), channel_id=1, source_target_pairs={{0,4},{1,5},{2,6},{3,7},{8,12},{9,13},{10,14},{11,15},{16,20},{17,... | collective-permute-start | bytes 393224 | tf_op jit(solution)/shard_map/ppermute | solution.py:101
  91.4 7.8 %collective-permute-start.26 = (bf16[1024,256]{1,0:T(8,128)(2,1)S(1)}, bf16[1024,256]{1,0:T(8,128)(2,1)S(1)}, u32[]{:S(2)}, u32[]{:S(2)}) collective-permute-start(bf16[1024,256]{1,0:T(8,128)(2,1)S(1)} %tie.11.refs_8_), channel_id=1, source_target_pairs={{0,1},{1,0},{2,3},{3,2},{4,5},{5,4},{6,7},{7,6},{8,9},{9,8},{10,11... | collective-permute-start | bytes 1572872 | tf_op jit(solution)/shard_map/ppermute | solution.py:87
  91.9 6.4 %collective-permute-start.23 = (bf16[256,256]{1,0:T(8,128)(2,1)S(1)}, bf16[256,256]{1,0:T(8,128)(2,1)S(1)}, u32[]{:S(2)}, u32[]{:S(2)}) collective-permute-start(bf16[256,256]{1,0:T(8,128)(2,1)S(1)} %get-tuple-element.145), channel_id=1, source_target_pairs={{0,2},{1,3},{2,0},{3,1},{4,6},{5,7},{6,4},{7,5},{8,10},{9,11},{10,... | collective-permute-start | bytes 393224 | tf_op jit(solution)/shard_map/ppermute | solution.py:87
  93.1 6.1 %collective-permute-start.24 = (bf16[256,256]{1,0:T(8,128)(2,1)S(1)}, bf16[256,256]{1,0:T(8,128)(2,1)S(1)}, u32[]{:S(2)}, u32[]{:S(2)}) collective-permute-start(bf16[256,256]{1,0:T(8,128)(2,1)S(1)} %get-tuple-element.146), channel_id=1, source_target_pairs={{0,3},{1,2},{2,1},{3,0},{4,7},{5,6},{6,5},{7,4},{8,11},{9,10},{10,... | collective-permute-start | bytes 393224 | tf_op jit(solution)/shard_map/ppermute | solution.py:87
  100.9 14.6 %collective-permute-start.33 = (bf16[256,1024]{1,0:T(8,128)(2,1)S(1)}, bf16[256,1024]{1,0:T(8,128)(2,1)S(1)}, u32[]{:S(2)}, u32[]{:S(2)}) collective-permute-start(bf16[256,1024]{1,0:T(8,128)(2,1)S(1)} %get-tuple-element.149.refs_0_), channel_id=1, source_target_pairs={{0,2},{1,3},{2,0},{3,1},{4,6},{5,7},{6,4},{7,5},{8,10},{9,11},{10,... | collective-permute-start | bytes 1572872 | tf_op jit(solution)/shard_map/ppermute | solution.py:87
  102.3 15.7 %collective-permute-start.31 = (bf16[128,2304]{1,0:T(8,128)(2,1)S(1)}, bf16[128,2304]{1,0:T(8,128)(2,1)S(1)}, u32[]{:S(2)}, u32[]{:S(2)}) collective-permute-start(bf16[128,2304]{1,0:T(8,128)(2,1)S(1)} %tie.13.refs_6_), channel_id=1, source_target_pairs={{0,16},{1,17},{2,18},{3,19},{4,20},{5,21},{6,22},{7,23},{8,24},{9,... | collective-permute-start | bytes 1769480 | tf_op jit(solution)/shard_map/ppermute | solution.py:87
  102.8 15.4 %collective-permute-start.32 = (bf16[128,2304]{1,0:T(8,128)(2,1)S(1)}, bf16[128,2304]{1,0:T(8,128)(2,1)S(1)}, u32[]{:S(2)}, u32[]{:S(2)}) collective-permute-start(bf16[128,2304]{1,0:T(8,128)(2,1)S(1)} %tie.14.refs_9_), channel_id=1, source_target_pairs={{0,8},{1,9},{2,10},{3,11},{4,12},{5,13},{6,14},{7,15},{8,0},{9,1},... | collective-permute-start | bytes 1769480 | tf_op jit(solution)/shard_map/ppermute | solution.py:87
  103.5 12.1 %collective-permute-start.35 = (bf16[256,1024]{1,0:T(8,128)(2,1)S(1)}, bf16[256,1024]{1,0:T(8,128)(2,1)S(1)}, u32[]{:S(2)}, u32[]{:S(2)}) collective-permute-start(bf16[256,1024]{1,0:T(8,128)(2,1)S(1)} %tie.15.refs_2_), channel_id=1, source_target_pairs={{0,1},{1,0},{2,3},{3,2},{4,5},{5,4},{6,7},{7,6},{8,9},{9,8},{10,11... | collective-permute-start | bytes 1572872 | tf_op jit(solution)/shard_map/ppermute | solution.py:87
  123.3 2.9 %collective-permute-start.30 = (bf16[256,1024]{1,0:T(8,128)(2,1)S(1)}, bf16[256,1024]{1,0:T(8,128)(2,1)S(1)}, u32[]{:S(2)}, u32[]{:S(2)}) collective-permute-start(bf16[256,1024]{1,0:T(8,128)(2,1)S(1)} %tie.10.refs_2_.refs_0_), channel_id=1, source_target_pairs={{0,1},{1,0},{2,3},{3,2},{4,5},{5,4},{6,7},{7,6},{8,9},{9,8},{10,11... | collective-permute-start | bytes 1572872 | tf_op jit(solution)/shard_map/ppermute | solution.py:87
  123.8 2.9 %collective-permute-start.29 = (bf16[256,1024]{1,0:T(8,128)(2,1)S(1)}, bf16[256,1024]{1,0:T(8,128)(2,1)S(1)}, u32[]{:S(2)}, u32[]{:S(2)}) collective-permute-start(bf16[256,1024]{1,0:T(8,128)(2,1)S(1)} %get-tuple-element.149.refs_0_), channel_id=1, source_target_pairs={{0,1},{1,0},{2,3},{3,2},{4,5},{5,4},{6,7},{7,6},{8,9},{9,8},{10,11... | collective-permute-start | bytes 1572872 | tf_op jit(solution)/shard_map/ppermute | solution.py:87
  125.3 26.3 %collective-permute-start.38 = (bf16[256,1024]{1,0:T(8,128)(2,1)S(1)}, bf16[256,1024]{1,0:T(8,128)(2,1)S(1)}, u32[]{:S(2)}, u32[]{:S(2)}) collective-permute-start(bf16[256,1024]{1,0:T(8,128)(2,1)S(1)} %add.91.refs_12_), channel_id=1, source_target_pairs={{0,2},{1,3},{2,0},{3,1},{4,6},{5,7},{6,4},{7,5},{8,10},{9,11},{10,... | collective-permute-start | bytes 1572872 | tf_op jit(solution)/shard_map/ppermute | solution.py:87
  131.8 19.9 %collective-permute-start.37 = (bf16[256,1024]{1,0:T(8,128)(2,1)S(1)}, bf16[256,1024]{1,0:T(8,128)(2,1)S(1)}, u32[]{:S(2)}, u32[]{:S(2)}) collective-permute-start(bf16[256,1024]{1,0:T(8,128)(2,1)S(1)} %get-tuple-element.153), channel_id=1, source_target_pairs={{0,1},{1,0},{2,3},{3,2},{4,5},{5,4},{6,7},{7,6},{8,9},{9,8},{10,11... | collective-permute-start | bytes 1572872 | tf_op jit(solution)/shard_map/ppermute | solution.py:87
  149.5 19.9 %collective-permute-start.44 = (bf16[2,128,1536]{2,1,0:T(8,128)(2,1)S(1)}, bf16[2,128,1536]{2,1,0:T(8,128)(2,1)S(1)}, u32[]{:S(2)}, u32[]{:S(2)}) collective-permute-start(bf16[2,128,1536]{2,1,0:T(8,128)(2,1)S(1)} %get-tuple-element.162.refs_10_), channel_id=1, source_target_pairs={{0,8},{1,9},{2,10},{3,11},{4,12},{5,13},{6,14},{7,15},{8,0},{9,1},... | collective-permute-start | bytes 2359304 | tf_op jit(solution)/shard_map/ppermute | solution.py:87
  150.3 20.8 %collective-permute-start.45 = (bf16[2,128,1536]{2,1,0:T(8,128)(2,1)S(1)}, bf16[2,128,1536]{2,1,0:T(8,128)(2,1)S(1)}, u32[]{:S(2)}, u32[]{:S(2)}) collective-permute-start(bf16[2,128,1536]{2,1,0:T(8,128)(2,1)S(1)} %get-tuple-element.186), channel_id=1, source_target_pairs={{0,16},{1,17},{2,18},{3,19},{4,20},{5,21},{6,22},{7,23},{8,24},{9,... | collective-permute-start | bytes 2359304 | tf_op jit(solution)/shard_map/ppermute | solution.py:87
  155.8 6.4 %collective-permute-start.40 = (bf16[256,256]{1,0:T(8,128)(2,1)S(1)}, bf16[256,256]{1,0:T(8,128)(2,1)S(1)}, u32[]{:S(2)}, u32[]{:S(2)}) collective-permute-start(bf16[256,256]{1,0:T(8,128)(2,1)S(1)} %get-tuple-element.165), channel_id=1, source_target_pairs={{0,2},{1,3},{2,0},{3,1},{4,6},{5,7},{6,4},{7,5},{8,10},{9,11},{10,... | collective-permute-start | bytes 393224 | tf_op jit(solution)/shard_map/ppermute | solution.py:87
  157.2 6.3 %collective-permute-start.41 = (bf16[256,256]{1,0:T(8,128)(2,1)S(1)}, bf16[256,256]{1,0:T(8,128)(2,1)S(1)}, u32[]{:S(2)}, u32[]{:S(2)}) collective-permute-start(bf16[256,256]{1,0:T(8,128)(2,1)S(1)} %get-tuple-element.166), channel_id=1, source_target_pairs={{0,3},{1,2},{2,1},{3,0},{4,7},{5,6},{6,5},{7,4},{8,11},{9,10},{10,... | collective-permute-start | bytes 393224 | tf_op jit(solution)/shard_map/ppermute | solution.py:87
  158.1 25.5 %collective-permute-start.48 = (bf16[1024,256]{1,0:T(8,128)(2,1)S(1)}, bf16[1024,256]{1,0:T(8,128)(2,1)S(1)}, u32[]{:S(2)}, u32[]{:S(2)}) collective-permute-start(bf16[1024,256]{1,0:T(8,128)(2,1)S(1)} %add.92.refs_10_), channel_id=1, source_target_pairs={{0,2},{1,3},{2,0},{3,1},{4,6},{5,7},{6,4},{7,5},{8,10},{9,11},{10,... | collective-permute-start | bytes 1572872 | tf_op jit(solution)/shard_map/ppermute | solution.py:87
  169.5 10.6 %collective-permute-start.46 = (bf16[128,1536]{1,0:T(8,128)(2,1)S(1)}, bf16[128,1536]{1,0:T(8,128)(2,1)S(1)}, u32[]{:S(2)}, u32[]{:S(2)}) collective-permute-start(bf16[128,1536]{1,0:T(8,128)(2,1)S(1)} %next.6.refs_11_), channel_id=1, source_target_pairs={{0,16},{1,17},{2,18},{3,19},{4,20},{5,21},{6,22},{7,23},{8,24},{9,... | collective-permute-start | bytes 1179656 | tf_op jit(solution)/shard_map/ppermute | solution.py:87
  171.1 10.4 %collective-permute-start.47 = (bf16[128,1536]{1,0:T(8,128)(2,1)S(1)}, bf16[128,1536]{1,0:T(8,128)(2,1)S(1)}, u32[]{:S(2)}, u32[]{:S(2)}) collective-permute-start(bf16[128,1536]{1,0:T(8,128)(2,1)S(1)} %next.7.refs_12_), channel_id=1, source_target_pairs={{0,8},{1,9},{2,10},{3,11},{4,12},{5,13},{6,14},{7,15},{8,0},{9,1},... | collective-permute-start | bytes 1179656 | tf_op jit(solution)/shard_map/ppermute | solution.py:87
  171.8 11.8 %collective-permute-start.43 = (f32[2,128,128]{2,1,0:T(8,128)S(1)}, f32[2,128,128]{2,1,0:T(8,128)S(1)}, u32[]{:S(2)}, u32[]{:S(2)}) collective-permute-start(f32[2,128,128]{2,1,0:T(8,128)S(1)} %get-tuple-element.177), channel_id=1, source_target_pairs={{4,0},{5,1},{6,2},{7,3},{12,8},{13,9},{14,10},{15,11},{20,16},{21,... | collective-permute-start | bytes 393224 | tf_op jit(solution)/shard_map/ppermute | solution.py:101
  187.7 7.2 %collective-permute-start.49 = (bf16[2,256,1024]{2,1,0:T(8,128)(2,1)S(1)}, bf16[2,256,1024]{2,1,0:T(8,128)(2,1)S(1)}, u32[]{:S(2)}, u32[]{:S(2)}) collective-permute-start(bf16[2,256,1024]{2,1,0:T(8,128)(2,1)S(1)} %get-tuple-element.199), channel_id=1, source_target_pairs={{0,1},{1,0},{2,3},{3,2},{4,5},{5,4},{6,7},{7,6},{8,9},{9,8},{10,11... | collective-permute-start | bytes 3145736 | tf_op jit(solution)/shard_map/ppermute | solution.py:87
  188.2 5.7 %collective-permute-start.52 = (bf16[1024,256]{1,0:T(8,128)(2,1)S(1)}, bf16[1024,256]{1,0:T(8,128)(2,1)S(1)}, u32[]{:S(2)}, u32[]{:S(2)}) collective-permute-start(bf16[1024,256]{1,0:T(8,128)(2,1)S(1)} %get-tuple-element.205), channel_id=1, source_target_pairs={{0,1},{1,0},{2,3},{3,2},{4,5},{5,4},{6,7},{7,6},{8,9},{9,8},{10,11... | collective-permute-start | bytes 1572872 | tf_op jit(solution)/shard_map/ppermute | solution.py:87
  188.2 17.1 %collective-permute-start.58 = (bf16[2,128,1280]{2,1,0:T(8,128)(2,1)S(1)}, bf16[2,128,1280]{2,1,0:T(8,128)(2,1)S(1)}, u32[]{:S(2)}, u32[]{:S(2)}) collective-permute-start(bf16[2,128,1280]{2,1,0:T(8,128)(2,1)S(1)} %get-tuple-element.197.refs_27_), channel_id=1, source_target_pairs={{0,8},{1,9},{2,10},{3,11},{4,12},{5,13},{6,14},{7,15},{8,0},{9,1},... | collective-permute-start | bytes 1966088 | tf_op jit(solution)/shard_map/ppermute | solution.py:87
  189.7 22.6 %collective-permute-start.61 = (bf16[2,128,1280]{2,1,0:T(8,128)(2,1)S(1)}, bf16[2,128,1280]{2,1,0:T(8,128)(2,1)S(1)}, u32[]{:S(2)}, u32[]{:S(2)}) collective-permute-start(bf16[2,128,1280]{2,1,0:T(8,128)(2,1)S(1)} %get-tuple-element.218), channel_id=1, source_target_pairs={{0,16},{1,17},{2,18},{3,19},{4,20},{5,21},{6,22},{7,23},{8,24},{9,... | collective-permute-start | bytes 1966088 | tf_op jit(solution)/shard_map/ppermute | solution.py:87
  190.3 21.3 %collective-permute-start.59 = (bf16[128,1536]{1,0:T(8,128)(2,1)S(1)}, bf16[128,1536]{1,0:T(8,128)(2,1)S(1)}, u32[]{:S(2)}, u32[]{:S(2)}) collective-permute-start(bf16[128,1536]{1,0:T(8,128)(2,1)S(1)} %get-tuple-element.216), channel_id=1, source_target_pairs={{0,4},{1,5},{2,6},{3,7},{4,0},{5,1},{6,2},{7,3},{8,12},{9,13},{10,... | collective-permute-start | bytes 1179656 | tf_op jit(solution)/shard_map/ppermute | solution.py:87
  193.9 48.7 %collective-permute-start.51 = (bf16[2,256,1024]{2,1,0:T(8,128)(2,1)S(1)}, bf16[2,256,1024]{2,1,0:T(8,128)(2,1)S(1)}, u32[]{:S(2)}, u32[]{:S(2)}) collective-permute-start(bf16[2,256,1024]{2,1,0:T(8,128)(2,1)S(1)} %add.93), channel_id=1, source_target_pairs={{0,2},{1,3},{2,0},{3,1},{4,6},{5,7},{6,4},{7,5},{8,10},{9,11},{10,... | collective-permute-start | bytes 3145736 | tf_op jit(solution)/shard_map/ppermute | solution.py:87
  196.4 19.3 %collective-permute-start.55 = (bf16[2,128,768]{2,1,0:T(8,128)(2,1)S(1)}, bf16[2,128,768]{2,1,0:T(8,128)(2,1)S(1)}, u32[]{:S(2)}, u32[]{:S(2)}) collective-permute-start(bf16[2,128,768]{2,1,0:T(8,128)(2,1)S(1)} %get-tuple-element.210), channel_id=1, source_target_pairs={{0,16},{1,17},{2,18},{3,19},{4,20},{5,21},{6,22},{7,23},{8,24},{9,... | collective-permute-start | bytes 1179656 | tf_op jit(solution)/shard_map/ppermute | solution.py:87
  205.3 12.0 %collective-permute-start.53 = (bf16[2,128,768]{2,1,0:T(8,128)(2,1)S(1)}, bf16[2,128,768]{2,1,0:T(8,128)(2,1)S(1)}, u32[]{:S(2)}, u32[]{:S(2)}) collective-permute-start(bf16[2,128,768]{2,1,0:T(8,128)(2,1)S(1)} %get-tuple-element.207.refs_2_), channel_id=1, source_target_pairs={{0,8},{1,9},{2,10},{3,11},{4,12},{5,13},{6,14},{7,15},{8,0},{9,1},... | collective-permute-start | bytes 1179656 | tf_op jit(solution)/shard_map/ppermute | solution.py:87
  211.7 11.1 %collective-permute-start.60 = (bf16[128,1280]{1,0:T(8,128)(2,1)S(1)}, bf16[128,1280]{1,0:T(8,128)(2,1)S(1)}, u32[]{:S(2)}, u32[]{:S(2)}) collective-permute-start(bf16[128,1280]{1,0:T(8,128)(2,1)S(1)} %next.10), channel_id=1, source_target_pairs={{0,16},{1,17},{2,18},{3,19},{4,20},{5,21},{6,22},{7,23},{8,24},{9,... | collective-permute-start | bytes 983048 | tf_op jit(solution)/shard_map/ppermute | solution.py:87
  212.4 12.0 %collective-permute-start.62 = (bf16[128,1280]{1,0:T(8,128)(2,1)S(1)}, bf16[128,1280]{1,0:T(8,128)(2,1)S(1)}, u32[]{:S(2)}, u32[]{:S(2)}) collective-permute-start(bf16[128,1280]{1,0:T(8,128)(2,1)S(1)} %next.11), channel_id=1, source_target_pairs={{0,8},{1,9},{2,10},{3,11},{4,12},{5,13},{6,14},{7,15},{8,0},{9,1},... | collective-permute-start | bytes 983048 | tf_op jit(solution)/shard_map/ppermute | solution.py:87
  215.8 13.0 %collective-permute-start.56 = (bf16[128,768]{1,0:T(8,128)(2,1)S(1)}, bf16[128,768]{1,0:T(8,128)(2,1)S(1)}, u32[]{:S(2)}, u32[]{:S(2)}) collective-permute-start(bf16[128,768]{1,0:T(8,128)(2,1)S(1)} %next.9), channel_id=1, source_target_pairs={{0,8},{1,9},{2,10},{3,11},{4,12},{5,13},{6,14},{7,15},{8,0},{9,1},... | collective-permute-start | bytes 589832 | tf_op jit(solution)/shard_map/ppermute | solution.py:87
  217.4 11.4 %collective-permute-start.54 = (bf16[128,768]{1,0:T(8,128)(2,1)S(1)}, bf16[128,768]{1,0:T(8,128)(2,1)S(1)}, u32[]{:S(2)}, u32[]{:S(2)}) collective-permute-start(bf16[128,768]{1,0:T(8,128)(2,1)S(1)} %next.8), channel_id=1, source_target_pairs={{0,16},{1,17},{2,18},{3,19},{4,20},{5,21},{6,22},{7,23},{8,24},{9,... | collective-permute-start | bytes 589832 | tf_op jit(solution)/shard_map/ppermute | solution.py:87
  224.6 20.4 %collective-permute-start.63 = (bf16[128,1280]{1,0:T(8,128)(2,1)S(1)}, bf16[128,1280]{1,0:T(8,128)(2,1)S(1)}, u32[]{:S(2)}, u32[]{:S(2)}) collective-permute-start(bf16[128,1280]{1,0:T(8,128)(2,1)S(1)} %get-tuple-element.221), channel_id=1, source_target_pairs={{0,4},{1,5},{2,6},{3,7},{4,0},{5,1},{6,2},{7,3},{8,12},{9,13},{10,... | collective-permute-start | bytes 983048 | tf_op jit(solution)/shard_map/ppermute | solution.py:87
  228.7 3.0 %collective-permute-start.64 = (bf16[32,1536]{1,0:T(8,128)(2,1)S(1)}, bf16[32,1536]{1,0:T(8,128)(2,1)S(1)}, u32[]{:S(2)}, u32[]{:S(2)}) collective-permute-start(bf16[32,1536]{1,0:T(8,128)(2,1)S(1)} %get-tuple-element.223), channel_id=1, source_target_pairs={{0,1},{1,0},{2,3},{3,2},{4,5},{5,4},{6,7},{7,6},{8,9},{9,8},{10,11... | collective-permute-start | bytes 294920 | tf_op jit(solution)/shard_map/ppermute | solution.py:87
  228.9 19.8 %collective-permute-start.57 = (bf16[128,768]{1,0:T(8,128)(2,1)S(1)}, bf16[128,768]{1,0:T(8,128)(2,1)S(1)}, u32[]{:S(2)}, u32[]{:S(2)}) collective-permute-start(bf16[128,768]{1,0:T(8,128)(2,1)S(1)} %get-tuple-element.213), channel_id=1, source_target_pairs={{0,4},{1,5},{2,6},{3,7},{4,0},{5,1},{6,2},{7,3},{8,12},{9,13},{10,... | collective-permute-start | bytes 589832 | tf_op jit(solution)/shard_map/ppermute | solution.py:87
  230.8 9.2 %collective-permute-start.65 = (bf16[32,1536]{1,0:T(8,128)(2,1)S(1)}, bf16[32,1536]{1,0:T(8,128)(2,1)S(1)}, u32[]{:S(2)}, u32[]{:S(2)}) collective-permute-start(bf16[32,1536]{1,0:T(8,128)(2,1)S(1)} %get-tuple-element.224), channel_id=1, source_target_pairs={{0,2},{1,3},{2,0},{3,1},{4,6},{5,7},{6,4},{7,5},{8,10},{9,11},{10,... | collective-permute-start | bytes 294920 | tf_op jit(solution)/shard_map/ppermute | solution.py:87
  231.7 9.4 %collective-permute-start.66 = (bf16[32,1536]{1,0:T(8,128)(2,1)S(1)}, bf16[32,1536]{1,0:T(8,128)(2,1)S(1)}, u32[]{:S(2)}, u32[]{:S(2)}) collective-permute-start(bf16[32,1536]{1,0:T(8,128)(2,1)S(1)} %get-tuple-element.225), channel_id=1, source_target_pairs={{0,3},{1,2},{2,1},{3,0},{4,7},{5,6},{6,5},{7,4},{8,11},{9,10},{10,... | collective-permute-start | bytes 294920 | tf_op jit(solution)/shard_map/ppermute | solution.py:87
  250.5 4.2 %collective-permute-start.67 = (bf16[32,2048]{1,0:T(8,128)(2,1)S(1)}, bf16[32,2048]{1,0:T(8,128)(2,1)S(1)}, u32[]{:S(2)}, u32[]{:S(2)}) collective-permute-start(bf16[32,2048]{1,0:T(8,128)(2,1)S(1)} %get-tuple-element.228), channel_id=1, source_target_pairs={{0,1},{1,0},{2,3},{3,2},{4,5},{5,4},{6,7},{7,6},{8,9},{9,8},{10,11... | collective-permute-start | bytes 393224 | tf_op jit(solution)/shard_map/ppermute | solution.py:87
  250.5 6.4 %collective-permute-start.68 = (bf16[32,2048]{1,0:T(8,128)(2,1)S(1)}, bf16[32,2048]{1,0:T(8,128)(2,1)S(1)}, u32[]{:S(2)}, u32[]{:S(2)}) collective-permute-start(bf16[32,2048]{1,0:T(8,128)(2,1)S(1)} %get-tuple-element.229), channel_id=1, source_target_pairs={{0,2},{1,3},{2,0},{3,1},{4,6},{5,7},{6,4},{7,5},{8,10},{9,11},{10,... | collective-permute-start | bytes 393224 | tf_op jit(solution)/shard_map/ppermute | solution.py:87
  250.7 8.1 %collective-permute-start.69 = (bf16[32,2048]{1,0:T(8,128)(2,1)S(1)}, bf16[32,2048]{1,0:T(8,128)(2,1)S(1)}, u32[]{:S(2)}, u32[]{:S(2)}) collective-permute-start(bf16[32,2048]{1,0:T(8,128)(2,1)S(1)} %get-tuple-element.230), channel_id=1, source_target_pairs={{0,3},{1,2},{2,1},{3,0},{4,7},{5,6},{6,5},{7,4},{8,11},{9,10},{10,... | collective-permute-start | bytes 393224 | tf_op jit(solution)/shard_map/ppermute | solution.py:87
  (15 other events, 86.5 us)
